TPU v7x, 32 devices: a whole 2x2x4 slice. The times are simulated.
32 devices in a mesh: rows: 8 (over z, y), frames: 4 (over x, core).
Axes of the slice: x: 2, y: 2, z: 4, core: 2. Of those that a mesh axis runs over, the one named last changes fastest.
Arguments:
- features: bfloat16 [24, 2048, 256], P('rows', 'frames')
- segment_ids: int32 [24, 2048], P('rows'), may hold values from 0 to 7, as said below
- timesteps: int32 [24, 8], P('rows'), may hold values from 0 to 999
- cotangent: bfloat16 [24, 1024, 256], P('rows', 'frames'), may hold values from -6 to 6
- narrow_slab: float32 [4352, 256], P('rows'), may hold values from -0.21875 to 0.21875
- broad_slab: float32 [256, 1536], P('rows')
- model_gains: float32 [12, 256], P(None, 'rows')
- hidden_gains: float32 [3, 1024], P(None, 'rows')
- narrow_first: float32 [4352, 256], P('rows'), may hold values from -128 to 128
- narrow_second: float32 [4352, 256], P('rows'), may hold values from 49.152 to 196.608
- broad_first: float32 [256, 1536], P('rows'), may hold values from -128 to 128
- broad_second: float32 [256, 1536], P('rows'), may hold values from 49.152 to 196.608
- gains_first: float32 [12, 256], P(None, 'rows'), may hold values from -128 to 128
- gains_second: float32 [12, 256], P(None, 'rows'), may hold values from 49.152 to 196.608
- hidden_first: float32 [3, 1024], P(None, 'rows'), may hold values from -128 to 128
- hidden_second: float32 [3, 1024], P(None, 'rows'), may hold values from 49.152 to 196.608
Outputs:
- frames_out: bfloat16 [24, 1024, 256], P('rows', 'frames')
- input_grad: float32 [24, 2048, 256], P('rows', 'frames')
- narrow_moment: float32 [4352, 256], P('rows')
- narrow_square: float32 [4352, 256], P('rows')
- narrow_update: float32 [4352, 256], P('rows')
- broad_moment: float32 [256, 1536], P('rows')
- broad_square: float32 [256, 1536], P('rows')
- broad_update: float32 [256, 1536], P('rows')
- gains_moment: float32 [12, 256], P(None, 'rows')
- gains_square: float32 [12, 256], P(None, 'rows')
- gains_update: float32 [12, 256], P(None, 'rows')
- hidden_moment: float32 [3, 1024], P(None, 'rows')
- hidden_square: float32 [3, 1024], P(None, 'rows')
- hidden_update: float32 [3, 1024], P(None, 'rows')
- narrow_copy: bfloat16 [4352, 256], P('rows')
- broad_copy: bfloat16 [256, 1536], P('rows')
Inputs may be any that keep to these rules, and one draw needn't show every extreme that they name: `segment_ids`: along each row the ids never fall, every id from 0 to 7 covers 2 or more frames, and each change of id lies at an even frame within the first or the last 256 frames of the row.
All inputs are finite; a program needn't handle non-finite values.
Results may differ from a plain program's by a relative error of at most 0.013.
Values may be sent and summed in bfloat16 or wider, within the bound.
A program may use at most 128 MiB of HBM per device.

v0:
```python
import math

import jax
import jax.numpy as jnp
from jax import lax
from jax.sharding import PartitionSpec as P

C = 256
TE = 1024
H = 2
HD = 64
FF = 1024
G = 8
NSEG = 8
STEP = 10
INNER = 128


PRECISE = lax.Precision.HIGHEST
EPS_NORM = 1e-05
EPS_ADAM = 1e-08
BETA_ONE = 0.9
BETA_TWO = 0.999
RATE_SLABS = 0.08
RATE_GAINS = 0.4
DECAY_RATE = 0.01
MASK_FILL = -1e30


def with_halo(block, sides, width):
    for axis, dim in sides:
        count = lax.axis_size(axis)
        forward = [(i, i + 1) for i in range(count - 1)]
        backward = [(target, source) for source, target in forward]
        low = lax.ppermute(
            lax.slice_in_dim(block, block.shape[dim] - width, None, axis=dim), axis, forward
        )
        high = lax.ppermute(lax.slice_in_dim(block, 0, width, axis=dim), axis, backward)
        block = jnp.concatenate([low, block, high], axis=dim)
    return block


def as_sent(array):
    return jax.tree.map(lambda a: a.astype(jnp.bfloat16) if a.dtype == jnp.float32 else a, array)


def passed_along(value, axis, steps):
    count = lax.axis_size(axis)
    first, last = (max(0, -steps), min(count, count - steps))
    return lax.ppermute(value, axis, [(source, source + steps) for source in range(first, last)])


def mish_act(values):
    return values * jnp.tanh(jax.nn.softplus(values))


def snake_beta(values, alpha_log, beta_log):
    return values + jnp.sin(jnp.exp(alpha_log) * values) ** 2 / jnp.exp(beta_log)


def layer_norm(values, gain_row, shift_row):
    centred = values - jnp.mean(values, axis=-1, keepdims=True)
    variance = jnp.mean(centred * centred, axis=-1, keepdims=True)
    return centred * lax.rsqrt(variance + EPS_NORM) * gain_row + shift_row


def time_embed(steps_in):
    half_width = TE // 2
    frequency = jnp.exp(-math.log(10000.0) * jnp.arange(half_width, dtype=jnp.float32) / half_width)
    angles = steps_in.astype(jnp.float32)[..., None] * frequency
    return jnp.concatenate([jnp.sin(angles), jnp.cos(angles)], axis=-1)


def conv_forward(inputs, weight, mask_prev, mask_next):
    padded = with_halo(inputs, (("frames", 1),), 1)
    left_side = padded[:, :-2] * mask_prev[..., None].astype(jnp.bfloat16)
    right_side = padded[:, 2:] * mask_next[..., None].astype(jnp.bfloat16)
    stacked = jnp.concatenate([left_side, inputs, right_side], axis=-1)
    return (jnp.einsum("rtk,kc->rtc", stacked, weight, preferred_element_type=jnp.float32), stacked)


def conv_backward(grad_low, stacked, weight, prev_ext, next_ext):
    weight_grad = jnp.einsum("rtk,rtc->kc", stacked, grad_low, preferred_element_type=jnp.float32)
    padded = with_halo(grad_low, (("frames", 1),), 1)
    projected = jnp.einsum("rtc,kc->rtk", padded, weight, preferred_element_type=jnp.float32)
    channel_count = weight.shape[1]
    input_part = projected[:, 2:, :channel_count] * prev_ext[:, 2:, None]
    input_part = input_part + projected[:, 1:-1, channel_count : 2 * channel_count]
    input_part = input_part + projected[:, :-2, 2 * channel_count :] * next_ext[:, :-2, None]
    return (input_part, weight_grad)


def group_reduce(values):
    return values.reshape(values.shape[0], values.shape[1], G, values.shape[2] // G).sum(-1)


def spread_groups(per_group, onehot):
    expanded = jnp.repeat(per_group, C // G, axis=-1)
    return jnp.einsum("rts,rsc->rtc", onehot, expanded, precision=PRECISE)


def norm_forward(values, onehot, counts, gain_row, shift_row):
    group_sums = group_reduce(jnp.einsum("rts,rtc->rsc", onehot, values, precision=PRECISE))
    squares = group_reduce(jnp.einsum("rts,rtc->rsc", onehot, values * values, precision=PRECISE))
    group_sums, squares = lax.psum((group_sums, squares), "frames")
    group_mean = group_sums / counts
    inverse_std = lax.rsqrt(squares / counts - group_mean * group_mean + EPS_NORM)
    frame_inverse = spread_groups(inverse_std, onehot)
    normed = (values - spread_groups(group_mean, onehot)) * frame_inverse
    return (normed * gain_row + shift_row, normed, frame_inverse)


def norm_backward(grad_out, normed, frame_inverse, onehot, counts, gain_row):
    gain_grad = jnp.sum(grad_out * normed, axis=(0, 1))
    shift_grad = jnp.sum(grad_out, axis=(0, 1))
    scaled = grad_out * gain_row
    mean_plain = group_reduce(jnp.einsum("rts,rtc->rsc", onehot, scaled, precision=PRECISE))
    mean_normed = group_reduce(
        jnp.einsum("rts,rtc->rsc", onehot, scaled * normed, precision=PRECISE)
    )
    mean_plain, mean_normed = lax.psum((mean_plain, mean_normed), "frames")
    input_part = frame_inverse * (
        scaled
        - spread_groups(mean_plain / counts, onehot)
        - normed * spread_groups(mean_normed / counts, onehot)
    )
    return (input_part, gain_grad, shift_grad)


def attend_row(query_rows, key_all, value_all, ids_here, ids_all):
    same_utterance = ids_here[:, None] == ids_all[None, :]
    head_outputs = []
    for head_index in range(H):
        column_start = head_index * HD
        column_end = column_start + HD
        scores = jnp.einsum(
            "qd,kd->qk",
            query_rows[:, column_start:column_end],
            key_all[:, column_start:column_end],
            preferred_element_type=jnp.float32,
        ) * HD ** (-0.5)
        probabilities = jax.nn.softmax(jnp.where(same_utterance, scores, MASK_FILL), axis=-1)
        head_outputs.append(
            jnp.dot(
                probabilities.astype(jnp.bfloat16),
                value_all[:, column_start:column_end],
                preferred_element_type=jnp.float32,
            )
        )
    return jnp.concatenate(head_outputs, axis=-1).astype(jnp.bfloat16)


def attend_back_row(query_rows, key_all, value_all, ids_here, ids_all, out_grad):
    same_utterance = ids_here[:, None] == ids_all[None, :]
    score_scale = HD ** (-0.5)
    query_parts = []
    key_parts = []
    value_parts = []
    for head_index in range(H):
        column_start = head_index * HD
        column_end = column_start + HD
        head_query = query_rows[:, column_start:column_end]
        head_key = key_all[:, column_start:column_end]
        head_value = value_all[:, column_start:column_end]
        head_grad = out_grad[:, column_start:column_end]
        scores = (
            jnp.einsum("qd,kd->qk", head_query, head_key, preferred_element_type=jnp.float32)
            * score_scale
        )
        probabilities = jax.nn.softmax(jnp.where(same_utterance, scores, MASK_FILL), axis=-1)
        value_parts.append(
            jnp.einsum(
                "qk,qd->kd",
                probabilities.astype(jnp.bfloat16),
                head_grad,
                preferred_element_type=jnp.float32,
            )
        )
        prob_grad = jnp.einsum(
            "qd,kd->qk", head_grad, head_value, preferred_element_type=jnp.float32
        )
        row_dot = jnp.sum(probabilities * prob_grad, axis=-1, keepdims=True)
        score_grad = (probabilities * (prob_grad - row_dot)).astype(jnp.bfloat16)
        query_parts.append(
            jnp.dot(score_grad, head_key, preferred_element_type=jnp.float32) * score_scale
        )
        key_parts.append(
            jnp.einsum("qk,qd->kd", score_grad, head_query, preferred_element_type=jnp.float32)
            * score_scale
        )
    return (
        jnp.concatenate(query_parts, axis=-1),
        jnp.concatenate(key_parts, axis=-1),
        jnp.concatenate(value_parts, axis=-1),
    )


def adam_update(grad, master, first, second, rate):
    moment = BETA_ONE * first + (1.0 - BETA_ONE) * grad
    square = BETA_TWO * second + (1.0 - BETA_TWO) * grad * grad
    corrected = moment / (1.0 - BETA_ONE**STEP)
    scaled = jnp.sqrt(square / (1.0 - BETA_TWO**STEP)) + EPS_ADAM
    return (moment, square, master - rate * (corrected / scaled + DECAY_RATE * master))


def local(
    features,
    segment_ids,
    timesteps,
    cotangent,
    narrow_slab,
    broad_slab,
    model_gains,
    hidden_gains,
    narrow_first,
    narrow_second,
    broad_first,
    broad_second,
    gains_first,
    gains_second,
    hidden_first,
    hidden_second,
):
    narrow_w, broad_w, gains_low, hidden_low = (
        lax.all_gather(narrow_slab.astype(jnp.bfloat16), "rows", axis=0, tiled=True),
        lax.all_gather(broad_slab.astype(jnp.bfloat16), "rows", axis=0, tiled=True),
        lax.all_gather(model_gains.astype(jnp.bfloat16), "rows", axis=1, tiled=True),
        lax.all_gather(hidden_gains.astype(jnp.bfloat16), "rows", axis=1, tiled=True),
    )
    gains_all = gains_low.astype(jnp.float32)
    hidden_all = hidden_low.astype(jnp.float32)
    conv_one = narrow_w[: 3 * C]
    conv_two = narrow_w[3 * C : 6 * C]
    conv_down = narrow_w[6 * C : 9 * C]
    time_w = narrow_w[9 * C : 9 * C + TE]
    ff_out = narrow_w[9 * C + TE :]
    qkv_w = broad_w[:, : 3 * INNER]
    proj_cols = broad_w[:, 3 * INNER : 4 * INNER]
    ff_in = broad_w[:, 4 * INNER :]
    rows_here = features.shape[0]
    frames_here = features.shape[1]
    half_frames = frames_here // 2
    first_frame = lax.axis_index("frames") * frames_here
    ids_padded = jnp.pad(segment_ids, ((0, 0), (2, 2)), constant_values=-1)

    def id_window(offset, length):
        return lax.dynamic_slice_in_dim(ids_padded, first_frame + offset, length, 1)

    ids_here = id_window(2, frames_here)
    ids_before = id_window(1, frames_here)
    ids_after = id_window(3, frames_here)
    mask_prev = (ids_before == ids_here).astype(jnp.float32)
    mask_next = (ids_after == ids_here).astype(jnp.float32)
    ext_here = id_window(1, frames_here + 2)
    ext_before = id_window(0, frames_here + 2)
    ext_after = id_window(2, frames_here + 2)
    prev_ext = ((ext_before == ext_here) & (ext_here >= 0)).astype(jnp.float32)
    next_ext = ((ext_after == ext_here) & (ext_here >= 0)).astype(jnp.float32)
    onehot = (ids_here[..., None] == jnp.arange(NSEG)).astype(jnp.float32)
    counts = jnp.sum((segment_ids[..., None] == jnp.arange(NSEG)).astype(jnp.float32), axis=1)[
        ..., None
    ] * (C // G)
    embedded = mish_act(time_embed(timesteps)).astype(jnp.bfloat16)
    time_term = (
        jnp.einsum("rse,ec->rsc", embedded, time_w, preferred_element_type=jnp.float32)
        + gains_all[2]
    )
    pre_one, stack_one = conv_forward(features, conv_one, mask_prev, mask_next)
    normed_one, plain_one, inverse_one = norm_forward(
        pre_one, onehot, counts, gains_all[0], gains_all[1]
    )
    hidden_one = mish_act(normed_one) + jnp.einsum(
        "rts,rsc->rtc", onehot, time_term, precision=PRECISE
    )
    pre_two, stack_two = conv_forward(
        hidden_one.astype(jnp.bfloat16), conv_two, mask_prev, mask_next
    )
    normed_two, plain_two, inverse_two = norm_forward(
        pre_two, onehot, counts, gains_all[3], gains_all[4]
    )
    resid = mish_act(normed_two) + features.astype(jnp.float32)
    layer_one, pull_layer = jax.vjp(layer_norm, resid, gains_all[5], gains_all[6])
    layer_low = layer_one.astype(jnp.bfloat16)
    qkv_rows = jnp.einsum(
        "rtc,ck->rtk", layer_low, qkv_w, preferred_element_type=jnp.float32
    ).astype(jnp.bfloat16)
    query_rows = qkv_rows[..., :INNER]
    key_rows = qkv_rows[..., INNER : 2 * INNER]
    value_rows = qkv_rows[..., 2 * INNER :]
    key_full, value_full = (
        lax.all_gather(key_rows, "frames", axis=1, tiled=True),
        lax.all_gather(value_rows, "frames", axis=1, tiled=True),
    )
    attended = lax.map(
        lambda member: attend_row(member[0], member[1], member[2], member[3], member[4]),
        (query_rows, key_full, value_full, ids_here, segment_ids),
    )
    mixed = (
        jnp.einsum("rti,ci->rtc", attended, proj_cols, preferred_element_type=jnp.float32)
        + gains_all[7]
    )
    resid_two = resid + mixed

    def ff_forward(resid_row):
        normed_row = layer_norm(resid_row, gains_all[8], gains_all[9]).astype(jnp.bfloat16)
        inner = jnp.dot(normed_row, ff_in, preferred_element_type=jnp.float32) + hidden_all[0]
        shaped = snake_beta(inner, hidden_all[1], hidden_all[2]).astype(jnp.bfloat16)
        return (
            resid_row
            + (jnp.dot(shaped, ff_out, preferred_element_type=jnp.float32) + gains_all[10])
        ).astype(jnp.bfloat16)

    resid_three = lax.map(ff_forward, resid_two)
    even_part = resid_three[:, 0::2]
    odd_part = resid_three[:, 1::2]
    carried = passed_along(as_sent(resid_three[:, frames_here - 1 :]), "frames", 1)
    before_odd = jnp.concatenate([carried, odd_part[:, :-1]], axis=1)
    ids_even = ids_here[:, 0::2]
    mask_before = (ids_before[:, 0::2] == ids_even).astype(jnp.bfloat16)
    mask_after = (ids_after[:, 0::2] == ids_even).astype(jnp.bfloat16)
    stack_down = jnp.concatenate(
        [before_odd * mask_before[..., None], even_part, odd_part * mask_after[..., None]], axis=-1
    )
    frames_out = (
        jnp.einsum("rjk,kc->rjc", stack_down, conv_down, preferred_element_type=jnp.float32)
        + gains_all[11]
    ).astype(jnp.bfloat16)
    down_grad = jnp.einsum("rjk,rjc->kc", stack_down, cotangent, preferred_element_type=jnp.float32)
    down_bias = jnp.sum(cotangent.astype(jnp.float32), axis=(0, 1))
    tail_grad = passed_along(cotangent[:, :1], "frames", -1)
    grad_ext = jnp.concatenate([cotangent, tail_grad], axis=1)
    blocks = jnp.einsum("rjc,kc->rjk", grad_ext, conv_down, preferred_element_type=jnp.float32)
    ext_even = id_window(2, frames_here + 2)[:, 0::2]
    ext_odd_before = id_window(1, frames_here + 2)[:, 0::2]
    mask_before_ext = ((ext_odd_before == ext_even) & (ext_even >= 0)).astype(jnp.float32)
    even_grad = blocks[:, :half_frames, C : 2 * C]
    odd_grad = (
        blocks[:, :half_frames, 2 * C :] * mask_after.astype(jnp.float32)[..., None]
        + blocks[:, 1:, :C] * mask_before_ext[:, 1:, None]
    )
    resid_three_grad = jnp.stack([even_grad, odd_grad], axis=2).reshape(rows_here, frames_here, C)

    def ff_backward(totals, member):
        resid_row, grad_row = member
        normed_row, pull_norm = jax.vjp(layer_norm, resid_row, gains_all[8], gains_all[9])
        normed_low = normed_row.astype(jnp.bfloat16)
        inner = jnp.dot(normed_low, ff_in, preferred_element_type=jnp.float32) + hidden_all[0]
        shaped, pull_snake = jax.vjp(snake_beta, inner, hidden_all[1], hidden_all[2])
        shaped_low = shaped.astype(jnp.bfloat16)
        grad_low = grad_row.astype(jnp.bfloat16)
        out_grad = jnp.einsum("tf,tc->fc", shaped_low, grad_low, preferred_element_type=jnp.float32)
        out_bias = jnp.sum(grad_low.astype(jnp.float32), axis=0)
        shaped_grad = jnp.einsum("tc,fc->tf", grad_low, ff_out, preferred_element_type=jnp.float32)
        inner_grad, alpha_grad, beta_grad = pull_snake(shaped_grad)
        inner_low = inner_grad.astype(jnp.bfloat16)
        in_grad = jnp.einsum("tc,tf->cf", normed_low, inner_low, preferred_element_type=jnp.float32)
        in_bias = jnp.sum(inner_low.astype(jnp.float32), axis=0)
        normed_grad = jnp.einsum("tf,cf->tc", inner_low, ff_in, preferred_element_type=jnp.float32)
        resid_grad, gain_grad, shift_grad = pull_norm(normed_grad)
        terms = (in_grad, in_bias, alpha_grad, beta_grad, out_grad, out_bias, gain_grad, shift_grad)
        return (jax.tree.map(jnp.add, totals, terms), resid_grad + grad_row)

    zero_totals = (
        jnp.zeros((C, FF), jnp.float32),
        jnp.zeros((FF,), jnp.float32),
        jnp.zeros((FF,), jnp.float32),
        jnp.zeros((FF,), jnp.float32),
        jnp.zeros((FF, C), jnp.float32),
        jnp.zeros((C,), jnp.float32),
        jnp.zeros((C,), jnp.float32),
        jnp.zeros((C,), jnp.float32),
    )
    ff_totals, resid_two_grad = lax.scan(ff_backward, zero_totals, (resid_two, resid_three_grad))
    in_grad, in_bias, alpha_grad, beta_grad, out_grad, out_bias, norm_gain, norm_shift = ff_totals
    mixed_low = resid_two_grad.astype(jnp.bfloat16)
    proj_grad = jnp.einsum("rtc,rti->ci", mixed_low, attended, preferred_element_type=jnp.float32)
    proj_bias = jnp.sum(mixed_low.astype(jnp.float32), axis=(0, 1))
    attended_grad = jnp.einsum(
        "rtc,ci->rti", mixed_low, proj_cols, preferred_element_type=jnp.float32
    ).astype(jnp.bfloat16)
    query_grad, key_part, value_part = lax.map(
        lambda member: attend_back_row(
            member[0], member[1], member[2], member[3], member[4], member[5]
        ),
        (query_rows, key_full, value_full, ids_here, segment_ids, attended_grad),
    )
    key_grad, value_grad = (
        lax.psum_scatter(
            key_part.astype(jnp.bfloat16), "frames", scatter_dimension=1, tiled=True
        ).astype(jnp.float32),
        lax.psum_scatter(
            value_part.astype(jnp.bfloat16), "frames", scatter_dimension=1, tiled=True
        ).astype(jnp.float32),
    )
    qkv_grad = jnp.concatenate(
        [
            query_grad.astype(jnp.bfloat16),
            key_grad.astype(jnp.bfloat16),
            value_grad.astype(jnp.bfloat16),
        ],
        axis=-1,
    )
    qkv_w_grad = jnp.einsum("rtc,rtk->ck", layer_low, qkv_grad, preferred_element_type=jnp.float32)
    layer_grad = jnp.einsum("rtk,ck->rtc", qkv_grad, qkv_w, preferred_element_type=jnp.float32)
    resid_from_layer, layer_gain, layer_shift = pull_layer(layer_grad)
    resid_grad = resid_two_grad + resid_from_layer
    pull_two = jax.vjp(mish_act, normed_two)[1]
    second_grad, gain_two, shift_two = norm_backward(
        pull_two(resid_grad)[0], plain_two, inverse_two, onehot, counts, gains_all[3]
    )
    hidden_grad, conv_two_grad = conv_backward(
        second_grad.astype(jnp.bfloat16), stack_two, conv_two, prev_ext, next_ext
    )
    time_grad = jnp.einsum("rts,rtc->rsc", onehot, hidden_grad, precision=PRECISE)
    time_w_grad = jnp.einsum(
        "rse,rsc->ec", embedded.astype(jnp.float32), time_grad, precision=PRECISE
    )
    time_bias = jnp.sum(time_grad, axis=(0, 1))
    pull_one = jax.vjp(mish_act, normed_one)[1]
    first_grad, gain_one, shift_one = norm_backward(
        pull_one(hidden_grad)[0], plain_one, inverse_one, onehot, counts, gains_all[0]
    )
    input_part, conv_one_grad = conv_backward(
        first_grad.astype(jnp.bfloat16), stack_one, conv_one, prev_ext, next_ext
    )
    input_grad = resid_grad + input_part
    narrow_grad = jnp.concatenate(
        [conv_one_grad, conv_two_grad, down_grad, time_w_grad, out_grad], axis=0
    )
    broad_grad = jnp.concatenate([qkv_w_grad, proj_grad, in_grad], axis=1)
    gains_grad = jnp.stack(
        [
            gain_one,
            shift_one,
            time_bias,
            gain_two,
            shift_two,
            layer_gain,
            layer_shift,
            proj_bias,
            norm_gain,
            norm_shift,
            out_bias,
            down_bias,
        ],
        axis=0,
    )
    hidden_grad_all = jnp.stack([in_bias, alpha_grad, beta_grad], axis=0)
    summed = lax.psum((narrow_grad, broad_grad, gains_grad, hidden_grad_all), ("rows", "frames"))
    owner_index = lax.axis_index("rows")
    owned = (
        lax.dynamic_slice_in_dim(
            summed[0], owner_index * narrow_slab.shape[0], narrow_slab.shape[0], 0
        ),
        lax.dynamic_slice_in_dim(
            summed[1], owner_index * broad_slab.shape[0], broad_slab.shape[0], 0
        ),
        lax.dynamic_slice_in_dim(
            summed[2], owner_index * model_gains.shape[1], model_gains.shape[1], 1
        ),
        lax.dynamic_slice_in_dim(
            summed[3], owner_index * hidden_gains.shape[1], hidden_gains.shape[1], 1
        ),
    )
    narrow_new = adam_update(owned[0], narrow_slab, narrow_first, narrow_second, RATE_SLABS)
    broad_new = adam_update(owned[1], broad_slab, broad_first, broad_second, RATE_SLABS)
    gains_new = adam_update(owned[2], model_gains, gains_first, gains_second, RATE_GAINS)
    hidden_new = adam_update(owned[3], hidden_gains, hidden_first, hidden_second, RATE_GAINS)
    return (
        frames_out,
        input_grad,
        narrow_new[0],
        narrow_new[1],
        narrow_new[2],
        broad_new[0],
        broad_new[1],
        broad_new[2],
        gains_new[0],
        gains_new[1],
        gains_new[2],
        hidden_new[0],
        hidden_new[1],
        hidden_new[2],
        narrow_new[2].astype(jnp.bfloat16),
        broad_new[2].astype(jnp.bfloat16),
    )


def solution(mesh):
    return jax.shard_map(
        local,
        mesh=mesh,
        in_specs=(
            P("rows", "frames", None),
            P("rows", None),
            P("rows", None),
            P("rows", "frames", None),
            P("rows", None),
            P("rows", None),
            P(None, "rows"),
            P(None, "rows"),
            P("rows", None),
            P("rows", None),
            P("rows", None),
            P("rows", None),
            P(None, "rows"),
            P(None, "rows"),
            P(None, "rows"),
            P(None, "rows"),
        ),
        out_specs=(
            P("rows", "frames", None),
            P("rows", "frames", None),
            P("rows", None),
            P("rows", None),
            P("rows", None),
            P("rows", None),
            P("rows", None),
            P("rows", None),
            P(None, "rows"),
            P(None, "rows"),
            P(None, "rows"),
            P(None, "rows"),
            P(None, "rows"),
            P(None, "rows"),
            P("rows", None),
            P("rows", None),
        ),
        check_vma=False,
    )
```

profile of v0, /device:TPU:0, one launch (start us, length us, event | category | flops | bytes accessed | tf_op | source)
XLA Modules:
  0.0 658.9 jit_solution(12991299621013142363)
XLA Ops:
  7.2 1.9 convert_element_type.181
  10.0 2.3 collective-permute-start
  15.0 31.7 %all-gather = bf16[8,32,12]{1,2,0:T(8,128)(2,1)S(1)} all-gather(bf16[1,32,12]{1,2,0:T(8,128)(2,1)S(1)} %convert_bitcast_fusion), channel_id=1, replica_groups=mesh['rows'=8,'frames'=4] {'rows'}, dimensions={0}, use_global_device_ids=true | all-gather | bytes 6912 | tf_op jit(solution)/shard_map/all_gather | solution.py:227
  54.5 1.8 fusion.115
  56.3 8.0 %all-gather.5.cloned.1.call-done = bf16[4352,256]{1,0:T(8,128)(2,1)} async-done(((bf16[544,256]{1,0:T(8,128)(2,1)}), bf16[4352,256]{1,0:T(8,128)(2,1)}) %all-gather.5.cloned.1.call-update) | async-done | bytes 2228240 | tf_op jit(solution)/shard_map/all_gather | solution.py:225
  64.3 2.0 fusion.97
  68.0 10.3 %all-reduce.6 = (f32[3,8,8]{2,1,0:T(8,128)S(1)}, f32[3,8,8]{2,1,0:T(8,128)S(1)}) all-reduce(f32[3,8,8]{2,1,0:T(8,128)S(1)} %reduce_sum.424, f32[3,8,8]{2,1,0:T(8,128)S(1)} %reduce_sum.422), channel_id=1, replica_groups=mesh['rows'=8,'frames'=4] {'frames'}, use_global_device_ids=true, to_apply=%region_4.5 | all-reduce | flops 384 | bytes 3072 | tf_op jit(solution)/shard_map/psum | solution.py:105
  80.8 1.6 convolution_add_fusion.4
  82.5 1.9 fusion.77
  84.4 2.0 collective-permute-start.2
  87.7 32.3 %all_gather.20 = bf16[256,1536]{1,0:T(8,128)(2,1)S(1)} all-gather(bf16[32,1536]{1,0:T(8,128)(2,1)S(1)} %copy-done.67), channel_id=1, replica_groups=mesh['rows'=8,'frames'=4] {'rows'}, dimensions={0}, use_global_device_ids=true | all-gather | bytes 884736 | tf_op jit(solution)/shard_map/all_gather | solution.py:226
  121.1 2.1 fusion.96
  124.9 12.1 %all-reduce.5 = (f32[3,8,8]{2,1,0:T(8,128)S(1)}, f32[3,8,8]{2,1,0:T(8,128)S(1)}) all-reduce(f32[3,8,8]{2,1,0:T(8,128)S(1)} %reduce_sum.426, f32[3,8,8]{2,1,0:T(8,128)S(1)} %reduce_sum.425), channel_id=1, replica_groups=mesh['rows'=8,'frames'=4] {'frames'}, use_global_device_ids=true, to_apply=%region_8.9 | all-reduce | flops 384 | bytes 3072 | tf_op jit(solution)/shard_map/psum | solution.py:105
  147.2 17.8 %all_gather.23 = bf16[3,1024]{1,0:T(4,128)(2,1)S(1)} all-gather(bf16[3,128]{1,0:T(4,128)(2,1)S(1)} %convert_element_type.192), channel_id=1, replica_groups=mesh['rows'=8,'frames'=4] {'rows'}, dimensions={1}, use_global_device_ids=true | all-gather | bytes 6912 | tf_op jit(solution)/shard_map/all_gather | solution.py:228
  169.2 1.9 slice.362
  173.1 2.4 copy.87
  175.4 3.4 reshape.262
  178.8 1.9 slice.365
  180.6 3.4 all-gather.7.cloned.1.call-done
  184.0 22.9 %while.68 = (s32[]{:T(128)}, bf16[3,512,128]{1,2,0:T(8,128)(2,1)S(1)}, s32[3,512]{1,0:T(4,128)S(1)}, s32[3,2048]{1,0:T(4,128)}, bf16[3,512,128]{2,1,0:T(8,128)(2...) while((s32[]{:T(128)}, bf16[3,512,128]{1,2,0:T(8,128)(2,1)S(1)}, ...), condition=%wide.region_16.17_spmd.clone, body=%wide.region_11.16_spmd.sunk.clone | while | flops 556070912 | bytes 30339176 | solution.py:294
  209.2 82.6 %while.71 = (s32[]{:T(128)}, f32[256,1024]{1,0:T(8,128)}, f32[1024]{0:T(1024)S(1)}, f32[1024]{0:T(1024)}, f32[1024]{0:T(1024)}, /*index=5*/f32[1024,256]{1,0:T(8...) while((s32[]{:T(128)}, f32[256,1024]{1,0:T(8,128)}, ...), condition=%wide.region_32.33_spmd.clone.clone, body=%wide.region_21.32_spmd.clone.sunk.clone | while | flops 1359621376 | bytes 43813600 | solution.py:373
  213.4 8.8 %convolution_add_fusion.10 = f32[1024,256]{1,0:T(8,128)S(1)} fusion(bf16[512,256]{1,0:T(8,128)(2,1)S(1)} %get-tuple-element.1178, f32[1024,256]{1,0:T(8,128)S(1)} %copy-done.43, f32[512,1024]{1,0:T(8,128)S(1)} %fusion.361, f32[1024]{0:T(1024)S(1)} %bitcast.372, f32[1024]{0:T(1024)S(1)} %copy-done.78, f32[1024]{0:T(1024)S(1)} %copy-done.80, ...), kind=kOutput, calls=%fused_computation.102.clone.1.clone | convolution fusion | flops 272105472 | bytes 4468737 | tf_op jit(solution)/shard_map/while/body/eval_jaxpr/tf,tc->fc/dot_general | solution.py:351
  222.3 9.9 %multiply_reduce_fusion.26 = (f32[1024]{0:T(1024)S(1)}, f32[1024]{0:T(1024)S(1)}, f32[1024]{0:T(1024)S(1)}, bf16[512,1024]{1,0:T(8,128)(2,1)S(1)}) fusion(f32[512,1024]{1,0:T(8,128)S(1)} %fusion.361, f32[1024]{0:T(1024)S(1)} %bitcast.371, f32[1024]{0:T(1024)S(1)} %bitcast.373, f32[1024]{0:T(1024)S(1)} %copy-done.80, f32[1024]{0:T(1024)S(1)} %copy-done.78, ...), kind=kOutput, calls=%fused_computation.96.clone.1.clone | convolution fusion | flops 277345280 | bytes 3960832 | tf_op jit(solution)/shard_map/while/body/eval_jaxpr/tc,fc->tf/dot_general | solution.py:353
  234.7 2.0 bitcast_dynamic-update-slice_fusion.3
  241.0 8.8 %convolution_add_fusion.10 = f32[1024,256]{1,0:T(8,128)S(1)} fusion(bf16[512,256]{1,0:T(8,128)(2,1)S(1)} %get-tuple-element.1178, f32[1024,256]{1,0:T(8,128)S(1)} %copy-done.43, f32[512,1024]{1,0:T(8,128)S(1)} %fusion.361, f32[1024]{0:T(1024)S(1)} %bitcast.372, f32[1024]{0:T(1024)S(1)} %copy-done.78, f32[1024]{0:T(1024)S(1)} %copy-done.80, ...), kind=kOutput, calls=%fused_computation.102.clone.1.clone | convolution fusion | flops 272105472 | bytes 4468737 | tf_op jit(solution)/shard_map/while/body/eval_jaxpr/tf,tc->fc/dot_general | solution.py:351
  249.8 9.9 %multiply_reduce_fusion.26 = (f32[1024]{0:T(1024)S(1)}, f32[1024]{0:T(1024)S(1)}, f32[1024]{0:T(1024)S(1)}, bf16[512,1024]{1,0:T(8,128)(2,1)S(1)}) fusion(f32[512,1024]{1,0:T(8,128)S(1)} %fusion.361, f32[1024]{0:T(1024)S(1)} %bitcast.371, f32[1024]{0:T(1024)S(1)} %bitcast.373, f32[1024]{0:T(1024)S(1)} %copy-done.80, f32[1024]{0:T(1024)S(1)} %copy-done.78, ...), kind=kOutput, calls=%fused_computation.96.clone.1.clone | convolution fusion | flops 277345280 | bytes 3960832 | tf_op jit(solution)/shard_map/while/body/eval_jaxpr/tc,fc->tf/dot_general | solution.py:353
  262.2 2.0 bitcast_dynamic-update-slice_fusion.3
  268.5 8.8 %convolution_add_fusion.10 = f32[1024,256]{1,0:T(8,128)S(1)} fusion(bf16[512,256]{1,0:T(8,128)(2,1)S(1)} %get-tuple-element.1178, f32[1024,256]{1,0:T(8,128)S(1)} %copy-done.43, f32[512,1024]{1,0:T(8,128)S(1)} %fusion.361, f32[1024]{0:T(1024)S(1)} %bitcast.372, f32[1024]{0:T(1024)S(1)} %copy-done.78, f32[1024]{0:T(1024)S(1)} %copy-done.80, ...), kind=kOutput, calls=%fused_computation.102.clone.1.clone | convolution fusion | flops 272105472 | bytes 4468737 | tf_op jit(solution)/shard_map/while/body/eval_jaxpr/tf,tc->fc/dot_general | solution.py:351
  277.4 9.9 %multiply_reduce_fusion.26 = (f32[1024]{0:T(1024)S(1)}, f32[1024]{0:T(1024)S(1)}, f32[1024]{0:T(1024)S(1)}, bf16[512,1024]{1,0:T(8,128)(2,1)S(1)}) fusion(f32[512,1024]{1,0:T(8,128)S(1)} %fusion.361, f32[1024]{0:T(1024)S(1)} %bitcast.371, f32[1024]{0:T(1024)S(1)} %bitcast.373, f32[1024]{0:T(1024)S(1)} %copy-done.80, f32[1024]{0:T(1024)S(1)} %copy-done.78, ...), kind=kOutput, calls=%fused_computation.96.clone.1.clone | convolution fusion | flops 277345280 | bytes 3960832 | tf_op jit(solution)/shard_map/while/body/eval_jaxpr/tc,fc->tf/dot_general | solution.py:353
  289.8 2.0 bitcast_dynamic-update-slice_fusion.3
  291.8 3.1 convolution_convert_fusion.1
  294.9 75.5 %while.70 = (s32[]{:T(128)}, bf16[3,512,128]{2,1,0:T(8,128)(2,1)}, bf16[3,2048,128]{2,1,0:T(8,128)(2,1)}, bf16[3,2048,128]{2,1,0:T(8,128)(2,1)}, s32[3,512]{1,0:...) while((s32[]{:T(128)}, bf16[3,512,128]{2,1,0:T(8,128)(2,1)}, ...), condition=%wide.region_40.41_spmd.clone, body=%wide.region_33.40_spmd.sunk.clone | while | flops 1382937600 | bytes 154620208 | solution.py:381
  307.3 3.6 multiply_reduce_fusion.24
  332.4 3.6 multiply_reduce_fusion.24
  357.4 3.6 multiply_reduce_fusion.24
  372.1 30.7 %while.69 = (s32[]{:T(128)}, bf16[3,512,256]{2,1,0:T(8,128)(2,1)}, f32[3,512,256]{2,1,0:T(8,128)S(1)}, f32[12,256]{1,0:T(8,128)}, bf16[256,1024]{1,0:T(8,128)(2,...) while((s32[]{:T(128)}, bf16[3,512,256]{2,1,0:T(8,128)(2,1)}, ...), condition=%wide.region_20.21_spmd.clone, body=%wide.region_17.20_spmd.sunk.clone | while | flops 541590016 | bytes 3457133 | solution.py:313
  374.2 8.2 %fusion.333 = bf16[3,512,256]{2,1,0:T(8,128)(2,1)} fusion(bf16[3,512,256]{2,1,0:T(8,128)(2,1)} %get-tuple-element.1244, s32[]{:T(128)S(6)} %copy.155, bf16[1024,256]{1,0:T(8,128)(2,1)S(1)} %get-tuple-element.1260, bf16[256,1024]{1,0:T(8,128)(2,1)S(1)} %get-tuple-element.1256, f32[1024]{0:T(1024)S(1)} %bitcast.364, f32[1024]{0:T(1024)S(1)} %bitcast.368, ...), kind=kOutput, calls=%fused_computation.31.clone.1.clone | convolution fusion | flops 541065216 | bytes 2379776 | tf_op jit(solution)/shard_map/while/body/eval_jaxpr/dot_general | solution.py:310
  384.4 8.2 %fusion.333 = bf16[3,512,256]{2,1,0:T(8,128)(2,1)} fusion(bf16[3,512,256]{2,1,0:T(8,128)(2,1)} %get-tuple-element.1244, s32[]{:T(128)S(6)} %copy.155, bf16[1024,256]{1,0:T(8,128)(2,1)S(1)} %get-tuple-element.1260, bf16[256,1024]{1,0:T(8,128)(2,1)S(1)} %get-tuple-element.1256, f32[1024]{0:T(1024)S(1)} %bitcast.364, f32[1024]{0:T(1024)S(1)} %bitcast.368, ...), kind=kOutput, calls=%fused_computation.31.clone.1.clone | convolution fusion | flops 541065216 | bytes 2379776 | tf_op jit(solution)/shard_map/while/body/eval_jaxpr/dot_general | solution.py:310
  394.5 8.2 %fusion.333 = bf16[3,512,256]{2,1,0:T(8,128)(2,1)} fusion(bf16[3,512,256]{2,1,0:T(8,128)(2,1)} %get-tuple-element.1244, s32[]{:T(128)S(6)} %copy.155, bf16[1024,256]{1,0:T(8,128)(2,1)S(1)} %get-tuple-element.1260, bf16[256,1024]{1,0:T(8,128)(2,1)S(1)} %get-tuple-element.1256, f32[1024]{0:T(1024)S(1)} %bitcast.364, f32[1024]{0:T(1024)S(1)} %bitcast.368, ...), kind=kOutput, calls=%fused_computation.31.clone.1.clone | convolution fusion | flops 541065216 | bytes 2379776 | tf_op jit(solution)/shard_map/while/body/eval_jaxpr/dot_general | solution.py:310
  404.2 4.7 slice.297
  408.8 2.8 collective-permute-start.4
  412.5 2.2 convolution_bitcast_fusion.5
  414.7 5.8 slice.301
  420.5 1.6 maximum_multiply_fusion
  422.1 7.4 %reduce-scatter.3.cloned.1.call-done = bf16[3,512,128]{2,1,0:T(8,128)(2,1)} async-done(((bf16[3,2048,128]{2,1,0:T(8,128)(2,1)}), bf16[3,512,128]{2,1,0:T(8,128)(2,1)}) %reduce-scatter.3.cloned.1.call-update) | async-done | bytes 393232 | tf_op jit(solution)/shard_map/reduce_scatter | solution.py:388
  429.5 2.2 multiply_reduce_fusion.8
  433.7 2.2 fusion.180
  438.1 10.3 %all-reduce.4 = (f32[3,8,8]{2,1,0:T(8,128)S(1)}, f32[3,8,8]{2,1,0:T(8,128)S(1)}) all-reduce(f32[3,8,8]{2,1,0:T(8,128)S(1)} %reduce_sum.431, f32[3,8,8]{2,1,0:T(8,128)S(1)} %reduce_sum.432), channel_id=1, replica_groups=mesh['rows'=8,'frames'=4] {'frames'}, use_global_device_ids=true, to_apply=%region_46.48 | all-reduce | flops 384 | bytes 3072 | tf_op jit(solution)/shard_map/psum | solution.py:121
  450.2 2.7 multiply_convert_fusion.3
  453.0 2.0 collective-permute-start.6
  459.4 1.9 fusion.98
  461.4 2.5 fusion.181
  466.3 12.9 %all-reduce.3 = (f32[3,8,8]{2,1,0:T(8,128)S(1)}, f32[3,8,8]{2,1,0:T(8,128)S(1)}) all-reduce(f32[3,8,8]{2,1,0:T(8,128)S(1)} %reduce_sum.433, f32[3,8,8]{2,1,0:T(8,128)S(1)} %reduce_sum.434), channel_id=1, replica_groups=mesh['rows'=8,'frames'=4] {'frames'}, use_global_device_ids=true, to_apply=%region_50.52 | all-reduce | flops 384 | bytes 3072 | tf_op jit(solution)/shard_map/psum | solution.py:121
  482.7 1.8 fusion.94
  485.1 1.7 fusion.93
  488.2 1.7 fusion.91
  492.2 2.0 collective-permute-start.8
  495.5 2.2 fusion.95
  498.4 2.3 fusion.104
  500.9 1.9 convert_reduce_fusion.2
  502.9 42.8 %all-reduce.1 = (f32[12,256]{1,0:T(8,128)S(1)}, f32[3,1024]{1,0:T(4,128)S(1)}) all-reduce(f32[12,256]{1,0:T(8,128)S(1)} %stack.75, f32[3,1024]{1,0:T(4,128)S(1)} %pad_maximum_fusion.19), channel_id=1, replica_groups=mesh['rows'=8,'frames'=4] {'rows','frames'}, use_global_device_ids=true, to_apply=%region_64.66 | all-reduce | flops 6144 | bytes 49152 | tf_op jit(solution)/shard_map/psum | solution.py:449
  547.0 100.1 %all-reduce.9.cloned.1.call-done = (f32[4352,256]{1,0:T(8,128)}, f32[256,1536]{1,0:T(8,128)}) async-done(((f32[4352,256]{1,0:T(8,128)}, f32[256,1536]{1,0:T(8,128)}), (f32[4352,256]{1,0:T(8,128)}, f32[256,1536]{1,0:T(8,128)})) %all-reduce.9.cloned.1.call-update) | async-done | bytes 6029328 | tf_op jit(solution)/shard_map/psum | solution.py:449
  647.1 1.9 fusion.183
  649.0 2.6 fusion.185
  (710 shorter events, 177.2 us)
Async XLA Ops:
  7.2 47.3 %copy-start.30 = (bf16[3,512,256]{2,1,0:T(8,128)(2,1)S(1)}, bf16[3,512,256]{2,1,0:T(8,128)(2,1)}, u32[]{:S(2)}) copy-start(bf16[3,512,256]{2,1,0:T(8,128)(2,1)} %param.25) | copy-start | bytes 2359300
  7.2 46.7 %copy-start.55 = (f32[32,1536]{1,0:T(8,128)S(1)}, f32[32,1536]{1,0:T(8,128)}, u32[]{:S(2)}) copy-start(f32[32,1536]{1,0:T(8,128)} %param.30) | copy-start | bytes 589828
  7.2 57.0 %all-gather.5.cloned.1.call-start = ((), (), s32[]{:S(2)}) async-start(), calls=%async_computation.2 | async-start | bytes 2506752 | tf_op jit(solution)/shard_map/all_gather | solution.py:225
  9.2 171.5 %all-gather.9.cloned.1.call-start = ((), (), s32[]{:S(2)}) async-start(), calls=%async_computation.4 | async-start | bytes 1966080 | tf_op jit(solution)/shard_map/all_gather | solution.py:292
  10.0 44.5 %collective-permute-start = (bf16[3,1,256]{2,1,0:T(2,128)(2,1)S(1)}, bf16[3,1,256]{2,1,0:T(2,128)(2,1)S(1)}, u32[]{:S(2)}, u32[]{:S(2)}) collective-permute-start(bf16[3,1,256]{2,1,0:T(2,128)(2,1)S(1)} %get-tuple-element.682), channel_id=1, source_target_pairs={{0,1},{1,2},{2,3},{4,5},{5,6},{6,7},{8,9},{9,10},{10,11},{12,13},{... | collective-permute-start | bytes 4616 | tf_op jit(solution)/shard_map/ppermute | solution.py:35
  12.3 42.2 %collective-permute-start.1 = (bf16[3,1,256]{2,1,0:T(2,128)(2,1)S(1)}, bf16[3,1,256]{2,1,0:T(2,128)(2,1)S(1)}, u32[]{:S(2)}, u32[]{:S(2)}) collective-permute-start(bf16[3,1,256]{2,1,0:T(2,128)(2,1)S(1)} %get-tuple-element.683), channel_id=1, source_target_pairs={{1,0},{2,1},{3,2},{5,4},{6,5},{7,6},{9,8},{10,9},{11,10},{13,12},{... | collective-permute-start | bytes 4616 | tf_op jit(solution)/shard_map/ppermute | solution.py:38
  46.8 17.5 %copy-start.75 = (f32[256,12]{0,1:T(8,128)}, f32[256,12]{0,1:T(8,128)S(1)}, u32[]{:S(2)}) copy-start(f32[256,12]{0,1:T(8,128)S(1)} %reshape.273) | copy-start | bytes 36868
  49.1 88.0 %copy-start.97 = (f32[3,8]{1,0:T(4,128)}, f32[3,8]{1,0:T(4,128)S(1)}, u32[]{:S(2)}) copy-start(f32[3,8]{1,0:T(4,128)S(1)} %broadcast_multiply_fusion.4) | copy-start | bytes 292
  49.7 32.7 %copy-start.116 = (f32[1,256]{1,0:T(1,128)}, f32[1,256]{1,0:T(1,128)S(1)}, u32[]{:S(2)}) copy-start(f32[1,256]{1,0:T(1,128)S(1)} %get-tuple-element.697) | copy-start | bytes 3076
  49.7 32.7 %copy-start.121 = (f32[1,256]{1,0:T(1,128)}, f32[1,256]{1,0:T(1,128)S(1)}, u32[]{:S(2)}) copy-start(f32[1,256]{1,0:T(1,128)S(1)} %get-tuple-element.696) | copy-start | bytes 3076
  49.7 89.9 %copy-start.101 = (f32[1,256]{1,0:T(1,128)}, f32[1,256]{1,0:T(1,128)S(1)}, u32[]{:S(2)}) copy-start(f32[1,256]{1,0:T(1,128)S(1)} %get-tuple-element.694) | copy-start | bytes 3076
  52.7 11.5 %copy-start.103 = (bf16[3,512]{1,0:T(4,128)(2,1)}, bf16[3,512]{1,0:T(4,128)(2,1)S(1)}, u32[]{:S(2)}) copy-start(bf16[3,512]{1,0:T(4,128)(2,1)S(1)} %get-tuple-element.636) | copy-start | bytes 9220
  52.7 11.5 %copy-start.105 = (bf16[3,512]{1,0:T(4,128)(2,1)}, bf16[3,512]{1,0:T(4,128)(2,1)S(1)}, u32[]{:S(2)}) copy-start(bf16[3,512]{1,0:T(4,128)(2,1)S(1)} %get-tuple-element.685) | copy-start | bytes 9220
  53.0 27.8 %copy-start.69 = (f32[3,8,512]{2,1,0:T(8,128)}, f32[3,8,512]{2,1,0:T(8,128)S(1)}, u32[]{:S(2)}) copy-start(f32[3,8,512]{2,1,0:T(8,128)S(1)} %get-tuple-element.703) | copy-start | bytes 147460
  53.0 27.8 %copy-start.71 = (f32[3,8,512]{2,1,0:T(8,128)}, f32[3,8,512]{2,1,0:T(8,128)S(1)}, u32[]{:S(2)}) copy-start(f32[3,8,512]{2,1,0:T(8,128)S(1)} %get-tuple-element.704) | copy-start | bytes 147460
  56.3 10.0 %copy-start.48 = (bf16[3,512,256]{2,1,0:T(8,128)(2,1)}, bf16[3,512,256]{2,1,0:T(8,128)(2,1)S(1)}, u32[]{:S(2)}) copy-start(bf16[3,512,256]{2,1,0:T(8,128)(2,1)S(1)} %get-tuple-element.680) | copy-start | bytes 2359300
  82.4 37.6 %copy-start.104 = (bf16[3,512]{1,0:T(4,128)(2,1)S(1)}, bf16[3,512]{1,0:T(4,128)(2,1)}, u32[]{:S(2)}) copy-start(bf16[3,512]{1,0:T(4,128)(2,1)} %copy-done.103) | copy-start | bytes 9220
  82.5 37.6 %copy-start.106 = (bf16[3,512]{1,0:T(4,128)(2,1)S(1)}, bf16[3,512]{1,0:T(4,128)(2,1)}, u32[]{:S(2)}) copy-start(bf16[3,512]{1,0:T(4,128)(2,1)} %copy-done.105) | copy-start | bytes 9220
  84.4 36.7 %copy-start.46 = (bf16[3,512,256]{2,1,0:T(8,128)(2,1)}, bf16[3,512,256]{2,1,0:T(8,128)(2,1)S(1)}, u32[]{:S(2)}) copy-start(bf16[3,512,256]{2,1,0:T(8,128)(2,1)S(1)} %fusion.77) | copy-start | bytes 2359300
  84.4 35.6 %collective-permute-start.2 = (bf16[3,1,256]{2,1,0:T(2,128)(2,1)S(1)}, bf16[3,1,256]{2,1,0:T(2,128)(2,1)S(1)}, u32[]{:S(2)}, u32[]{:S(2)}) collective-permute-start(bf16[3,1,256]{2,1,0:T(2,128)(2,1)S(1)} %get-tuple-element.678), channel_id=1, source_target_pairs={{0,1},{1,2},{2,3},{4,5},{5,6},{6,7},{8,9},{9,10},{10,11},{12,13},{... | collective-permute-start | bytes 4616 | tf_op jit(solution)/shard_map/ppermute | solution.py:35
  86.4 33.6 %collective-permute-start.3 = (bf16[3,1,256]{2,1,0:T(2,128)(2,1)S(1)}, bf16[3,1,256]{2,1,0:T(2,128)(2,1)S(1)}, u32[]{:S(2)}, u32[]{:S(2)}) collective-permute-start(bf16[3,1,256]{2,1,0:T(2,128)(2,1)S(1)} %get-tuple-element.679), channel_id=1, source_target_pairs={{1,0},{2,1},{3,2},{5,4},{6,5},{7,6},{9,8},{10,9},{11,10},{13,12},{... | collective-permute-start | bytes 4616 | tf_op jit(solution)/shard_map/ppermute | solution.py:38
  120.0 22.1 %copy-start.27 = (bf16[256,1536]{1,0:T(8,128)(2,1)}, bf16[256,1536]{1,0:T(8,128)(2,1)S(1)}, u32[]{:S(2)}) copy-start(bf16[256,1536]{1,0:T(8,128)(2,1)S(1)} %all_gather.20) | copy-start | bytes 2359300
  124.5 13.9 %copy-start.119 = (f32[1,256]{1,0:T(1,128)S(1)}, f32[1,256]{1,0:T(1,128)}, u32[]{:S(2)}) copy-start(f32[1,256]{1,0:T(1,128)} %get-tuple-element.693) | copy-start | bytes 3076
  141.0 66.7 %copy-start.6 = (f32[3,512,256]{2,1,0:T(8,128)}, f32[3,512,256]{2,1,0:T(8,128)S(1)}, u32[]{:S(2)}) copy-start(f32[3,512,256]{2,1,0:T(8,128)S(1)} %get-tuple-element.635) | copy-start | bytes 4718596
  144.0 40.1 %all-gather.7.cloned.1.call-start = ((), (), s32[]{:S(2)}) async-start(), calls=%async_computation.3 | async-start | bytes 1966080 | tf_op jit(solution)/shard_map/all_gather | solution.py:291
  144.7 277.4 %reduce-scatter.5.cloned.1.call-start = ((), (), s32[]{:S(2)}) async-start(), calls=%async_computation.6 | async-start | bytes 1966080 | tf_op jit(solution)/shard_map/reduce_scatter | solution.py:391
  144.8 26.3 %collective-permute-start.5 = (bf16[3,1,256]{2,1,0:T(2,128)(2,1)S(1)}, bf16[3,1,256]{2,1,0:T(2,128)(2,1)S(1)}, u32[]{:S(2)}, u32[]{:S(2)}) collective-permute-start(bf16[3,1,256]{2,1,0:T(2,128)(2,1)S(1)} %slice.305), channel_id=1, source_target_pairs={{1,0},{2,1},{3,2},{5,4},{6,5},{7,6},{9,8},{10,9},{11,10},{13,12},{... | collective-permute-start | bytes 4616 | tf_op jit(solution)/shard_map/ppermute | solution.py:50
  213.4 8.8 %copy-start.62 = (bf16[1024,256]{1,0:T(8,128)(2,1)S(1)}, bf16[1024,256]{1,0:T(8,128)(2,1)}, u32[]{:S(2)}) copy-start(bf16[1024,256]{1,0:T(8,128)(2,1)} %get-tuple-element.1316) | copy-start | bytes 1572868 | tf_op jit(solution)/shard_map/while
  222.3 10.0 %copy-start.44 = (f32[1024,256]{1,0:T(8,128)}, f32[1024,256]{1,0:T(8,128)S(1)}, u32[]{:S(2)}) copy-start(f32[1024,256]{1,0:T(8,128)S(1)} %convolution_add_fusion.10) | copy-start | bytes 3145732 | tf_op jit(solution)/shard_map/while
  222.3 10.0 %copy-start.85 = (f32[1024]{0:T(1024)S(1)}, f32[1024]{0:T(1024)}, u32[]{:S(2)}) copy-start(f32[1024]{0:T(1024)} %get-tuple-element.1285) | copy-start | bytes 12292 | tf_op jit(solution)/shard_map/while
  222.3 10.0 %copy-start.82 = (f32[1024]{0:T(1024)S(1)}, f32[1024]{0:T(1024)}, u32[]{:S(2)}) copy-start(f32[1024]{0:T(1024)} %get-tuple-element.1286) | copy-start | bytes 12292 | tf_op jit(solution)/shard_map/while
  249.8 10.0 %copy-start.44 = (f32[1024,256]{1,0:T(8,128)}, f32[1024,256]{1,0:T(8,128)S(1)}, u32[]{:S(2)}) copy-start(f32[1024,256]{1,0:T(8,128)S(1)} %convolution_add_fusion.10) | copy-start | bytes 3145732 | tf_op jit(solution)/shard_map/while
  249.8 10.0 %copy-start.85 = (f32[1024]{0:T(1024)S(1)}, f32[1024]{0:T(1024)}, u32[]{:S(2)}) copy-start(f32[1024]{0:T(1024)} %get-tuple-element.1285) | copy-start | bytes 12292 | tf_op jit(solution)/shard_map/while
  249.8 10.0 %copy-start.82 = (f32[1024]{0:T(1024)S(1)}, f32[1024]{0:T(1024)}, u32[]{:S(2)}) copy-start(f32[1024]{0:T(1024)} %get-tuple-element.1286) | copy-start | bytes 12292 | tf_op jit(solution)/shard_map/while
  277.3 10.0 %copy-start.44 = (f32[1024,256]{1,0:T(8,128)}, f32[1024,256]{1,0:T(8,128)S(1)}, u32[]{:S(2)}) copy-start(f32[1024,256]{1,0:T(8,128)S(1)} %convolution_add_fusion.10) | copy-start | bytes 3145732 | tf_op jit(solution)/shard_map/while
  277.4 10.0 %copy-start.85 = (f32[1024]{0:T(1024)S(1)}, f32[1024]{0:T(1024)}, u32[]{:S(2)}) copy-start(f32[1024]{0:T(1024)} %get-tuple-element.1285) | copy-start | bytes 12292 | tf_op jit(solution)/shard_map/while
  277.4 10.0 %copy-start.82 = (f32[1024]{0:T(1024)S(1)}, f32[1024]{0:T(1024)}, u32[]{:S(2)}) copy-start(f32[1024]{0:T(1024)} %get-tuple-element.1286) | copy-start | bytes 12292 | tf_op jit(solution)/shard_map/while
  370.4 59.0 %reduce-scatter.3.cloned.1.call-start = ((), (), s32[]{:S(2)}) async-start(), calls=%async_computation.5 | async-start | bytes 1966080 | tf_op jit(solution)/shard_map/reduce_scatter | solution.py:388
  371.0 276.1 %all-reduce.9.cloned.1.call-start = ((), (), s32[]{:S(2)}) async-start(), calls=%async_computation.7 | async-start | bytes 12058624 | tf_op jit(solution)/shard_map/psum | solution.py:449
  372.1 39.5 %copy-start.126 = (bf16[3,256]{1,0:T(4,128)(2,1)S(1)}, bf16[3,256]{1,0:T(4,128)(2,1)}, u32[]{:S(2)}) copy-start(bf16[3,256]{1,0:T(4,128)(2,1)} %get-tuple-element.633) | copy-start | bytes 4612
  402.8 9.8 %copy-start.15 = (f32[3,512,256]{2,1,0:T(8,128)S(1)}, f32[3,512,256]{2,1,0:T(8,128)}, u32[]{:S(2)}) copy-start(f32[3,512,256]{2,1,0:T(8,128)} %get-tuple-element.403) | copy-start | bytes 4718596
  408.8 11.6 %collective-permute-start.4 = (bf16[3,1,256]{2,1,0:T(2,128)(2,1)}, bf16[3,1,256]{2,1,0:T(2,128)(2,1)}, u32[]{:S(2)}, u32[]{:S(2)}) collective-permute-start(bf16[3,1,256]{2,1,0:T(2,128)(2,1)} %slice.296), channel_id=1, source_target_pairs={{0,1},{1,2},{2,3},{4,5},{5,6},{6,7},{8,9},{9,10},{10,11},{12,13},{... | collective-permute-start | bytes 4616 | tf_op jit(solution)/shard_map/ppermute | solution.py:50
  412.5 17.0 %copy-start.7 = (f32[3,512,256]{2,1,0:T(8,128)S(1)}, f32[3,512,256]{2,1,0:T(8,128)}, u32[]{:S(2)}) copy-start(f32[3,512,256]{2,1,0:T(8,128)} %copy-done.6) | copy-start | bytes 4718596
  412.5 17.0 %copy-start.89 = (f32[3,512]{1,0:T(4,128)S(1)}, f32[3,512]{1,0:T(4,128)}, u32[]{:S(2)}) copy-start(f32[3,512]{1,0:T(4,128)} %copy-done.88) | copy-start | bytes 18436
  414.7 14.8 %copy-start.91 = (f32[3,512]{1,0:T(4,128)S(1)}, f32[3,512]{1,0:T(4,128)}, u32[]{:S(2)}) copy-start(f32[3,512]{1,0:T(4,128)} %copy-done.90) | copy-start | bytes 18436
  414.7 14.8 %copy-start.124 = (f32[1,256]{1,0:T(1,128)S(1)}, f32[1,256]{1,0:T(1,128)}, u32[]{:S(2)}) copy-start(f32[1,256]{1,0:T(1,128)} %get-tuple-element.692) | copy-start | bytes 3076
  414.7 14.8 %copy-start.135 = (bf16[3,512,128]{2,1,0:T(8,128)(2,1)S(1)}, bf16[3,512,128]{2,1,0:T(8,128)(2,1)}, u32[]{:S(2)}) copy-start(bf16[3,512,128]{2,1,0:T(8,128)(2,1)} %get-tuple-element.404) | copy-start | bytes 1179652
  437.0 11.3 %copy-start.98 = (f32[3,8]{1,0:T(4,128)S(1)}, f32[3,8]{1,0:T(4,128)}, u32[]{:S(2)}) copy-start(f32[3,8]{1,0:T(4,128)} %copy-done.97) | copy-start | bytes 292
  453.0 6.2 collective-permute-start.6
  455.1 4.3 collective-permute-start.7
  492.2 5.6 collective-permute-start.8
  494.2 4.2 collective-permute-start.9
  500.8 44.9 %copy-start.129 = (f32[3,128]{1,0:T(4,128)S(1)}, f32[3,128]{1,0:T(4,128)}, u32[]{:S(2)}) copy-start(f32[3,128]{1,0:T(4,128)} %param.32) | copy-start | bytes 4612
  500.8 44.9 %copy-start.132 = (f32[3,128]{1,0:T(4,128)S(1)}, f32[3,128]{1,0:T(4,128)}, u32[]{:S(2)}) copy-start(f32[3,128]{1,0:T(4,128)} %param.40) | copy-start | bytes 4612
  500.8 44.9 %copy-start.133 = (f32[3,128]{1,0:T(4,128)S(1)}, f32[3,128]{1,0:T(4,128)}, u32[]{:S(2)}) copy-start(f32[3,128]{1,0:T(4,128)} %param.39) | copy-start | bytes 4612
  500.8 45.5 %copy-start.118 = (f32[12,32]{1,0:T(8,128)S(1)}, f32[12,32]{1,0:T(8,128)}, u32[]{:S(2)}) copy-start(f32[12,32]{1,0:T(8,128)} %param.31) | copy-start | bytes 4612
  500.8 45.5 %copy-start.127 = (f32[12,32]{1,0:T(8,128)S(1)}, f32[12,32]{1,0:T(8,128)}, u32[]{:S(2)}) copy-start(f32[12,32]{1,0:T(8,128)} %param.38) | copy-start | bytes 4612
  500.8 45.5 %copy-start.128 = (f32[12,32]{1,0:T(8,128)S(1)}, f32[12,32]{1,0:T(8,128)}, u32[]{:S(2)}) copy-start(f32[12,32]{1,0:T(8,128)} %param.37) | copy-start | bytes 4612
  500.8 146.3 %copy-start.56 = (f32[32,1536]{1,0:T(8,128)S(1)}, f32[32,1536]{1,0:T(8,128)}, u32[]{:S(2)}) copy-start(f32[32,1536]{1,0:T(8,128)} %param.30) | copy-start | bytes 589828
  500.9 146.3 %copy-start.73 = (f32[32,1536]{1,0:T(8,128)S(1)}, f32[32,1536]{1,0:T(8,128)}, u32[]{:S(2)}) copy-start(f32[32,1536]{1,0:T(8,128)} %param.36) | copy-start | bytes 589828
  500.9 146.3 %copy-start.74 = (f32[32,1536]{1,0:T(8,128)S(1)}, f32[32,1536]{1,0:T(8,128)}, u32[]{:S(2)}) copy-start(f32[32,1536]{1,0:T(8,128)} %param.35) | copy-start | bytes 589828
  500.9 148.1 %copy-start.58 = (f32[544,256]{1,0:T(8,128)S(1)}, f32[544,256]{1,0:T(8,128)}, u32[]{:S(2)}) copy-start(f32[544,256]{1,0:T(8,128)} %param.33) | copy-start | bytes 1671172
  502.8 146.2 %copy-start.36 = (f32[544,256]{1,0:T(8,128)S(1)}, f32[544,256]{1,0:T(8,128)}, u32[]{:S(2)}) copy-start(f32[544,256]{1,0:T(8,128)} %param.29) | copy-start | bytes 1671172
  502.8 146.2 %copy-start.57 = (f32[544,256]{1,0:T(8,128)S(1)}, f32[544,256]{1,0:T(8,128)}, u32[]{:S(2)}) copy-start(f32[544,256]{1,0:T(8,128)} %param.34) | copy-start | bytes 1671172
  (139 other events, 330.2 us)
Sparse Core Ops, SparseCore 0:
  10.8 53.4 all-gather.4
  144.1 18.6 all-gather.8
  164.3 19.6 all-gather.6
  370.6 28.1 reduce-scatter.4
  401.3 28.1 reduce-scatter.2
  491.2 155.9 all-reduce.8
where the time goes:
time: 671 us; the launch traced here: 659 us
  matrix products  181 us (27%)
  blocking collectives  170 us (25%)
  waiting for transfers between devices  121 us (18%)
  local copies, waits for them, and re-layouts  85.4 us (13%)
  other arithmetic  64.8 us (10%)
  starting transfers between devices  18 us (3%)
  between operations  16.1 us (2%)
    psum x1, waiting for transfers between devices, local(): lax.psum((narrow_grad, broad_grad, gains_grad, hidden_grad_all), ('rows',...  100 us
    psum x1, blocking collectives, local(): lax.psum((narrow_grad, broad_grad, gains_grad, hidden_grad_all), ('rows',...  42.8 us
    all_gather x1, blocking collectives, local(): lax.all_gather(broad_slab.astype(jnp.bfloat16), 'rows', axis=0, tiled=True)  32.3 us
    all_gather x1, blocking collectives, local(): lax.all_gather(model_gains.astype(jnp.bfloat16), 'rows', axis=1, tiled=True)  31.7 us
    dot_general x3, matrix products, ff_backward(): jnp.einsum('tc,fc->tf', grad_low, ff_out, preferred_element_type=jnp.floa...  29.8 us
    dot_general x3, matrix products, ff_backward(): jnp.einsum('tf,tc->fc', shaped_low, grad_low, preferred_element_type=jnp....  26.4 us
    dot_general x3, matrix products, ff_forward(): jnp.dot(shaped, ff_out, preferred_element_type=jnp.float32) + gains_all[10]  24.7 us
    psum x2, blocking collectives, norm_backward(): mean_plain, mean_normed = lax.psum((mean_plain, mean_normed), 'frames')  23.1 us
  transfers between devices with their start and end apart: 16, of which 6 were waited for; matrix products, arithmetic and copies ran while one was open for 13% of the time, Pallas kernels for 0%

commit v1 on v0

v1 whole, which is shorter than its diff:
```python
import functools
import math

import jax
import jax.numpy as jnp
from jax import lax
from jax.experimental import pallas as pl
from jax.experimental.pallas import tpu as pltpu
from jax.sharding import PartitionSpec as P

C = 256
TE = 1024
H = 2
HD = 64
FF = 1024
G = 8
NSEG = 8
STEP = 10
INNER = 128
EPS_NORM = 1e-05
EPS_ADAM = 1e-08
BETA_ONE = 0.9
BETA_TWO = 0.999
RATE_SLABS = 0.08
RATE_GAINS = 0.4
DECAY_RATE = 0.01
MASK_FILL = -1e30

F32 = jnp.float32
BF = jnp.bfloat16
MESH = pl.DeviceIdType.MESH
OFF = 32
GROUP = C // G


def dot(a, b):
    return jnp.dot(a, b, preferred_element_type=F32)


def dot_nt(a, b):
    return lax.dot_general(a, b, (((1,), (1,)), ((), ())), preferred_element_type=F32)


def dot_tn(a, b):
    return lax.dot_general(a, b, (((0,), (0,)), ((), ())), preferred_element_type=F32)


def recip(x):
    r = pltpu.reciprocal(x, approx=True)
    return r * (2.0 - x * r)


def split2(x):
    hi = x.astype(BF)
    lo = (x - hi.astype(F32)).astype(BF)
    return hi, lo


def split3(x):
    hi = x.astype(BF).astype(F32)
    mid = (x - hi).astype(BF).astype(F32)
    lo = (x - hi - mid).astype(BF).astype(F32)
    return hi, mid, lo


def mish_parts(y):
    e = jnp.exp(jnp.minimum(y, 30.0))
    n = e * (e + 2.0)
    rc = recip(n + 2.0)
    t = n * rc
    d = t + y * (2.0 * rc) * (1.0 + t) * (e * recip(1.0 + e))
    return t, d


def reduced_angle(a):
    k = jnp.floor(a * (1.0 / math.pi) + 0.5)
    r = (a - k * 3.140625) - k * 9.67653589793e-4
    r2 = r * r
    s = r * (1.0 + r2 * (-1.0 / 6 + r2 * (1.0 / 120 + r2 * (-1.0 / 5040 + r2 * (1.0 / 362880)))))
    c = 1.0 + r2 * (
        -0.5 + r2 * (1.0 / 24 + r2 * (-1.0 / 720 + r2 * (1.0 / 40320 + r2 * (-1.0 / 3628800))))
    )
    return k, s, c


def iota(shape, dim):
    return lax.broadcasted_iota(jnp.int32, shape, dim)


def group_sum_matrix(shift):
    return jnp.where(iota((C, 128), 0) // GROUP + shift == iota((C, 128), 1), 1.0, 0.0).astype(BF)


def group_spread_matrix():
    return jnp.where(iota((128, C), 0) == iota((128, C), 1) // GROUP, 1.0, 0.0).astype(BF)


def compact(sums, squares):
    a = jnp.concatenate(split3(sums), axis=0).astype(BF)
    b = jnp.concatenate(split3(squares), axis=0).astype(BF)
    both = dot(a, group_sum_matrix(0)) + dot(b, group_sum_matrix(G))
    return both[0:8] + both[8:16] + both[16:24]


def expand(tables):
    stacked = jnp.concatenate([p for t in tables for p in split3(t)], axis=0).astype(BF)
    wide = dot(stacked, group_spread_matrix())
    return [
        wide[24 * i : 24 * i + 8] + wide[24 * i + 8 : 24 * i + 16] + wide[24 * i + 16 : 24 * i + 24]
        for i in range(len(tables))
    ]


def table_of(columns):
    parts = split3(columns)
    zero = jnp.zeros((104, columns.shape[1]), F32)
    return jnp.concatenate(list(parts) + [zero], axis=0).astype(BF)


def segment_sums(onehot_rows, values):
    hi, lo = split2(values)
    return dot(onehot_rows, hi) + dot(onehot_rows, lo)


def layer_norm_parts(v):
    mu = jnp.mean(v, axis=-1, keepdims=True)
    cen = v - mu
    rs = lax.rsqrt(jnp.mean(cen * cen, axis=-1, keepdims=True) + EPS_NORM)
    return cen * rs, rs


def layer_norm_back(d, n, rs, gain):
    dg = d * gain
    return (dg - jnp.mean(dg, axis=-1, keepdims=True) - n * jnp.mean(dg * n, axis=-1, keepdims=True)) * rs


def colsum(x):
    return jnp.sum(x, axis=0, keepdims=True)


def main_kernel(
    feat, ids, steps, cot, narrow, broad, gains, hidden,
    fout, igrad, ngrad, bgrad, ggrad, hgrad,
    uext, gyext, meta, metab, ohrow, keymask, idp, counts, emb, tterm,
    zs, nrm1, der1, u2, nrm2, der2, resid, n3, rs3, ll1, qs, kall, vall,
    statin, statout,
    kt, vt, sbuf, ebuf, otb, invl, dos, dost,
    gr3, gf, nl2, shaped, ginner, r3s, r3b, gm, att, dq,
    part, rbuf, rbuf2, sumbuf, dqkv, g2, tg,
    halo_s, halo_r, cot_s, cot_r, stat_s, stat_r, kv_s, kv_r, dkv_s, dkv_r, gh_s, gh_r, r3_s, r3_r,
):
    R, T = feat.shape[0], feat.shape[1]
    gr2, dn, g3 = igrad, resid, shaped
    TX = T + 2 * OFF
    L = ids.shape[1]
    HT = T // 2
    f = lax.axis_index("frames")
    rw = lax.axis_index("rows")
    sib = f + 1 - 2 * (f % 2)
    cross = (f + 2) % 4
    diag = 3 - f
    peers = (sib, cross, diag)

    barrier = pltpu.get_barrier_semaphore()
    for p in peers:
        pl.semaphore_signal(barrier, inc=1, device_id=(rw, p), device_id_type=MESH)
    pl.semaphore_wait(barrier, 3)

    def remote(src, dst, ssem, rsem, target):
        return pltpu.make_async_remote_copy(
            src_ref=src, dst_ref=dst, send_sem=ssem, recv_sem=rsem,
            device_id=(rw, target), device_id_type=MESH,
        )

    def to_next(src, dst, ssem, rsem):
        return remote(src, dst, ssem, rsem, (f + 1) % 4)

    def to_prev(src, dst, ssem, rsem):
        return remote(src, dst, ssem, rsem, (f + 3) % 4)

    feat_down = to_next(feat.at[:, pl.ds(T - 16, 16)], uext.at[:, pl.ds(OFF - 16, 16)], halo_s.at[0], halo_r.at[0])
    feat_up = to_prev(feat.at[:, pl.ds(0, 16)], uext.at[:, pl.ds(OFF + T, 16)], halo_s.at[1], halo_r.at[1])
    cot_up = to_prev(cot.at[:, pl.ds(0, 16)], gyext.at[:, pl.ds(HT, 16)], cot_s.at[0], cot_r.at[0])

    @pl.when(f < 3)
    def _():
        feat_down.start()

    @pl.when(f > 0)
    def _():
        feat_up.start()
        cot_up.start()

    uext[:, 0 : OFF - 16, :] = jnp.zeros((R, OFF - 16, C), BF)
    uext[:, OFF + T + 16 :, :] = jnp.zeros((R, TX - OFF - T - 16, C), BF)
    g2[:, 0 : OFF - 16, :] = jnp.zeros((R, OFF - 16, C), BF)
    g2[:, OFF + T + 16 :, :] = jnp.zeros((R, TX - OFF - T - 16, C), BF)

    @pl.when(f == 0)
    def _():
        uext[:, OFF - 16 : OFF, :] = jnp.zeros((R, 16, C), BF)

    @pl.when(f == 3)
    def _():
        uext[:, OFF + T : OFF + T + 16, :] = jnp.zeros((R, 16, C), BF)
        gyext[:, HT : HT + 16, :] = jnp.zeros((R, 16, C), BF)

    ggrad[...] = jnp.zeros(ggrad.shape, F32)
    hgrad[...] = jnp.zeros(hgrad.shape, F32)

    idp[...] = jnp.full(idp.shape, -1.0, F32)
    idp[0:R, 128 : 128 + L] = ids[...].astype(F32)
    idv = idp[0:8]
    width = idv.shape[1]
    prev_row = jnp.where(pltpu.roll(idv, 1, 1) == idv, 1.0, 0.0)
    next_row = jnp.where(pltpu.roll(idv, width - 1, 1) == idv, 1.0, 0.0)
    idp[8:16, :] = prev_row
    idp[16:24, :] = next_row
    base = pl.multiple_of(f * T, 128)
    WX = T + 256
    win = idp[:, pl.ds(base, WX)]
    win = pltpu.roll(win, WX - (128 - OFF), 1)[:, : T + 128]
    own = idp[:, pl.ds(pl.multiple_of(base + 128, 128), T)]
    for r in range(R):
        n_lane = T + 128
        row_id = jnp.broadcast_to(win[r : r + 1], (8, n_lane))
        lab = iota((8, n_lane), 0).astype(F32)
        oh = jnp.where(row_id == lab, 1.0, 0.0)
        pn = jnp.where(
            lab == 0.0,
            jnp.broadcast_to(win[8 + r : 9 + r], (8, n_lane)),
            jnp.where(lab == 1.0, jnp.broadcast_to(win[16 + r : 17 + r], (8, n_lane)), 0.0),
        )
        block = jnp.concatenate([oh, oh, oh, pn, jnp.zeros((96, n_lane), F32)], axis=0)
        turned = block.T
        meta[r] = turned[:TX]
        metab[r] = turned[:TX].astype(BF)
        lab_own = iota((8, T), 0).astype(F32)
        ohrow[r] = jnp.where(jnp.broadcast_to(own[r : r + 1], (8, T)) == lab_own, 1.0, 0.0)
        full = jnp.broadcast_to(idv[r : r + 1, 128 : 128 + L], (8, L))
        lab_full = iota((8, L), 0).astype(F32)
        ohf = jnp.where(full == lab_full, 1.0, 0.0)
        counts[r] = jnp.broadcast_to(jnp.sum(ohf, axis=1, keepdims=True) * float(GROUP), (8, 128))
        km = jnp.concatenate([(1.0 - ohf) * MASK_FILL, jnp.zeros((120, L), F32)], axis=0)
        keymask[r] = km.T.astype(BF)

    uext[:, OFF : OFF + T, :] = feat[...]
    gyext[:, 0:HT, :] = cot[...]

    half = TE // 2
    freq = jnp.exp(iota((8, half), 1).astype(F32) * (-math.log(10000.0) / half))
    for r in range(R):
        ang = steps[8 * r : 8 * r + 8, :] * freq
        k, s, c = reduced_angle(ang)
        sign = 1.0 - 2.0 * (k - 2.0 * jnp.floor(k * 0.5))
        both = jnp.concatenate([s * sign, c * sign], axis=1)
        emb[8 * r : 8 * r + 8, :] = both * mish_parts(both)[0]
    embb = emb[...].astype(BF)
    tw = 9 * C
    tterm[...] = dot(embb, narrow[tw : tw + TE, :]) + gains[2:3, :]

    def own_prev(r):
        return meta[r, OFF : OFF + T, 24:25]

    def own_next(r):
        return meta[r, OFF : OFF + T, 25:26]

    def stat_copies(phase, r):
        return [
            remote(statout.at[phase, r], statin.at[phase, r, i], stat_s.at[phase, r, i], stat_r.at[phase, r, i], peers[i])
            for i in range(3)
        ]

    def send_stats(phase, r, sums, squares):
        statout[phase, r] = compact(sums, squares)
        for cp in stat_copies(phase, r):
            cp.start()

    def total_stats(phase, r):
        for cp in stat_copies(phase, r):
            cp.wait()
        return statout[phase, r] + statin[phase, r, 0] + statin[phase, r, 1] + statin[phase, r, 2]

    def norm_tables(phase, r):
        tot = total_stats(phase, r) / jnp.maximum(counts[r], 1.0)
        second = pltpu.roll(tot, 128 - G, 1)
        inv = lax.rsqrt(jnp.maximum(second - tot * tot, 0.0) + EPS_NORM)
        lanes = iota((8, 128), 1) < G
        inv = jnp.where(lanes, inv, 0.0)
        return tot * inv, inv

    def conv_into(r, src, first_row):
        for j in range(3):
            zs[j] = dot(src[r], narrow[first_row + j * C : first_row + (j + 1) * C, :])

    @pl.when(f > 0)
    def _():
        feat_down.wait_recv()

    @pl.when(f < 3)
    def _():
        feat_up.wait_recv()

    def phase_one(r, carry):
        conv_into(r, uext, 0)
        lo, hi = OFF - 16, OFF + T + 16
        n = hi - lo
        v = (
            zs[0, lo - 1 : hi - 1] * meta[r, lo:hi, 24:25]
            + zs[1, lo:hi]
            + zs[2, lo + 1 : hi + 1] * meta[r, lo:hi, 25:26]
        )
        nrm1[r, lo:hi] = v
        nrm1[r, 0:lo] = jnp.zeros((lo, C), F32)
        nrm1[r, hi:] = jnp.zeros((TX - hi, C), F32)
        vo = v[OFF - lo : OFF - lo + T]
        oh = ohrow[r].astype(BF)
        send_stats(0, r, segment_sums(oh, vo), segment_sums(oh, vo * vo))
        return carry

    lax.fori_loop(0, R, phase_one, 0)

    CH = TX // 4

    def phase_two(r, carry):
        mi, iv = expand(norm_tables(0, r))
        tt = tterm[pl.ds(pl.multiple_of(8 * r, 8), 8), :]
        tab = table_of(jnp.concatenate([mi, iv, tt], axis=1))

        def chunk(i, c2):
            rows = pl.ds(pl.multiple_of(i * CH, 16), CH)
            sp = dot(metab[r, rows], tab)
            n = nrm1[r, rows] * sp[:, C : 2 * C] - sp[:, :C]
            y = n * gains[0:1, :] + gains[1:2, :]
            t, d = mish_parts(y)
            nrm1[r, rows] = n
            der1[r, rows] = d
            u2[r, rows] = (y * t + sp[:, 2 * C :]).astype(BF)
            return c2

        lax.fori_loop(0, 4, chunk, 0)
        conv_into(r, u2, 3 * C)
        v = (
            zs[0, OFF - 1 : OFF + T - 1] * own_prev(r)
            + zs[1, OFF : OFF + T]
            + zs[2, OFF + 1 : OFF + T + 1] * own_next(r)
        )
        nrm2[r] = v
        oh = ohrow[r].astype(BF)
        send_stats(1, r, segment_sums(oh, v), segment_sums(oh, v * v))
        return carry

    lax.fori_loop(0, R, phase_two, 0)

    def kv_slot(ref, r, g):
        return ref.at[r, pl.ds(pl.multiple_of(g * T, 128), T)]

    def kv_copies(r):
        out = []
        for i, ref in enumerate((kall, vall)):
            out.append(remote(kv_slot(ref, r, f), kv_slot(ref, r, f), kv_s.at[i, 0, r], kv_r.at[i, 0, r], sib))
            out.append(remote(kv_slot(ref, r, f), kv_slot(ref, r, f), kv_s.at[i, 1, r], kv_r.at[i, 1, r], cross))
            out.append(remote(kv_slot(ref, r, cross), kv_slot(ref, r, cross), kv_s.at[i, 2, r], kv_r.at[i, 2, r], sib))
        return out

    NCH = 4
    CT = T // NCH

    def phase_three(r, carry):
        mi, iv = expand(norm_tables(1, r))
        tab = table_of(jnp.concatenate([mi, iv], axis=1))

        def chunk(i, c2):
            rows = pl.ds(pl.multiple_of(i * CT, 16), CT)
            xrows = pl.ds(pl.multiple_of(OFF + i * CT, 16), CT)
            sp = dot(metab[r, xrows], tab)
            n = nrm2[r, rows] * sp[:, C : 2 * C] - sp[:, :C]
            y = n * gains[3:4, :] + gains[4:5, :]
            t, d = mish_parts(y)
            nrm2[r, rows] = n
            der2[r, rows] = d
            res = y * t + feat[r, rows].astype(F32)
            resid[r, rows] = res
            m, rs = layer_norm_parts(res)
            n3[r, rows] = m
            rs3[r, rows] = jnp.broadcast_to(rs, (CT, 128))
            low = (m * gains[5:6, :] + gains[6:7, :]).astype(BF)
            ll1[r, rows] = low
            qkv = dot(low, broad[:, : 3 * INNER])
            qs[r, rows] = (qkv[:, :INNER].astype(BF).astype(F32) * HD ** (-0.5)).astype(BF)
            krows = pl.ds(pl.multiple_of(f * T + i * CT, 16), CT)
            kall[r, krows] = qkv[:, INNER : 2 * INNER].astype(BF)
            vall[r, krows] = qkv[:, 2 * INNER :].astype(BF)
            return c2

        lax.fori_loop(0, NCH, chunk, 0)
        cps = kv_copies(r)
        for i in (0, 1, 3, 4):
            cps[i].start()
        return carry

    lax.fori_loop(0, R, phase_three, 0)

    @pl.when(f < 3)
    def _():
        cot_up.wait_recv()

    down = 6 * C

    def phase_down_back(r, carry):
        gy = gyext[r, 0:HT]
        even = dot_nt(gy, narrow[down + C : down + 2 * C, :])
        own_gy = dot_nt(gy, narrow[down + 2 * C : down + 3 * C, :])
        nxt = dot_nt(gyext[r], narrow[down : down + C, :])
        zs[0, 0 : HT + 16] = nxt
        for hh in range(2):
            cols = slice(hh * 128, hh * 128 + 128)
            pm = r3s[2, pl.ds(8 + 1, HT, stride=2), :]
            nm = r3s[3, pl.ds(8 + 1, HT, stride=2), :]
            gr3[r, hh, pl.ds(0, HT, stride=2), :] = even[:, cols]
            gr3[r, hh, pl.ds(1, HT, stride=2), :] = own_gy[:, cols] * pm + zs[0, 1 : HT + 1, cols] * nm
        return carry

    def masks_strided(r):
        r3s[2, 8 : 8 + T] = jnp.broadcast_to(own_prev(r), (T, 128))
        r3s[3, 8 : 8 + T] = jnp.broadcast_to(own_next(r), (T, 128))

    def down_back(r, carry):
        masks_strided(r)
        phase_down_back(r, carry)
        ggrad[11:12, :] += colsum(gyext[r, 0:HT].astype(F32))
        for hh in range(2):
            gf[r, :, hh * 128 : hh * 128 + 128] = gr3[r, hh].astype(BF)
        ggrad[10:11, :] += colsum(gf[r].astype(F32))
        return carry

    lax.fori_loop(0, R, down_back, 0)

    def relay(r, carry):
        cps = kv_copies(r)
        for i in (1, 4):
            cps[i].wait_recv()
            cps[i + 1].start()
        return carry

    lax.fori_loop(0, R, relay, 0)

    alpha = jnp.exp(hidden[1:2, :])
    inv_beta = jnp.exp(-hidden[2:3, :])
    alpha_beta = alpha * inv_beta
    NK = L // 256
    lane128 = iota((T, 128), 1)

    def dkv_copies(r):
        out = []
        for i in range(2):
            blk = lambda g: part.at[r, i, pl.ds(pl.multiple_of(g * T, 128), T)]
            out.append(remote(blk(sib), rbuf.at[r, i, 0], dkv_s.at[i, 0, r], dkv_r.at[i, 0, r], sib))
            out.append(remote(blk(diag), rbuf.at[r, i, 1], dkv_s.at[i, 1, r], dkv_r.at[i, 1, r], sib))
            out.append(remote(sumbuf.at[r, i], rbuf2.at[r, i], dkv_s.at[i, 2, r], dkv_r.at[i, 2, r], cross))
        return out

    def phase_four(r, carry):
        cps = kv_copies(r)
        for i in (0, 2, 3, 5):
            cps[i].wait_recv()
        for i in range(6):
            cps[i].wait_send()
        kt[...] = kall[r].T
        vt[...] = vall[r].T
        qv = qs[r]
        ohq = jnp.where(lane128 < 8, meta[r, OFF : OFF + T], 0.0).astype(BF)
        zero_q = jnp.zeros((T, 128), BF)
        q_heads = [jnp.where(lane128 // HD == h, qv, zero_q) for h in range(H)]
        for h in range(H):
            qa = jnp.concatenate([q_heads[h], ohq], axis=1)

            def score(i, m):
                keys = pl.ds(pl.multiple_of(i * 256, 256), 256)
                ka = jnp.concatenate([kall[r, keys], keymask[r, keys]], axis=1)
                s = dot_nt(ka, qa)
                sbuf[keys] = s
                return jnp.maximum(m, jnp.max(s.reshape(32, 8, T), axis=0))

            m8 = lax.fori_loop(0, NK, score, jnp.full((8, T), -3e38, F32))
            m1 = jnp.max(m8, axis=0, keepdims=True)

            def expo(i, l8):
                keys = pl.ds(pl.multiple_of(i * 256, 256), 256)
                e = jnp.exp(sbuf[keys] - m1)
                ebuf[h, keys] = e.astype(BF)
                return l8 + jnp.sum(e.reshape(32, 8, T), axis=0)

            l8 = lax.fori_loop(0, NK, expo, jnp.zeros((8, T), F32))
            inv = 1.0 / jnp.sum(l8, axis=0, keepdims=True)
            invl[h] = jnp.broadcast_to(inv, (8, T))
            otb[h * HD : (h + 1) * HD, :] = dot(vt[h * HD : (h + 1) * HD, :], ebuf[h]) * inv
        att[r] = otb[...].T.astype(BF)

        def ff_chunk(i, c2):
            rows = pl.ds(pl.multiple_of(i * CT, 16), CT)
            res2 = resid[r, rows] + (dot_nt(att[r, rows], broad[:, 3 * INNER : 4 * INNER]) + gains[7:8, :])
            n, rs = layer_norm_parts(res2)
            low = (n * gains[8:9, :] + gains[9:10, :]).astype(BF)
            nl2[r, rows] = low
            gfr = gf[r, rows]
            out = jnp.zeros((CT, C), F32)
            back = jnp.zeros((CT, C), F32)
            for b in range(4):
                cols = slice(b * 256, b * 256 + 256)
                w_in = broad[:, 4 * INNER + b * 256 : 4 * INNER + b * 256 + 256]
                w_out = narrow[tw + TE + b * 256 : tw + TE + b * 256 + 256, :]
                inner = dot(low, w_in) + hidden[0:1, cols]
                gs = dot_nt(gfr, w_out)
                _, s, c = reduced_angle(inner * alpha[:, cols])
                s2 = s * s
                sc2 = (2.0 * s) * c
                sh = (inner + s2 * inv_beta[:, cols]).astype(BF)
                shaped[r, rows, cols] = sh
                gi = (gs * (1.0 + sc2 * alpha_beta[:, cols])).astype(BF)
                ginner[r, rows, cols] = gi
                hgrad[0:1, cols] += colsum(gi.astype(F32))
                hgrad[1:2, cols] += colsum(gs * inner * sc2)
                hgrad[2:3, cols] += colsum(gs * s2)
                out = out + dot(sh, w_out)
                back = back + dot_nt(gi, w_in)
            r3 = (res2 + (out + gains[10:11, :])).astype(BF)
            r3b[r, rows] = r3
            g_in = jnp.concatenate([gr3[r, 0, rows], gr3[r, 1, rows]], axis=1)
            ggrad[8:9, :] += colsum(back * n)
            ggrad[9:10, :] += colsum(back)
            g_res2 = g_in + layer_norm_back(back, n, rs, gains[8:9, :])
            gr2[r, rows] = g_res2
            low_g = g_res2.astype(BF)
            gm[r, rows] = low_g
            ggrad[7:8, :] += colsum(low_g.astype(F32))
            dos[rows] = dot(low_g, broad[:, 3 * INNER : 4 * INNER]).astype(BF).astype(F32)
            return c2

        lax.fori_loop(0, NCH, ff_chunk, 0)

        @pl.when(f < 3)
        def _():
            to_next(r3b.at[r, pl.ds(T - 16, 16)], r3b.at[r, pl.ds(T, 16)], r3_s.at[r], r3_r.at[r]).start()

        dot_t = dos[...].T
        for h in range(H):
            hrows = slice(h * HD, (h + 1) * HD)
            dost[hrows, :] = dot_t[hrows] * invl[h, 0:1, :]
        dscaled = dost[...].T.astype(BF)
        zero_t = jnp.zeros((HD, T), BF)
        d_rows, d_cols = [], []
        for h in range(H):
            hrows = slice(h * HD, (h + 1) * HD)
            d_rows.append(colsum(otb[hrows, :] * dost[hrows, :]))
            dh = dost[hrows, :].astype(BF)
            d_cols.append(jnp.concatenate([dh, zero_t] if h == 0 else [zero_t, dh], axis=0))
        d_heads = [jnp.where(lane128 // HD == h, dscaled, zero_q) for h in range(H)]
        dq[...] = jnp.zeros((INNER, T), F32)

        def key_grad(i, c2):
            keys = pl.ds(pl.multiple_of(i * 256, 256), 256)
            dk = jnp.zeros((256, INNER), F32)
            dv = jnp.zeros((256, INNER), F32)
            for h in range(H):
                hrows = slice(h * HD, (h + 1) * HD)
                eh = ebuf[h, keys]
                dp = dot(vall[r, keys], d_cols[h])
                ds = (eh.astype(F32) * (dp - d_rows[h])).astype(BF)
                dk = dk + dot(ds, q_heads[h])
                dv = dv + dot(eh, d_heads[h])
                dq[hrows, :] += dot(kt[hrows, keys], ds)
            part[r, 0, keys] = dk.astype(BF)
            part[r, 1, keys] = dv.astype(BF)
            return c2

        lax.fori_loop(0, NK, key_grad, 0)
        dqkv[r, :, 0:INNER] = (dq[...].T * HD ** (-0.5)).astype(BF)
        cps = dkv_copies(r)
        for i in (1, 4, 0, 3):
            cps[i].start()
        return carry

    lax.fori_loop(0, R, phase_four, 0)

    def phase_sum(r, carry):
        cps = dkv_copies(r)
        for i in (1, 4):
            cps[i].wait_recv()
        blk = pl.ds(pl.multiple_of(cross * T, 128), T)
        for i in range(2):
            sumbuf[r, i] = (part[r, i, blk].astype(F32) + rbuf[r, i, 1].astype(F32)).astype(BF)
        for i in (2, 5):
            cps[i].start()
        return carry

    lax.fori_loop(0, R, phase_sum, 0)

    flat = lambda ref: ref[...].reshape(R * T, ref.shape[2])
    gf_all = flat(gf)
    for b in range(4):
        cols = slice(b * 256, b * 256 + 256)
        ngrad[tw + TE + b * 256 : tw + TE + b * 256 + 256, :] = dot_tn(
            shaped[:, :, cols].reshape(R * T, 256), gf_all
        ).astype(BF)
        bgrad[:, 4 * INNER + b * 256 : 4 * INNER + b * 256 + 256] = dot_tn(
            flat(nl2), ginner[:, :, cols].reshape(R * T, 256)
        ).astype(BF)
    bgrad[:, 3 * INNER : 4 * INNER] = dot_tn(flat(gm), flat(att)).astype(BF)
    hgrad[1:2, :] = hgrad[1:2, :] * alpha_beta
    hgrad[2:3, :] = hgrad[2:3, :] * (-inv_beta)

    zs[:, 0:C, :] = jnp.zeros((3, C, C), F32)

    def down_forward(r, carry):
        @pl.when(f > 0)
        def _():
            to_next(r3b.at[r, pl.ds(T - 16, 16)], r3b.at[r, pl.ds(T, 16)], r3_s.at[r], r3_r.at[r]).wait_recv()

        @pl.when(f < 3)
        def _():
            to_next(r3b.at[r, pl.ds(T - 16, 16)], r3b.at[r, pl.ds(T, 16)], r3_s.at[r], r3_r.at[r]).wait_send()

        @pl.when(f == 0)
        def _():
            r3b[r, T : T + 16, :] = jnp.zeros((16, C), BF)

        masks_strided(r)
        for hh in range(2):
            cols = slice(hh * 128, hh * 128 + 128)
            r3s[hh, 8 : 8 + T] = r3b[r, 0:T, cols].astype(F32)
            r3s[hh, 0:8] = r3b[r, T : T + 16, cols].astype(F32)[8:16]
        even = jnp.concatenate([r3s[hh, pl.ds(8, HT, stride=2), :] for hh in range(2)], axis=1).astype(BF)
        m_after = r3s[3, pl.ds(8, HT, stride=2), :]
        m_before = r3s[2, pl.ds(8, HT, stride=2), :]
        odd = jnp.concatenate([r3s[hh, pl.ds(9, HT, stride=2), :] * m_after for hh in range(2)], axis=1).astype(BF)
        before = jnp.concatenate([r3s[hh, pl.ds(7, HT, stride=2), :] * m_before for hh in range(2)], axis=1).astype(BF)
        gy = cot[r]
        out = gains[11:12, :]
        for j, blk in enumerate((before, even, odd)):
            w = slice(down + j * C, down + (j + 1) * C)
            out = out + dot(blk, narrow[w, :])
            zs[j, 0:C, :] += dot_tn(blk, gy)
        fout[r] = out.astype(BF)
        return carry

    lax.fori_loop(0, R, down_forward, 0)
    for j in range(3):
        ngrad[down + j * C : down + (j + 1) * C, :] = zs[j, 0:C, :].astype(BF)

    def mean_tables(phase, r, norm_phase):
        tot = total_stats(phase, r) / jnp.maximum(counts[r], 1.0)
        lanes = iota((8, 128), 1) < G
        m1 = jnp.where(lanes, tot, 0.0)
        m2 = jnp.where(lanes, pltpu.roll(tot, 128 - G, 1), 0.0)
        nt = (statout[norm_phase, r] + statin[norm_phase, r, 0] + statin[norm_phase, r, 1] + statin[norm_phase, r, 2]) / jnp.maximum(counts[r], 1.0)
        second = pltpu.roll(nt, 128 - G, 1)
        iv = jnp.where(lanes, lax.rsqrt(jnp.maximum(second - nt * nt, 0.0) + EPS_NORM), 0.0)
        return m1 * iv, m2 * iv, iv

    def norm_back_start(phase, r, d, n, gain_row):
        ggrad[gain_row : gain_row + 1, :] += colsum(d * n)
        ggrad[gain_row + 1 : gain_row + 2, :] += colsum(d)
        scaled = d * gains[gain_row : gain_row + 1, :]
        dn[r] = scaled
        oh = ohrow[r].astype(BF)
        send_stats(phase, r, segment_sums(oh, scaled), segment_sums(oh, scaled * n))

    def phase_five(r, carry):
        cps = dkv_copies(r)
        for i in (0, 3, 2, 5):
            cps[i].wait_recv()
        for i in range(6):
            cps[i].wait_send()
        blk = pl.ds(pl.multiple_of(f * T, 128), T)
        for i in range(2):
            tot = part[r, i, blk].astype(F32) + rbuf[r, i, 0].astype(F32) + rbuf2[r, i].astype(F32)
            dqkv[r, :, (i + 1) * INNER : (i + 2) * INNER] = tot.astype(BF)
        back = dot_nt(dqkv[r], broad[:, : 3 * INNER])
        n = n3[r]
        ggrad[5:6, :] += colsum(back * n)
        ggrad[6:7, :] += colsum(back)
        g_res = gr2[r] + layer_norm_back(back, n, rs3[r][:, 0:1], gains[5:6, :])
        gr2[r] = g_res
        norm_back_start(2, r, g_res * der2[r], nrm2[r], 3)
        return carry

    lax.fori_loop(0, R, phase_five, 0)
    bgrad[:, : 3 * INNER] = dot_tn(flat(ll1), flat(dqkv)).astype(BF)

    def gh_copies(phase, r):
        return (
            to_next(g2.at[r, pl.ds(OFF + T - 16, 16)], g2.at[r, pl.ds(OFF - 16, 16)], gh_s.at[phase, 0, r], gh_r.at[phase, 0, r]),
            to_prev(g2.at[r, pl.ds(OFF, 16)], g2.at[r, pl.ds(OFF + T, 16)], gh_s.at[phase, 1, r], gh_r.at[phase, 1, r]),
        )

    def norm_back_end(phase, r, n, which):
        a, b, iv = expand(mean_tables(phase, r, which))
        tab = table_of(jnp.concatenate([a, b, iv], axis=1))
        sp = dot(metab[r, OFF : OFF + T], tab)
        g = dn[r] * sp[:, 2 * C :] - sp[:, :C] - n * sp[:, C : 2 * C]
        g2[r, OFF : OFF + T] = g.astype(BF)
        down_cp, up_cp = gh_copies(which, r)

        @pl.when(f < 3)
        def _():
            down_cp.start()

        @pl.when(f > 0)
        def _():
            up_cp.start()

    def conv_back(which, r, first_row):
        down_cp, up_cp = gh_copies(which, r)

        @pl.when(f < 3)
        def _():
            down_cp.wait_send()
            up_cp.wait_recv()

        @pl.when(f > 0)
        def _():
            up_cp.wait_send()
            down_cp.wait_recv()

        @pl.when(f == 0)
        def _():
            g2[r, OFF - 16 : OFF, :] = jnp.zeros((16, C), BF)

        @pl.when(f == 3)
        def _():
            g2[r, OFF + T : OFF + T + 16, :] = jnp.zeros((16, C), BF)

        g = g2[r].astype(F32)
        zs[0] = g * meta[r, :, 24:25]
        zs[2] = g * meta[r, :, 25:26]
        g3[r, :, 0:C] = zs[0, OFF + 1 : OFF + T + 1].astype(BF)
        g3[r, :, C : 2 * C] = g2[r, OFF : OFF + T]
        g3[r, :, 2 * C : 3 * C] = zs[2, OFF - 1 : OFF + T - 1].astype(BF)
        out = jnp.zeros((T, C), F32)
        for j in range(3):
            out = out + dot_nt(g3[r, :, j * C : (j + 1) * C], narrow[first_row + j * C : first_row + (j + 1) * C, :])
        return out

    def kernel_grad(src, first_row):
        u = src[:, OFF : OFF + T, :].reshape(R * T, C)
        for j in range(3):
            ngrad[first_row + j * C : first_row + (j + 1) * C, :] = dot_tn(
                u, g3[:, :, j * C : (j + 1) * C].reshape(R * T, C)
            ).astype(BF)

    def phase_six(r, carry):
        norm_back_end(2, r, nrm2[r], 1)
        return carry

    lax.fori_loop(0, R, phase_six, 0)

    def phase_seven(r, carry):
        gh = conv_back(1, r, 3 * C)
        oh = ohrow[r].astype(BF)
        tgr = segment_sums(oh, gh)
        tg[pl.ds(pl.multiple_of(8 * r, 8), 8), :] = tgr
        ggrad[2:3, :] += colsum(tgr)
        norm_back_start(3, r, gh * der1[r, OFF : OFF + T], nrm1[r, OFF : OFF + T], 0)
        return carry

    lax.fori_loop(0, R, phase_seven, 0)
    kernel_grad(u2, 3 * C)
    t_hi, t_lo = split2(tg[...])
    eb = emb[...].astype(BF)
    ngrad[tw : tw + TE, :] = (dot_tn(eb, t_hi) + dot_tn(eb, t_lo)).astype(BF)

    def phase_eight(r, carry):
        norm_back_end(3, r, nrm1[r, OFF : OFF + T], 0)
        return carry

    lax.fori_loop(0, R, phase_eight, 0)

    def phase_nine(r, carry):
        igrad[r] = gr2[r] + conv_back(0, r, 0)
        return carry

    lax.fori_loop(0, R, phase_nine, 0)
    kernel_grad(uext, 0)

    @pl.when(f < 3)
    def _():
        feat_down.wait_send()

    @pl.when(f > 0)
    def _():
        feat_up.wait_send()
        cot_up.wait_send()


def run_main(feat, ids, steps, cot, narrow, broad, gains, hidden):
    R, T, _ = feat.shape
    L = ids.shape[1]
    TX = T + 2 * OFF
    vm = lambda shape, dt=F32: pltpu.VMEM(shape, dt)
    dma = lambda *shape: pltpu.SemaphoreType.DMA(shape)
    scratch = [
        vm((R, TX, C), BF), vm((R, T // 2 + 16, C), BF), vm((R, TX, 128)), vm((R, TX, 128), BF),
        vm((R, 8, T)), vm((R, L, 128), BF), vm((24, L + 256)), vm((R, 8, 128)), vm((8 * R, TE)), vm((8 * R, C)),
        vm((3, TX, C)), vm((R, TX, C)), vm((R, TX, C)), vm((R, TX, C), BF), vm((R, T, C)),
        vm((R, T, C)), vm((R, T, C)), vm((R, T, C)), vm((R, T, 128)), vm((R, T, C), BF), vm((R, T, INNER), BF),
        vm((R, L, INNER), BF), vm((R, L, INNER), BF),
        vm((4, R, 3, 8, 128)), vm((4, R, 8, 128)),
        vm((INNER, L), BF), vm((INNER, L), BF), vm((L, T)), vm((H, L, T), BF), vm((INNER, T)),
        vm((H, 8, T)), vm((T, INNER)), vm((INNER, T)),
        vm((R, 2, T, 128)), vm((R, T, C), BF), vm((R, T, C), BF),
        vm((R, T, FF), BF), vm((R, T, FF), BF), vm((4, T + 8, 128)), vm((R, T + 16, C), BF),
        vm((R, T, C), BF), vm((R, T, INNER), BF), vm((INNER, T)),
        vm((R, 2, L, INNER), BF), vm((R, 2, 2, T, INNER), BF), vm((R, 2, T, INNER), BF), vm((R, 2, T, INNER), BF),
        vm((R, T, 3 * INNER), BF), vm((R, TX, C), BF), vm((8 * R, C)),
        dma(2), dma(2), dma(1), dma(1), dma(4, R, 3), dma(4, R, 3), dma(2, 3, R), dma(2, 3, R),
        dma(2, 3, R), dma(2, 3, R), dma(2, 2, R), dma(2, 2, R), dma(R), dma(R),
    ]
    out_shape = (
        jax.ShapeDtypeStruct((R, T // 2, C), BF),
        jax.ShapeDtypeStruct((R, T, C), F32),
        jax.ShapeDtypeStruct(narrow.shape, BF),
        jax.ShapeDtypeStruct(broad.shape, BF),
        jax.ShapeDtypeStruct((16, C), F32),
        jax.ShapeDtypeStruct((8, FF), F32),
    )
    spec = pl.BlockSpec(memory_space=pltpu.VMEM)
    return pl.pallas_call(
        main_kernel,
        out_shape=out_shape,
        in_specs=[spec] * 8,
        out_specs=tuple([spec] * 6),
        scratch_shapes=scratch,
        compiler_params=pltpu.CompilerParams(collective_id=0, has_side_effects=True, vmem_limit_bytes=63 * 2**20),
        cost_estimate=pl.CostEstimate(flops=2 * 10**10, bytes_accessed=2 * 10**7, transcendentals=10**7),
    )(feat, ids, steps, cot, narrow, broad, gains, hidden)


def adam_update(grad, master, first, second, rate):
    moment = BETA_ONE * first + (1.0 - BETA_ONE) * grad
    square = BETA_TWO * second + (1.0 - BETA_TWO) * grad * grad
    corrected = moment / (1.0 - BETA_ONE**STEP)
    scaled = jnp.sqrt(square / (1.0 - BETA_TWO**STEP)) + EPS_ADAM
    return (moment, square, master - rate * (corrected / scaled + DECAY_RATE * master))


def local(
    features, segment_ids, timesteps, cotangent, narrow_slab, broad_slab, model_gains, hidden_gains,
    narrow_first, narrow_second, broad_first, broad_second, gains_first, gains_second, hidden_first, hidden_second,
):
    narrow_w = lax.all_gather(narrow_slab.astype(BF), "rows", axis=0, tiled=True)
    broad_w = lax.all_gather(broad_slab.astype(BF), "rows", axis=0, tiled=True)
    gains_all = lax.all_gather(model_gains.astype(BF), "rows", axis=1, tiled=True).astype(F32)
    hidden_all = lax.all_gather(hidden_gains.astype(BF), "rows", axis=1, tiled=True).astype(F32)
    steps = timesteps.astype(F32).reshape(-1, 1)
    fout, igrad, ngrad, bgrad, ggrad, hgrad = run_main(
        features, segment_ids, steps, cotangent, narrow_w, broad_w, gains_all, hidden_all
    )
    scat = lambda x, d: lax.psum(
        lax.psum_scatter(x, "rows", scatter_dimension=d, tiled=True), "frames"
    )
    narrow_g = scat(ngrad, 0)
    broad_g = scat(bgrad, 0)
    small = lax.psum((ggrad[:12], hgrad[:3]), ("rows", "frames"))
    i = lax.axis_index("rows")
    gains_g = lax.dynamic_slice_in_dim(small[0], i * model_gains.shape[1], model_gains.shape[1], 1)
    hidden_g = lax.dynamic_slice_in_dim(small[1], i * hidden_gains.shape[1], hidden_gains.shape[1], 1)
    narrow_new = adam_update(narrow_g, narrow_slab, narrow_first, narrow_second, RATE_SLABS)
    broad_new = adam_update(broad_g, broad_slab, broad_first, broad_second, RATE_SLABS)
    gains_new = adam_update(gains_g, model_gains, gains_first, gains_second, RATE_GAINS)
    hidden_new = adam_update(hidden_g, hidden_gains, hidden_first, hidden_second, RATE_GAINS)
    return (
        fout, igrad, *narrow_new, *broad_new, *gains_new, *hidden_new,
        narrow_new[2].astype(BF), broad_new[2].astype(BF),
    )


def solution(mesh):
    rows = P("rows", None)
    cols = P(None, "rows")
    act = P("rows", "frames", None)
    return jax.shard_map(
        local,
        mesh=mesh,
        in_specs=(act, rows, rows, act, rows, rows, cols, cols, rows, rows, rows, rows, cols, cols, cols, cols),
        out_specs=(act, act, rows, rows, rows, rows, rows, rows, cols, cols, cols, cols, cols, cols, rows, rows),
        check_vma=False,
    )
```

time: 671 us -> 416 us (0.62); the launches traced: 659 us -> 416 us
  matrix products: 181 us -> 0 us
  Pallas kernels: 0 us -> 137 us
  local copies, waits for them, and re-layouts: 85.4 us -> 3.36 us
  other arithmetic: 64.8 us -> 10.3 us
  blocking collectives: 170 us -> 124 us
  starting transfers between devices: 18 us -> 0.16 us
    dot_general x95 -> x0, matrix products: 181 us -> none  [the longest x3 29.8 us: ff_backward(): jnp.einsum('tc,fc->tf', grad_low, ff_out, preferred_element_type=jnp.floa...]
    pallas_call x0 -> x1, Pallas kernels: none -> 137 us  [run_main(): pl.pallas_call(main_kernel, out_shape=out_shape, in_specs=[spec] * 8, out...]
    reduce_scatter x2, waiting for transfers between devices: 7.39 us -> 92.4 us  [local(): lax.psum_scatter(x, 'rows', scatter_dimension=d, tiled=True)]
    psum x1, waiting for transfers between devices: 100 us -> 33.3 us  [local(): lax.psum(lax.psum_scatter(x, 'rows', scatter_dimension=d, tiled=True), 'f...]
    psum x5 -> x1, blocking collectives: 88.3 us -> 37.5 us  [local(): small = lax.psum((ggrad[:12], hgrad[:3]), ('rows', 'frames'))]
    slice x29 -> x1, local copies, waits for them, and re-layouts: 29.7 us -> 0.01 us  [local(): small = lax.psum((ggrad[:12], hgrad[:3]), ('rows', 'frames'))]
    reduce_sum x43 -> x0, other arithmetic: 26.3 us -> none  [the longest x2 4.64 us: norm_backward(): shift_grad = jnp.sum(grad_out, axis=(0, 1))]
    ppermute x10 -> x0, starting transfers between devices: 17.7 us -> none  [the longest x4 8.39 us: with_halo(): lax.ppermute(lax.slice_in_dim(block, block.shape[dim] - width, None, axis...]
  transfers between devices with their start and end apart: 16 -> 4, of which waited for: 6 -> 3; matrix products, arithmetic and copies ran while one was open for 13% -> 2% of each run, Pallas kernels for 0% -> 0%
where the time goes in v1:
time: 416 us
  Pallas kernels  137 us (33%)
  waiting for transfers between devices  126 us (30%)
  blocking collectives  124 us (30%)
  between operations  14 us (3%)
  other arithmetic  10.3 us (2%)
    pallas_call x1, Pallas kernels, run_main(): pl.pallas_call(main_kernel, out_shape=out_shape, in_specs=[spec] * 8, out...  137 us
    reduce_scatter x2, waiting for transfers between devices, local(): lax.psum_scatter(x, 'rows', scatter_dimension=d, tiled=True)  92.4 us
    psum x1, blocking collectives, local(): small = lax.psum((ggrad[:12], hgrad[:3]), ('rows', 'frames'))  37.5 us
    all_gather x1, blocking collectives, local(): broad_w = lax.all_gather(broad_slab.astype(BF), 'rows', axis=0, tiled=True)  33.9 us
    psum x1, waiting for transfers between devices, local(): lax.psum(lax.psum_scatter(x, 'rows', scatter_dimension=d, tiled=True), 'f...  33.3 us
    all_gather x1, blocking collectives, local(): lax.all_gather(model_gains.astype(BF), 'rows', axis=1, tiled=True)  32.4 us
    all_gather x1, blocking collectives, local(): lax.all_gather(hidden_gains.astype(BF), 'rows', axis=1, tiled=True)  20.5 us
  transfers between devices with their start and end apart: 4, of which 3 were waited for; matrix products, arithmetic and copies ran while one was open for 2% of the time, Pallas kernels for 0%

profile of v1, /device:TPU:0, one launch (start us, length us, event | category | flops | bytes accessed | tf_op | source)
XLA Modules:
  0.0 415.6 jit_solution(16217871687154820006)
XLA Ops:
  7.2 0.0 all-gather.3.cloned.1.call-start
  7.2 1.8 convert_element_type.40
  9.0 0.0 all-gather.3.cloned.1.call-update
  9.0 0.0 reduce-scatter.5.cloned.1.call-start
  9.1 0.9 convert_element_type.41
  10.0 0.7 convert_bitcast_fusion
  10.7 32.4 %all-gather = bf16[8,32,12]{1,2,0:T(8,128)(2,1)S(1)} all-gather(bf16[1,32,12]{1,2,0:T(8,128)(2,1)S(1)} %convert_bitcast_fusion), channel_id=1, replica_groups=mesh['rows'=8,'frames'=4] {'rows'}, dimensions={0}, use_global_device_ids=true | all-gather | bytes 6912 | tf_op jit(solution)/shard_map/all_gather | solution.py:853
  43.2 0.7 reshape.38
  43.9 0.7 convert_element_type.44
  44.5 20.5 %all_gather.15 = bf16[3,1024]{1,0:T(4,128)(2,1)S(1)} all-gather(bf16[3,128]{1,0:T(4,128)(2,1)S(1)} %convert_element_type.44), channel_id=1, replica_groups=mesh['rows'=8,'frames'=4] {'rows'}, dimensions={1}, use_global_device_ids=true | all-gather | bytes 6912 | tf_op jit(solution)/shard_map/all_gather | solution.py:854
  65.0 0.6 convert_element_type.45.hidden
  65.6 0.7 convert_element_type.39
  66.3 0.7 reshape.39.steps
  67.0 33.9 %all_gather.13.broad = bf16[256,1536]{1,0:T(8,128)(2,1)} all-gather(bf16[32,1536]{1,0:T(8,128)(2,1)S(1)} %convert_element_type.41), channel_id=1, replica_groups=mesh['rows'=8,'frames'=4] {'rows'}, dimensions={0}, use_global_device_ids=true | all-gather | bytes 884736 | tf_op jit(solution)/shard_map/all_gather | solution.py:852
  100.9 0.0 all-gather.3.cloned.1.call-done.narrow
  100.9 137.0 %shard_map.279 = (bf16[3,256,256]{2,1,0:T(8,128)(2,1)}, f32[3,512,256]{2,1,0:T(8,128)}, bf16[4352,256]{1,0:T(8,128)(2,1)}, bf16[256,1536]{1,0:T(8,128)(2,1)}, f32[16,256]{1,0:T(8,128)}, /*index=5*/f32[8,1024]{1,0:T(8,128)}) custom-call(bf16[3,512,256]{2,1,0:T(8,128)(2,1)} %feat.1, s32[3,2048]{1,0:T(4,128)} %ids.1, f32[24,1]{1,0:T(8,128)} %reshape.39.steps, ...), custom_call_target="tpu_custom_call" | custom-call | flops 20000000000 | bytes 20000000 | tf_op jit(solution)/shard_map/pallas_call | solution.py:828
  237.9 0.0 copy-start.13
  237.9 0.0 copy-start.10
  237.9 0.0 copy-start.9
  237.9 0.0 copy-start.11
  237.9 0.0 copy-start.12
  237.9 0.0 copy-start.14
  238.0 0.0 copy-start.15
  238.0 0.0 copy-start.16
  238.0 0.0 copy-start
  238.0 0.0 copy-start.3
  238.0 0.0 copy-start.4
  238.0 0.0 reduce-scatter.5.cloned.1.call-update
  238.0 0.0 reduce-scatter.3.cloned.1.call-start
  238.1 0.7 reduce-scatter.3.cloned.1.call-update
  238.8 0.0 all-reduce.4.cloned.1.call-start
  238.8 0.0 copy-start.2
  238.8 0.0 copy-start.6
  238.9 0.0 copy-start.7
  238.9 0.0 copy-done.13
  238.9 0.0 copy-done.10
  238.9 37.5 %all-reduce = (f32[12,256]{1,0:T(8,128)S(1)}, f32[3,1024]{1,0:T(4,128)S(1)}) all-reduce(f32[12,256]{1,0:T(8,128)S(1)} %bitcast.8, f32[3,1024]{1,0:T(4,128)S(1)} %slice.7), channel_id=1, replica_groups=mesh['rows'=8,'frames'=4] {'rows','frames'}, use_global_device_ids=true, to_apply=%region_4.0 | all-reduce | flops 6144 | bytes 49152 | tf_op jit(solution)/shard_map/psum | solution.py:864
  276.4 0.0 copy-done.9
  276.4 0.0 copy-done.11
  276.4 0.0 copy-done.12
  276.5 0.7 multiply_subtract_fusion.2
  277.2 21.2 %reduce-scatter.5.cloned.1.call-done = bf16[32,1536]{1,0:T(8,128)(2,1)} async-done(((bf16[256,1536]{1,0:T(8,128)(2,1)}), bf16[32,1536]{1,0:T(8,128)(2,1)}) %reduce-scatter.5.cloned.1.call-update) | async-done | bytes 98320 | tf_op jit(solution)/shard_map/reduce_scatter | solution.py:860
  298.4 71.2 %reduce-scatter.3.cloned.1.call-done = bf16[544,256]{1,0:T(8,128)(2,1)} async-done(((bf16[4352,256]{1,0:T(8,128)(2,1)}), bf16[544,256]{1,0:T(8,128)(2,1)}) %reduce-scatter.3.cloned.1.call-update) | async-done | bytes 278544 | tf_op jit(solution)/shard_map/reduce_scatter | solution.py:860
  369.6 0.0 all-reduce.4.cloned.1.call-update
  369.6 0.0 copy-done.14
  369.6 0.0 copy-done.15
  369.6 0.0 copy-done.16
  369.6 0.6 multiply_subtract_fusion.3
  370.3 33.3 %all-reduce.4.cloned.1.call-done = (bf16[544,256]{1,0:T(8,128)(2,1)}, bf16[32,1536]{1,0:T(8,128)(2,1)}) async-done(((bf16[544,256]{1,0:T(8,128)(2,1)}, bf16[32,1536]{1,0:T(8,128)(2,1)}), (bf16[544,256]{1,0:T(8,128)(2,1)}, bf16[32,1536]{1,0:T(8,128)(2,1)})) %all-reduce.4.cloned.1.call-update) | async-done | bytes 376848 | tf_op jit(solution)/shard_map/psum | solution.py:859
  403.5 0.0 copy-done
  403.5 0.0 copy-done.3
  403.5 0.0 copy-done.4
  403.5 0.0 copy-start.5
  403.5 0.0 copy-start.1
  403.6 2.6 fusion.3
  406.2 0.0 copy-done.2
  406.2 0.0 copy-done.6
  406.2 0.0 copy-done.7
  406.2 0.0 copy-done.8
  406.2 0.9 fusion.2
  407.1 0.0 copy-done.5
  407.1 0.7 copy.43
  407.9 0.0 copy-done.1
  407.9 1.1 copy.44
  (3 shorter events, 0.0 us)
Async XLA Ops:
  7.2 93.7 %all-gather.3.cloned.1.call-start = ((), (), s32[]{:S(2)}) async-start(), calls=%async_computation.2 | async-start | bytes 2506752 | tf_op jit(solution)/shard_map/all_gather | solution.py:851
  9.0 289.4 %reduce-scatter.5.cloned.1.call-start = ((), (), s32[]{:S(2)}) async-start(), calls=%async_computation.4 | async-start | bytes 884736 | tf_op jit(solution)/shard_map/reduce_scatter | solution.py:860
  237.9 1.0 copy-start.13
  237.9 1.0 copy-start.10
  237.9 38.5 %copy-start.9 = (f32[12,32]{1,0:T(8,128)S(1)}, f32[12,32]{1,0:T(8,128)}, u32[]{:S(2)}) copy-start(f32[12,32]{1,0:T(8,128)} %param.22) | copy-start | bytes 4612
  237.9 38.5 %copy-start.11 = (f32[12,32]{1,0:T(8,128)S(1)}, f32[12,32]{1,0:T(8,128)}, u32[]{:S(2)}) copy-start(f32[12,32]{1,0:T(8,128)} %param.29) | copy-start | bytes 4612
  237.9 38.5 %copy-start.12 = (f32[12,32]{1,0:T(8,128)S(1)}, f32[12,32]{1,0:T(8,128)}, u32[]{:S(2)}) copy-start(f32[12,32]{1,0:T(8,128)} %param.28) | copy-start | bytes 4612
  237.9 131.7 %copy-start.14 = (f32[3,128]{1,0:T(4,128)S(1)}, f32[3,128]{1,0:T(4,128)}, u32[]{:S(2)}) copy-start(f32[3,128]{1,0:T(4,128)} %param.23) | copy-start | bytes 4612
  238.0 131.7 %copy-start.15 = (f32[3,128]{1,0:T(4,128)S(1)}, f32[3,128]{1,0:T(4,128)}, u32[]{:S(2)}) copy-start(f32[3,128]{1,0:T(4,128)} %param.31) | copy-start | bytes 4612
  238.0 131.7 %copy-start.16 = (f32[3,128]{1,0:T(4,128)S(1)}, f32[3,128]{1,0:T(4,128)}, u32[]{:S(2)}) copy-start(f32[3,128]{1,0:T(4,128)} %param.30) | copy-start | bytes 4612
  238.0 165.6 %copy-start = (f32[544,256]{1,0:T(8,128)S(1)}, f32[544,256]{1,0:T(8,128)}, u32[]{:S(2)}) copy-start(f32[544,256]{1,0:T(8,128)} %param.20) | copy-start | bytes 1671172
  238.0 165.5 %copy-start.3 = (f32[544,256]{1,0:T(8,128)S(1)}, f32[544,256]{1,0:T(8,128)}, u32[]{:S(2)}) copy-start(f32[544,256]{1,0:T(8,128)} %param.25) | copy-start | bytes 1671172
  238.0 165.5 %copy-start.4 = (f32[544,256]{1,0:T(8,128)S(1)}, f32[544,256]{1,0:T(8,128)}, u32[]{:S(2)}) copy-start(f32[544,256]{1,0:T(8,128)} %param.24) | copy-start | bytes 1671172
  238.0 131.5 %reduce-scatter.3.cloned.1.call-start = ((), (), s32[]{:S(2)}) async-start(), calls=%async_computation.3 | async-start | bytes 2506752 | tf_op jit(solution)/shard_map/reduce_scatter | solution.py:860
  238.8 164.7 %all-reduce.4.cloned.1.call-start = ((), (), s32[]{:S(2)}) async-start(), calls=%async_computation.5 | async-start | bytes 753664 | tf_op jit(solution)/shard_map/psum | solution.py:859
  238.8 167.4 %copy-start.2 = (f32[32,1536]{1,0:T(8,128)S(1)}, f32[32,1536]{1,0:T(8,128)}, u32[]{:S(2)}) copy-start(f32[32,1536]{1,0:T(8,128)} %param.21) | copy-start | bytes 589828
  238.8 167.4 %copy-start.6 = (f32[32,1536]{1,0:T(8,128)S(1)}, f32[32,1536]{1,0:T(8,128)}, u32[]{:S(2)}) copy-start(f32[32,1536]{1,0:T(8,128)} %param.27) | copy-start | bytes 589828
  238.9 167.3 %copy-start.7 = (f32[32,1536]{1,0:T(8,128)S(1)}, f32[32,1536]{1,0:T(8,128)}, u32[]{:S(2)}) copy-start(f32[32,1536]{1,0:T(8,128)} %param.26) | copy-start | bytes 589828
  403.5 2.7 copy-start.8
  403.5 3.6 copy-start.5
  403.5 4.3 %copy-start.1 = (f32[3,512,256]{2,1,0:T(8,128)S(1)}, f32[3,512,256]{2,1,0:T(8,128)}, u32[]{:S(2)}) copy-start(f32[3,512,256]{2,1,0:T(8,128)} %get-tuple-element.63) | copy-start | bytes 4718596
Sparse Core Ops, SparseCore 0:
  10.8 54.6 all-gather.2
  238.2 60.1 reduce-scatter.4
  302.3 67.2 reduce-scatter.2
  372.0 31.4 all-reduce.3

commit v2 on v1

--- a/solution.py
+++ b/solution.py
@@ -16,6 +16,8 @@
 G = 8
 NSEG = 8
 STEP = 10
+KC = 4352
+KR = 1536
 INNER = 128
 EPS_NORM = 1e-05
 EPS_ADAM = 1e-08
@@ -138,15 +140,22 @@
     return jnp.sum(x, axis=0, keepdims=True)
 
 
+def piece_rows(first, count, x):
+    return pl.ds(pl.multiple_of(first + x * (count // 2), 16), count // 2)
+
+
 def main_kernel(
-    feat, ids, steps, cot, narrow, broad, gains, hidden,
-    fout, igrad, ngrad, bgrad, ggrad, hgrad,
-    uext, gyext, meta, metab, ohrow, keymask, idp, counts, emb, tterm,
+    NR,
+    feat, ids, steps, cot, narrow_in, broad_in, gains_in, hidden_in,
+    fout, igrad, ngrad, bgrad, small,
+    narrow_s, broad_s, gains, hidden, smallw, packf, hgrad,
+    uext, gyext, metab, ohrow, keymask, idp, counts, emb, tterm,
     zs, nrm1, der1, u2, nrm2, der2, resid, n3, rs3, ll1, qs, kall, vall,
     statin, statout,
     kt, vt, sbuf, ebuf, otb, invl, dos, dost,
     gr3, gf, nl2, shaped, ginner, r3s, r3b, gm, att, dq,
     part, rbuf, rbuf2, sumbuf, dqkv, g2, tg,
+    ga_s, ga_r, gx_s, gx_r, gc_s, gc_r,
     halo_s, halo_r, cot_s, cot_r, stat_s, stat_r, kv_s, kv_r, dkv_s, dkv_r, gh_s, gh_r, r3_s, r3_r,
 ):
     R, T = feat.shape[0], feat.shape[1]
@@ -161,16 +170,116 @@
     diag = 3 - f
     peers = (sib, cross, diag)
 
+    gather = NR > 0
     barrier = pltpu.get_barrier_semaphore()
     for p in peers:
         pl.semaphore_signal(barrier, inc=1, device_id=(rw, p), device_id_type=MESH)
-    pl.semaphore_wait(barrier, 3)
+    for k in range(1, NR):
+        pl.semaphore_signal(barrier, inc=1, device_id=((rw + k) % NR, f), device_id_type=MESH)
+    narrow, broad = (narrow_s, broad_s) if gather else (narrow_in, broad_in)
+    ggrad = small
+    if gather:
+        SH, SB = narrow_in.shape[0], broad_in.shape[0]
+        gx, gc = f // 2, f % 2
+        narrow[pl.ds(pl.multiple_of(rw * SH, 16), SH), :] = narrow_in[...].astype(BF)
+        broad[pl.ds(pl.multiple_of(rw * SB, 16), SB), :] = broad_in[...].astype(BF)
+        packf[...] = jnp.zeros(packf.shape, F32)
+        packf[0:12, 0 : C // NR] = gains_in[...]
+        packf[12:15, :] = hidden_in[...]
+        smallw[rw] = packf[...].astype(BF)
+    else:
+        gains[0:12, :] = gains_in[...]
+        hidden[0:3, :] = hidden_in[...]
+    pl.semaphore_wait(barrier, 3 + max(NR - 1, 0))
 
     def remote(src, dst, ssem, rsem, target):
         return pltpu.make_async_remote_copy(
             src_ref=src, dst_ref=dst, send_sem=ssem, recv_sem=rsem,
             device_id=(rw, target), device_id_type=MESH,
         )
+
+    if gather:
+        conv_first = {0: (0, SH), 1: (SH, 3 * C - SH)}
+        rest = {s: (s * SH, SH) for s in range(2, NR)}
+        rest[1] = (3 * C, 2 * SH - 3 * C)
+
+        def quarter_of(g, kind, s):
+            x, c = g // 2, g % 2
+            if kind == 3:
+                return smallw.at[s]
+            if kind == 2:
+                return broad.at[pl.ds(s * SB, SB), pl.ds(pl.multiple_of((2 * c + x) * (6 * C // 4), 128), 6 * C // 4)]
+            first, count = (conv_first if kind == 0 else rest)[s]
+            return narrow.at[piece_rows(first, count, x), pl.ds(pl.multiple_of(c * 128, 128), 128)]
+
+        def spread_copy(kind, s, k):
+            ref = quarter_of(f, kind, s)
+            return pltpu.make_async_remote_copy(
+                src_ref=ref, dst_ref=ref, send_sem=ga_s.at[kind, k], recv_sem=ga_r.at[kind, s],
+                device_id=((s + k) % NR, f), device_id_type=MESH,
+            )
+
+        def has(kind, s):
+            return {0: s in conv_first, 1: s in rest, 2: True, 3: True}[kind]
+
+        def spread_start(kind):
+            for s in range(NR):
+                if has(kind, s):
+
+                    @pl.when(rw == s)
+                    def _():
+                        for k in range(1, NR):
+                            spread_copy(kind, s, k).start()
+
+        def spread_end(kind):
+            for s in range(NR):
+                if has(kind, s):
+
+                    @pl.when(rw == s)
+                    def _():
+                        for k in range(1, NR):
+                            spread_copy(kind, s, k).wait_send()
+
+        def cross_copy(kind, s):
+            ref = quarter_of(f, kind, s)
+            return remote(ref, ref, gx_s.at[kind, s], gx_r.at[kind, s], cross)
+
+        def sib_copies(kind, s):
+            a, b = quarter_of(f, kind, s), quarter_of(cross, kind, s)
+            return (
+                remote(a, a, gc_s.at[kind, 0, s], gc_r.at[kind, 0, s], sib),
+                remote(b, b, gc_s.at[kind, 1, s], gc_r.at[kind, 1, s], sib),
+            )
+
+        def pass_on(kind, order):
+            for s in order:
+
+                @pl.when(rw != s)
+                def _():
+                    spread_copy(kind, s, 1).wait_recv()
+                    cross_copy(kind, s).start()
+                    sib_copies(kind, s)[0].start()
+
+        def pass_across(kind, order):
+            for s in order:
+
+                @pl.when(rw != s)
+                def _():
+                    cross_copy(kind, s).wait_recv()
+                    sib_copies(kind, s)[1].start()
+
+        def arrive(kind, order):
+            for s in order:
+
+                @pl.when(rw != s)
+                def _():
+                    for cp in sib_copies(kind, s):
+                        cp.wait_recv()
+                        cp.wait_send()
+                    cross_copy(kind, s).wait_send()
+
+        spread_start(3)
+        spread_start(0)
 
     def to_next(src, dst, ssem, rsem):
         return remote(src, dst, ssem, rsem, (f + 1) % 4)
@@ -233,7 +342,6 @@
         )
         block = jnp.concatenate([oh, oh, oh, pn, jnp.zeros((96, n_lane), F32)], axis=0)
         turned = block.T
-        meta[r] = turned[:TX]
         metab[r] = turned[:TX].astype(BF)
         lab_own = iota((8, T), 0).astype(F32)
         ohrow[r] = jnp.where(jnp.broadcast_to(own[r : r + 1], (8, T)) == lab_own, 1.0, 0.0)
@@ -255,15 +363,29 @@
         sign = 1.0 - 2.0 * (k - 2.0 * jnp.floor(k * 0.5))
         both = jnp.concatenate([s * sign, c * sign], axis=1)
         emb[8 * r : 8 * r + 8, :] = both * mish_parts(both)[0]
-    embb = emb[...].astype(BF)
     tw = 9 * C
-    tterm[...] = dot(embb, narrow[tw : tw + TE, :]) + gains[2:3, :]
+
+    if gather:
+        spread_start(1)
+        spread_start(2)
+        pass_on(0, (0, 1))
+        for s in range(NR):
+
+            @pl.when(rw != s)
+            def _():
+                spread_copy(3, s, 1).wait_recv()
+
+        wide = smallw[...].astype(F32)
+        gains[...] = jnp.concatenate([wide[s, :, 0 : C // NR] for s in range(NR)], axis=1)
+        hidden[0:3, :] = jnp.concatenate([wide[s, 12:15, :] for s in range(NR)], axis=1)
+        pass_across(0, (0, 1))
+        arrive(0, (0, 1))
 
     def own_prev(r):
-        return meta[r, OFF : OFF + T, 24:25]
+        return metab[r, OFF : OFF + T, 24:25].astype(F32)
 
     def own_next(r):
-        return meta[r, OFF : OFF + T, 25:26]
+        return metab[r, OFF : OFF + T, 25:26].astype(F32)
 
     def stat_copies(phase, r):
         return [
@@ -306,9 +428,9 @@
         lo, hi = OFF - 16, OFF + T + 16
         n = hi - lo
         v = (
-            zs[0, lo - 1 : hi - 1] * meta[r, lo:hi, 24:25]
+            zs[0, lo - 1 : hi - 1] * metab[r, lo:hi, 24:25].astype(F32)
             + zs[1, lo:hi]
-            + zs[2, lo + 1 : hi + 1] * meta[r, lo:hi, 25:26]
+            + zs[2, lo + 1 : hi + 1] * metab[r, lo:hi, 25:26].astype(F32)
         )
         nrm1[r, lo:hi] = v
         nrm1[r, 0:lo] = jnp.zeros((lo, C), F32)
@@ -319,6 +441,19 @@
         return carry
 
     lax.fori_loop(0, R, phase_one, 0)
+
+    if gather:
+        order = (4, 5, 6, 1, 2, 3, 7)
+        every = tuple(range(NR))
+        pass_on(1, order)
+        pass_on(2, every)
+        pass_across(1, order)
+        pass_across(2, every)
+        arrive(1, order)
+        arrive(2, every)
+        for kind in range(4):
+            spread_end(kind)
+    tterm[...] = dot(emb[...].astype(BF), narrow[tw : tw + TE, :]) + gains[2:3, :]
 
     CH = TX // 4
 
@@ -469,7 +604,7 @@
         kt[...] = kall[r].T
         vt[...] = vall[r].T
         qv = qs[r]
-        ohq = jnp.where(lane128 < 8, meta[r, OFF : OFF + T], 0.0).astype(BF)
+        ohq = jnp.where(lane128 < 8, metab[r, OFF : OFF + T], jnp.zeros((T, 128), BF))
         zero_q = jnp.zeros((T, 128), BF)
         q_heads = [jnp.where(lane128 // HD == h, qv, zero_q) for h in range(H)]
         for h in range(H):
@@ -732,8 +867,8 @@
             g2[r, OFF + T : OFF + T + 16, :] = jnp.zeros((16, C), BF)
 
         g = g2[r].astype(F32)
-        zs[0] = g * meta[r, :, 24:25]
-        zs[2] = g * meta[r, :, 25:26]
+        zs[0] = g * metab[r, :, 24:25].astype(F32)
+        zs[2] = g * metab[r, :, 25:26].astype(F32)
         g3[r, :, 0:C] = zs[0, OFF + 1 : OFF + T + 1].astype(BF)
         g3[r, :, C : 2 * C] = g2[r, OFF : OFF + T]
         g3[r, :, 2 * C : 3 * C] = zs[2, OFF - 1 : OFF + T - 1].astype(BF)
@@ -783,6 +918,10 @@
     lax.fori_loop(0, R, phase_nine, 0)
     kernel_grad(uext, 0)
 
+    for k in range(3):
+        for q in range(FF // C):
+            small[16 + 4 * k + q : 17 + 4 * k + q, :] = hgrad[k : k + 1, q * C : (q + 1) * C]
+
     @pl.when(f < 3)
     def _():
         feat_down.wait_send()
@@ -793,14 +932,18 @@
         cot_up.wait_send()
 
 
-def run_main(feat, ids, steps, cot, narrow, broad, gains, hidden):
+def run_main(fused, feat, ids, steps, cot, narrow, broad, gains, hidden):
     R, T, _ = feat.shape
     L = ids.shape[1]
     TX = T + 2 * OFF
+    NR = fused
     vm = lambda shape, dt=F32: pltpu.VMEM(shape, dt)
     dma = lambda *shape: pltpu.SemaphoreType.DMA(shape)
+    wide_n, wide_b = ((KC, C), (C, KR)) if NR else ((16, 128), (16, 128))
+    slots = max(NR, 1)
     scratch = [
-        vm((R, TX, C), BF), vm((R, T // 2 + 16, C), BF), vm((R, TX, 128)), vm((R, TX, 128), BF),
+        vm(wide_n, BF), vm(wide_b, BF), vm((16, C)), vm((8, FF)), vm((slots, 16, 128), BF), vm((16, 128)), vm((8, FF)),
+        vm((R, TX, C), BF), vm((R, T // 2 + 16, C), BF), vm((R, TX, 128), BF),
         vm((R, 8, T)), vm((R, L, 128), BF), vm((24, L + 256)), vm((R, 8, 128)), vm((8 * R, TE)), vm((8 * R, C)),
         vm((3, TX, C)), vm((R, TX, C)), vm((R, TX, C)), vm((R, TX, C), BF), vm((R, T, C)),
         vm((R, T, C)), vm((R, T, C)), vm((R, T, C)), vm((R, T, 128)), vm((R, T, C), BF), vm((R, T, INNER), BF),
@@ -813,23 +956,23 @@
         vm((R, T, C), BF), vm((R, T, INNER), BF), vm((INNER, T)),
         vm((R, 2, L, INNER), BF), vm((R, 2, 2, T, INNER), BF), vm((R, 2, T, INNER), BF), vm((R, 2, T, INNER), BF),
         vm((R, T, 3 * INNER), BF), vm((R, TX, C), BF), vm((8 * R, C)),
+        dma(4, slots), dma(4, slots), dma(4, slots), dma(4, slots), dma(4, 2, slots), dma(4, 2, slots),
         dma(2), dma(2), dma(1), dma(1), dma(4, R, 3), dma(4, R, 3), dma(2, 3, R), dma(2, 3, R),
         dma(2, 3, R), dma(2, 3, R), dma(2, 2, R), dma(2, 2, R), dma(R), dma(R),
     ]
     out_shape = (
         jax.ShapeDtypeStruct((R, T // 2, C), BF),
         jax.ShapeDtypeStruct((R, T, C), F32),
-        jax.ShapeDtypeStruct(narrow.shape, BF),
-        jax.ShapeDtypeStruct(broad.shape, BF),
-        jax.ShapeDtypeStruct((16, C), F32),
-        jax.ShapeDtypeStruct((8, FF), F32),
+        jax.ShapeDtypeStruct((KC, C), BF),
+        jax.ShapeDtypeStruct((C, KR), BF),
+        jax.ShapeDtypeStruct((32, C), F32),
     )
     spec = pl.BlockSpec(memory_space=pltpu.VMEM)
     return pl.pallas_call(
-        main_kernel,
+        functools.partial(main_kernel, NR),
         out_shape=out_shape,
         in_specs=[spec] * 8,
-        out_specs=tuple([spec] * 6),
+        out_specs=tuple([spec] * 5),
         scratch_shapes=scratch,
         compiler_params=pltpu.CompilerParams(collective_id=0, has_side_effects=True, vmem_limit_bytes=63 * 2**20),
         cost_estimate=pl.CostEstimate(flops=2 * 10**10, bytes_accessed=2 * 10**7, transcendentals=10**7),
@@ -844,27 +987,202 @@
     return (moment, square, master - rate * (corrected / scaled + DECAY_RATE * master))
 
 
+def reduce_kernel(
+    NR,
+    ngrad, bgrad, small, nm, nf, ns, bm, bf_, bs, gm, gf, gs, hm, hf, hs,
+    nmo, nso, nuo, bmo, bso, buo, gmo, gso, guo, hmo, hso, huo, nco, bco,
+    half, bhalf, inh, inb, quart, bquart, inq, inbq, own, bown, got, bgot, full, bfull,
+    s_own, s_in, s_rows, s_all,
+    c_s, c_r, x_s, x_r, d_s, d_r, f_s, f_r, sa_s, sa_r, sb_s, sb_r, sc_s, sc_r,
+):
+    f = lax.axis_index("frames")
+    rw = lax.axis_index("rows")
+    sib = f + 1 - 2 * (f % 2)
+    cross = (f + 2) % 4
+    diag = 3 - f
+    peers = (sib, cross, diag)
+    x, c = f // 2, f % 2
+    SH, SB = nm.shape[0], bm.shape[0]
+    BH, BQ = KR // 2, KR // 4
+
+    def remote(src, dst, ssem, rsem, row, frame):
+        return pltpu.make_async_remote_copy(
+            src_ref=src, dst_ref=dst, send_sem=ssem, recv_sem=rsem,
+            device_id=(row, frame), device_id_type=MESH,
+        )
+
+    barrier = pltpu.get_barrier_semaphore()
+    for p in peers:
+        pl.semaphore_signal(barrier, inc=1, device_id=(rw, p), device_id_type=MESH)
+    for k in range(1, NR):
+        pl.semaphore_signal(barrier, inc=1, device_id=((rw + k) % NR, f), device_id_type=MESH)
+    pl.semaphore_wait(barrier, 3 + NR - 1)
+
+    def cols(core, n):
+        return pl.ds(pl.multiple_of(core * n, 128), n)
+
+    core_n = remote(ngrad.at[:, cols(1 - c, 128)], inh, c_s.at[0], c_r.at[0], rw, sib)
+    core_b = remote(bgrad.at[:, cols(1 - c, BH)], inb, c_s.at[1], c_r.at[1], rw, sib)
+    core_n.start()
+    core_b.start()
+    small_a = [
+        remote(small.at[pl.ds(pl.multiple_of(8 * p, 8), 8)], s_in.at[i], sa_s.at[i], sa_r.at[i], rw, p)
+        for i, p in enumerate(peers)
+    ]
+    for cp in small_a:
+        cp.start()
+    core_n.wait()
+    for s in range(NR):
+        rows = slice(s * SH, (s + 1) * SH)
+        half[s] = (ngrad[rows, cols(c, 128)].astype(F32) + inh[rows].astype(F32)).astype(BF)
+    cross_n = remote(
+        half.at[:, pl.ds(pl.multiple_of((1 - x) * (SH // 2), 16), SH // 2)], inq, x_s.at[0], x_r.at[0], rw, cross
+    )
+    cross_n.start()
+    core_b.wait()
+    bhalf[...] = (bgrad[:, cols(c, BH)].astype(F32) + inb[...].astype(F32)).astype(BF)
+    cross_b = remote(bhalf.at[:, cols(1 - x, BQ)], inbq, x_s.at[1], x_r.at[1], rw, cross)
+    cross_b.start()
+    for cp in small_a:
+        cp.wait()
+    s_own[...] = small[pl.ds(pl.multiple_of(8 * f, 8), 8)] + s_in[0] + s_in[1] + s_in[2]
+    small_b = [remote(s_own, s_rows.at[k - 1], sb_s.at[k - 1], sb_r.at[k - 1], (rw + k) % NR, f) for k in range(1, NR)]
+    for cp in small_b:
+        cp.start()
+    cross_n.wait()
+    own_rows = pl.ds(pl.multiple_of(x * (SH // 2), 16), SH // 2)
+    for s in range(NR):
+        quart[s] = (half[s, own_rows].astype(F32) + inq[s].astype(F32)).astype(BF)
+    direct = []
+    for k in range(1, NR):
+        to = (rw + k) % NR
+        direct.append(remote(quart.at[to], got.at[k - 1], d_s.at[0, k - 1], d_r.at[0, k - 1], to, f))
+        direct[-1].start()
+    cross_b.wait()
+    bquart[...] = (bhalf[:, cols(x, BQ)].astype(F32) + inbq[...].astype(F32)).astype(BF)
+    directb = []
+    for k in range(1, NR):
+        to = (rw + k) % NR
+        rows = pl.ds(pl.multiple_of(to * SB, 16), SB)
+        directb.append(remote(bquart.at[rows], bgot.at[k - 1], d_s.at[1, k - 1], d_r.at[1, k - 1], to, f))
+        directb[-1].start()
+    for cp in small_b:
+        cp.wait()
+    s_all[pl.ds(pl.multiple_of(8 * f, 8), 8)] = (
+        s_own[...] + s_rows[0] + s_rows[1] + s_rows[2] + s_rows[3] + s_rows[4] + s_rows[5] + s_rows[6]
+    )
+    mine = s_all.at[pl.ds(pl.multiple_of(8 * f, 8), 8)]
+    small_c = [remote(mine, mine, sc_s.at[i], sc_r.at[i], rw, p) for i, p in enumerate(peers)]
+    for cp in small_c:
+        cp.start()
+    for cp in direct:
+        cp.wait()
+    total = quart[rw].astype(F32)
+    for k in range(NR - 1):
+        total = total + got[k].astype(F32)
+    blk = full.at[own_rows, cols(c, 128)]
+    full[own_rows, cols(c, 128)] = total.astype(BF)
+    fin = [remote(blk, blk, f_s.at[0, i], f_r.at[0, i], rw, p) for i, p in enumerate(peers)]
+    for cp in fin:
+        cp.start()
+    for cp in directb:
+        cp.wait()
+    totalb = bquart[pl.ds(pl.multiple_of(rw * SB, 16), SB), :].astype(F32)
+    for k in range(NR - 1):
+        totalb = totalb + bgot[k].astype(F32)
+    bcols = pl.ds(pl.multiple_of(c * BH + x * BQ, 128), BQ)
+    bfull[:, bcols] = totalb.astype(BF)
+    finb = [remote(bfull.at[:, bcols], bfull.at[:, bcols], f_s.at[1, i], f_r.at[1, i], rw, p) for i, p in enumerate(peers)]
+    for cp in finb:
+        cp.start()
+
+    for cp in small_c:
+        cp.wait()
+    tot = s_all[...]
+    gains_g = pltpu.roll(tot[0:16], (NR - rw) * (C // NR), 1)[:12, : C // NR]
+    q = rw * (FF // NR) // C
+    off = rw * (FF // NR) % C
+    pick = iota((4, C), 0) == q
+    hid = jnp.concatenate(
+        [jnp.sum(jnp.where(pick, tot[16 + 4 * k : 20 + 4 * k], 0.0), axis=0, keepdims=True) for k in range(3)]
+        + [jnp.zeros((5, C), F32)],
+        axis=0,
+    )
+    hidden_g = pltpu.roll(hid, C - off, 1)[:3, : FF // NR]
+    gmo[...], gso[...], guo[...] = adam_update(gains_g, gm[...], gf[...], gs[...], RATE_GAINS)
+    hmo[...], hso[...], huo[...] = adam_update(hidden_g, hm[...], hf[...], hs[...], RATE_GAINS)
+    for cp in fin:
+        cp.wait()
+    for lo in range(0, SH, 136):
+        rows = slice(lo, lo + 136)
+        m, sq, up = adam_update(full[...][rows].astype(F32), nm[rows], nf[rows], ns[rows], RATE_SLABS)
+        nmo[rows], nso[rows], nuo[rows] = m, sq, up
+    nco[...] = nuo[...].astype(BF)
+    for cp in finb:
+        cp.wait()
+    m, sq, up = adam_update(bfull[...].astype(F32), bm[...], bf_[...], bs[...], RATE_SLABS)
+    bmo[...], bso[...], buo[...] = m, sq, up
+    bco[...] = up.astype(BF)
+
+
+def run_reduce(NR, ngrad, bgrad, small, *state):
+    vm = lambda shape, dt=BF: pltpu.VMEM(shape, dt)
+    dma = lambda *shape: pltpu.SemaphoreType.DMA(shape)
+    SH, SB = KC // NR, C // NR
+    shape = lambda a, dt=F32: jax.ShapeDtypeStruct(a.shape, dt)
+    nm, bm, gm, hm = state[0], state[3], state[6], state[9]
+    out_shape = tuple(shape(a) for a in (nm, bm, gm, hm) for _ in range(3)) + (shape(nm, BF), shape(bm, BF))
+    spec = pl.BlockSpec(memory_space=pltpu.VMEM)
+    scratch = [
+        vm((NR, SH, 128)), vm((C, KR // 2)), vm((KC, 128)), vm((C, KR // 2)),
+        vm((NR, SH // 2, 128)), vm((C, KR // 4)), vm((NR, SH // 2, 128)), vm((C, KR // 4)),
+        vm((16, 128)), vm((16, 128)), vm((NR - 1, SH // 2, 128)), vm((NR - 1, SB, KR // 4)),
+        vm((SH, C)), vm((SB, KR)),
+        vm((8, C), F32), vm((3, 8, C), F32), vm((NR - 1, 8, C), F32), vm((32, C), F32),
+        dma(2), dma(2), dma(2), dma(2), dma(2, NR - 1), dma(2, NR - 1), dma(2, 3), dma(2, 3),
+        dma(3), dma(3), dma(NR - 1), dma(NR - 1), dma(3), dma(3),
+    ]
+    return pl.pallas_call(
+        functools.partial(reduce_kernel, NR),
+        out_shape=out_shape,
+        in_specs=[spec] * 15,
+        out_specs=tuple([spec] * 14),
+        scratch_shapes=scratch,
+        compiler_params=pltpu.CompilerParams(collective_id=1, has_side_effects=True, vmem_limit_bytes=48 * 2**20),
+    )(ngrad, bgrad, small, *state)
+
+
 def local(
     features, segment_ids, timesteps, cotangent, narrow_slab, broad_slab, model_gains, hidden_gains,
     narrow_first, narrow_second, broad_first, broad_second, gains_first, gains_second, hidden_first, hidden_second,
 ):
+    steps = timesteps.astype(F32).reshape(-1, 1)
+    groups = lax.axis_size("rows")
+    if groups == 8:
+        fout, igrad, ngrad, bgrad, small = run_main(
+            groups, features, segment_ids, steps, cotangent, narrow_slab, broad_slab, model_gains, hidden_gains
+        )
+        new = run_reduce(
+            groups, ngrad, bgrad, small,
+            narrow_slab, narrow_first, narrow_second, broad_slab, broad_first, broad_second,
+            model_gains, gains_first, gains_second, hidden_gains, hidden_first, hidden_second,
+        )
+        return (fout, igrad, *new)
     narrow_w = lax.all_gather(narrow_slab.astype(BF), "rows", axis=0, tiled=True)
     broad_w = lax.all_gather(broad_slab.astype(BF), "rows", axis=0, tiled=True)
     gains_all = lax.all_gather(model_gains.astype(BF), "rows", axis=1, tiled=True).astype(F32)
     hidden_all = lax.all_gather(hidden_gains.astype(BF), "rows", axis=1, tiled=True).astype(F32)
-    steps = timesteps.astype(F32).reshape(-1, 1)
-    fout, igrad, ngrad, bgrad, ggrad, hgrad = run_main(
-        features, segment_ids, steps, cotangent, narrow_w, broad_w, gains_all, hidden_all
+    fout, igrad, ngrad, bgrad, small = run_main(
+        0, features, segment_ids, steps, cotangent, narrow_w, broad_w, gains_all, hidden_all
     )
-    scat = lambda x, d: lax.psum(
-        lax.psum_scatter(x, "rows", scatter_dimension=d, tiled=True), "frames"
-    )
-    narrow_g = scat(ngrad, 0)
-    broad_g = scat(bgrad, 0)
-    small = lax.psum((ggrad[:12], hgrad[:3]), ("rows", "frames"))
+    scat = lambda v: lax.psum(lax.psum_scatter(v, "rows", scatter_dimension=0, tiled=True), "frames")
+    narrow_g = scat(ngrad.astype(F32))
+    broad_g = scat(bgrad.astype(F32))
+    small = lax.psum(small, ("rows", "frames"))
     i = lax.axis_index("rows")
-    gains_g = lax.dynamic_slice_in_dim(small[0], i * model_gains.shape[1], model_gains.shape[1], 1)
-    hidden_g = lax.dynamic_slice_in_dim(small[1], i * hidden_gains.shape[1], hidden_gains.shape[1], 1)
+    own = lambda a, n: lax.dynamic_slice_in_dim(a, i * n, n, 1)
+    gains_g = own(small[:12], model_gains.shape[1])
+    hidden_g = own(small[16:28].reshape(3, FF), hidden_gains.shape[1])
     narrow_new = adam_update(narrow_g, narrow_slab, narrow_first, narrow_second, RATE_SLABS)
     broad_new = adam_update(broad_g, broad_slab, broad_first, broad_second, RATE_SLABS)
     gains_new = adam_update(gains_g, model_gains, gains_first, gains_second, RATE_GAINS)

time: 416 us -> 236 us (0.57)
  waiting for transfers between devices: 126 us -> 0 us
  blocking collectives: 124 us -> 0 us
  Pallas kernels: 137 us -> 217 us
  local copies, waits for them, and re-layouts: 3.36 us -> 17.5 us
  between operations: 14 us -> 0.79 us
  other arithmetic: 10.3 us -> 0.68 us
    reduce_scatter x2 -> x0, waiting for transfers between devices: 92.4 us -> none  [local(): lax.psum_scatter(x, 'rows', scatter_dimension=d, tiled=True)]
    all_gather x3 -> x0, blocking collectives: 86.8 us -> none  [the longest x1 33.9 us: local(): broad_w = lax.all_gather(broad_slab.astype(BF), 'rows', axis=0, tiled=True)]
    pallas_call x1 -> x2, Pallas kernels: 137 us -> 217 us  [the longest x1 167 us: run_main(): pl.pallas_call(functools.partial(main_kernel, NR), out_shape=out_shape, i...]
    psum x1 -> x0, blocking collectives: 37.5 us -> none  [local(): small = lax.psum((ggrad[:12], hgrad[:3]), ('rows', 'frames'))]
    psum x1 -> x0, waiting for transfers between devices: 33.3 us -> none  [local(): lax.psum(lax.psum_scatter(x, 'rows', scatter_dimension=d, tiled=True), 'f...]
    unnamed x36 -> x48, local copies, waits for them, and re-layouts: 1.98 us -> 16.8 us
    convert_element_type x7 -> x0, other arithmetic: 7.6 us -> none  [the longest x1 2.63 us: local(): narrow_new[2].astype(BF)]
  transfers between devices with their start and end apart: 4 -> 0, of which waited for: 3 -> 0; matrix products, arithmetic and copies ran while one was open for 2% -> 0% of each run, Pallas kernels for 0% -> 0%
where the time goes in v2:
time: 236 us
  Pallas kernels  217 us (92%)
  local copies, waits for them, and re-layouts  17.5 us (7%)
    pallas_call x1, Pallas kernels, run_main(): pl.pallas_call(functools.partial(main_kernel, NR), out_shape=out_shape, i...  167 us
    pallas_call x1, Pallas kernels, run_reduce(): pl.pallas_call(functools.partial(reduce_kernel, NR), out_shape=out_shape,...  49.5 us
    unnamed x48, local copies, waits for them, and re-layouts  16.8 us

profile of v2, /device:TPU:0, one launch (start us, length us, event | category | flops | bytes accessed | tf_op | source)
XLA Modules:
  0.0 236.0 jit_solution(17957281796041810217)
XLA Ops:
  0.6 0.7 convert_element_type.3
  1.3 0.7 reshape.36.steps
  2.0 0.0 copy-start.1
  2.0 0.0 copy-start.4
  2.0 0.0 copy-start.5
  2.0 0.0 copy-start.8
  2.0 0.0 copy-start.9
  2.0 0.0 copy-start.10
  2.0 0.0 copy-start.11
  2.1 0.0 copy-start.12
  2.1 167.5 %shard_map.279 = (bf16[3,256,256]{2,1,0:T(8,128)(2,1)}, f32[3,512,256]{2,1,0:T(8,128)}, bf16[4352,256]{1,0:T(8,128)(2,1)}, bf16[256,1536]{1,0:T(8,128)(2,1)}, f32[32,256]{1,0:T(8,128)}) custom-call(bf16[3,512,256]{2,1,0:T(8,128)(2,1)} %feat.1, s32[3,2048]{1,0:T(4,128)} %ids.1, f32[24,1]{1,0:T(8,128)} %reshape.36.steps, bf16[3,256,256]{2,1,0:T(8,128)(2,1)} %cot.1, ...), custom_call_target="tpu_custom_call" | custom-call | flops 20000000000 | bytes 20000000 | tf_op jit(solution)/shard_map/pallas_call | solution.py:971
  169.5 0.0 copy-done.1
  169.6 0.0 copy-done.4
  169.6 0.0 copy-done.5
  169.6 0.0 copy-done.8
  169.6 0.0 copy-done.9
  169.6 0.0 copy-done.10
  169.6 0.0 copy-done.11
  169.6 0.0 copy-done.12
  169.6 0.0 copy-start
  169.6 1.1 copy-done
  170.8 0.0 copy-start.2
  170.8 1.1 copy-done.2
  171.8 0.0 copy-start.3
  171.8 1.1 copy-done.3
  172.9 0.0 copy-start.6
  172.9 0.9 copy-done.6
  173.8 0.0 copy-start.7
  173.8 0.8 copy-done.7
  174.5 0.0 copy-start.13
  174.6 0.7 copy-done.13
  175.2 0.0 copy-start.15
  175.2 0.0 copy-start.14
  175.2 49.5 %shard_map.280 = (f32[544,256]{1,0:T(8,128)S(1)}, f32[544,256]{1,0:T(8,128)S(1)}, f32[544,256]{1,0:T(8,128)S(1)}, f32[32,1536]{1,0:T(8,128)S(1)}, f32[32,1536]{1...) custom-call(bf16[4352,256]{1,0:T(8,128)(2,1)} %get-tuple-element.37., ...), custom_call_target="tpu_custom_call" | custom-call | tf_op jit(solution)/shard_map/pallas_call | solution.py:1145
  224.8 0.0 copy-done.15
  224.8 0.7 copy.49
  225.5 0.0 copy-done.14
  225.5 1.1 copy.50
  226.7 0.8 copy.51
  227.5 0.8 copy.52
  228.3 0.8 copy.53
  229.1 0.7 copy.54
  229.8 0.7 copy.55
  230.4 0.7 copy.56
  231.1 0.6 copy.57
  231.7 0.6 copy.58
  232.3 0.6 copy.59
  232.9 0.6 copy.60
  233.5 0.6 copy.61
  234.1 0.6 copy.62
  234.6 0.7 copy.63
  235.4 0.6 copy.64
Async XLA Ops:
  2.0 167.5 %copy-start.1 = (f32[544,256]{1,0:T(8,128)S(1)}, f32[544,256]{1,0:T(8,128)}, u32[]{:S(2)}) copy-start(f32[544,256]{1,0:T(8,128)} %nm.1) | copy-start | bytes 1671172
  2.0 167.5 %copy-start.4 = (f32[32,1536]{1,0:T(8,128)S(1)}, f32[32,1536]{1,0:T(8,128)}, u32[]{:S(2)}) copy-start(f32[32,1536]{1,0:T(8,128)} %bm.1) | copy-start | bytes 589828
  2.0 167.5 %copy-start.5 = (f32[32,1536]{1,0:T(8,128)S(1)}, f32[32,1536]{1,0:T(8,128)}, u32[]{:S(2)}) copy-start(f32[32,1536]{1,0:T(8,128)} %bf_.1) | copy-start | bytes 589828
  2.0 167.6 %copy-start.8 = (f32[12,32]{1,0:T(8,128)S(1)}, f32[12,32]{1,0:T(8,128)}, u32[]{:S(2)}) copy-start(f32[12,32]{1,0:T(8,128)} %gm.1) | copy-start | bytes 4612
  2.0 167.6 %copy-start.9 = (f32[12,32]{1,0:T(8,128)S(1)}, f32[12,32]{1,0:T(8,128)}, u32[]{:S(2)}) copy-start(f32[12,32]{1,0:T(8,128)} %gf.1) | copy-start | bytes 4612
  2.0 167.6 %copy-start.10 = (f32[12,32]{1,0:T(8,128)S(1)}, f32[12,32]{1,0:T(8,128)}, u32[]{:S(2)}) copy-start(f32[12,32]{1,0:T(8,128)} %gs.1) | copy-start | bytes 4612
  2.0 167.6 %copy-start.11 = (f32[3,128]{1,0:T(4,128)S(1)}, f32[3,128]{1,0:T(4,128)}, u32[]{:S(2)}) copy-start(f32[3,128]{1,0:T(4,128)} %hm.1) | copy-start | bytes 4612
  2.1 167.6 %copy-start.12 = (f32[3,128]{1,0:T(4,128)S(1)}, f32[3,128]{1,0:T(4,128)}, u32[]{:S(2)}) copy-start(f32[3,128]{1,0:T(4,128)} %hf.1) | copy-start | bytes 4612
  169.6 1.1 copy-start
  170.8 1.1 copy-start.2
  171.8 1.1 copy-start.3
  172.9 0.9 copy-start.6
  173.8 0.8 copy-start.7
  174.5 0.7 copy-start.13
  175.2 49.5 %copy-start.15 = (bf16[3,256,256]{2,1,0:T(8,128)(2,1)S(1)}, bf16[3,256,256]{2,1,0:T(8,128)(2,1)}, u32[]{:S(2)}) copy-start(bf16[3,256,256]{2,1,0:T(8,128)(2,1)} %get-tuple-element.70) | copy-start | bytes 1179652
  175.2 50.3 %copy-start.14 = (f32[3,512,256]{2,1,0:T(8,128)S(1)}, f32[3,512,256]{2,1,0:T(8,128)}, u32[]{:S(2)}) copy-start(f32[3,512,256]{2,1,0:T(8,128)} %get-tuple-element.71) | copy-start | bytes 4718596

commit v3 on v2

--- a/solution.py
+++ b/solution.py
@@ -98,19 +98,19 @@
 
 
 def compact(sums, squares):
+    n = sums.shape[0]
     a = jnp.concatenate(split3(sums), axis=0).astype(BF)
     b = jnp.concatenate(split3(squares), axis=0).astype(BF)
     both = dot(a, group_sum_matrix(0)) + dot(b, group_sum_matrix(G))
-    return both[0:8] + both[8:16] + both[16:24]
+    return both[0:n] + both[n : 2 * n] + both[2 * n : 3 * n]
 
 
 def expand(tables):
+    n = tables[0].shape[0]
     stacked = jnp.concatenate([p for t in tables for p in split3(t)], axis=0).astype(BF)
     wide = dot(stacked, group_spread_matrix())
-    return [
-        wide[24 * i : 24 * i + 8] + wide[24 * i + 8 : 24 * i + 16] + wide[24 * i + 16 : 24 * i + 24]
-        for i in range(len(tables))
-    ]
+    part = lambda i: wide[n * i : n * i + n]
+    return [part(3 * i) + part(3 * i + 1) + part(3 * i + 2) for i in range(len(tables))]
 
 
 def table_of(columns):
@@ -147,15 +147,17 @@
 def main_kernel(
     NR,
     feat, ids, steps, cot, narrow_in, broad_in, gains_in, hidden_in,
-    fout, igrad, ngrad, bgrad, small,
-    narrow_s, broad_s, gains, hidden, smallw, packf, hgrad,
-    uext, gyext, metab, ohrow, keymask, idp, counts, emb, tterm,
-    zs, nrm1, der1, u2, nrm2, der2, resid, n3, rs3, ll1, qs, kall, vall,
+    fout, igrad, small, out_n, out_b,
+    narrow_s, broad_s, gains, hidden, smallw, packf, hgrad, ggrad,
+    ngrad_s, bgrad_s, inh, inb, inq, inbq, got, bgot, gfull, bfull, s_pack, s_in, s_own, s_rows, s_all,
+    uext, gyext, metab, ohrow, keymask, idp, counts, emb, tterm, sums, squares, tabs,
+    zs, nrm1, der1, u2, nrm2, der2, resid, ll1, qs, kall, vall,
     statin, statout,
     kt, vt, sbuf, ebuf, otb, invl, dos, dost,
-    gr3, gf, nl2, shaped, ginner, r3s, r3b, gm, att, dq,
+    gf, nl2, shaped, ginner, r3s, r3b, gm, att, dq,
     part, rbuf, rbuf2, sumbuf, dqkv, g2, tg,
     ga_s, ga_r, gx_s, gx_r, gc_s, gc_r,
+    rc_s, rc_r, rx_s, rx_r, rd_s, rd_r, rf_s, rf_r, sa_s, sa_r, sb_s, sb_r, sc_s, sc_r,
     halo_s, halo_r, cot_s, cot_r, stat_s, stat_r, kv_s, kv_r, dkv_s, dkv_r, gh_s, gh_r, r3_s, r3_r,
 ):
     R, T = feat.shape[0], feat.shape[1]
@@ -177,10 +179,9 @@
     for k in range(1, NR):
         pl.semaphore_signal(barrier, inc=1, device_id=((rw + k) % NR, f), device_id_type=MESH)
     narrow, broad = (narrow_s, broad_s) if gather else (narrow_in, broad_in)
-    ggrad = small
+    ngrad, bgrad = (ngrad_s, bgrad_s) if gather else (out_n, out_b)
     if gather:
         SH, SB = narrow_in.shape[0], broad_in.shape[0]
-        gx, gc = f // 2, f % 2
         narrow[pl.ds(pl.multiple_of(rw * SH, 16), SH), :] = narrow_in[...].astype(BF)
         broad[pl.ds(pl.multiple_of(rw * SB, 16), SB), :] = broad_in[...].astype(BF)
         packf[...] = jnp.zeros(packf.shape, F32)
@@ -278,6 +279,7 @@
                         cp.wait_send()
                     cross_copy(kind, s).wait_send()
 
+        every = tuple(range(NR))
         spread_start(3)
         spread_start(0)
 
@@ -348,7 +350,7 @@
         full = jnp.broadcast_to(idv[r : r + 1, 128 : 128 + L], (8, L))
         lab_full = iota((8, L), 0).astype(F32)
         ohf = jnp.where(full == lab_full, 1.0, 0.0)
-        counts[r] = jnp.broadcast_to(jnp.sum(ohf, axis=1, keepdims=True) * float(GROUP), (8, 128))
+        counts[8 * r : 8 * r + 8] = jnp.broadcast_to(jnp.sum(ohf, axis=1, keepdims=True) * float(GROUP), (8, 128))
         km = jnp.concatenate([(1.0 - ohf) * MASK_FILL, jnp.zeros((120, L), F32)], axis=0)
         keymask[r] = km.T.astype(BF)
 
@@ -358,7 +360,8 @@
     half = TE // 2
     freq = jnp.exp(iota((8, half), 1).astype(F32) * (-math.log(10000.0) / half))
     for r in range(R):
-        ang = steps[8 * r : 8 * r + 8, :] * freq
+        turn = jnp.broadcast_to(steps[r : r + 1, :].astype(F32), (8, NSEG))
+        ang = jnp.sum(jnp.where(iota((8, NSEG), 0) == iota((8, NSEG), 1), turn, 0.0), axis=1, keepdims=True) * freq
         k, s, c = reduced_angle(ang)
         sign = 1.0 - 2.0 * (k - 2.0 * jnp.floor(k * 0.5))
         both = jnp.concatenate([s * sign, c * sign], axis=1)
@@ -387,29 +390,42 @@
     def own_next(r):
         return metab[r, OFF : OFF + T, 25:26].astype(F32)
 
-    def stat_copies(phase, r):
+    def stat_copies(phase):
         return [
-            remote(statout.at[phase, r], statin.at[phase, r, i], stat_s.at[phase, r, i], stat_r.at[phase, r, i], peers[i])
+            remote(statout.at[phase], statin.at[phase, i], stat_s.at[phase, i], stat_r.at[phase, i], peers[i])
             for i in range(3)
         ]
 
-    def send_stats(phase, r, sums, squares):
-        statout[phase, r] = compact(sums, squares)
-        for cp in stat_copies(phase, r):
+    def keep_sums(r, first, second):
+        oh = ohrow[r].astype(BF)
+        at = pl.ds(pl.multiple_of(8 * r, 8), 8)
+        sums[at] = segment_sums(oh, first)
+        squares[at] = segment_sums(oh, second)
+
+    def send_stats(phase):
+        statout[phase] = compact(sums[...], squares[...])
+        for cp in stat_copies(phase):
             cp.start()
 
-    def total_stats(phase, r):
-        for cp in stat_copies(phase, r):
-            cp.wait()
-        return statout[phase, r] + statin[phase, r, 0] + statin[phase, r, 1] + statin[phase, r, 2]
-
-    def norm_tables(phase, r):
-        tot = total_stats(phase, r) / jnp.maximum(counts[r], 1.0)
+    def total_stats(phase, wait=True):
+        if wait:
+            for cp in stat_copies(phase):
+                cp.wait()
+        return (statout[phase] + statin[phase, 0] + statin[phase, 1] + statin[phase, 2]) / jnp.maximum(counts[...], 1.0)
+
+    group_lanes = iota((8 * R, 128), 1) < G
+
+    def norm_scale(tot):
         second = pltpu.roll(tot, 128 - G, 1)
-        inv = lax.rsqrt(jnp.maximum(second - tot * tot, 0.0) + EPS_NORM)
-        lanes = iota((8, 128), 1) < G
-        inv = jnp.where(lanes, inv, 0.0)
-        return tot * inv, inv
+        return jnp.where(group_lanes, lax.rsqrt(jnp.maximum(second - tot * tot, 0.0) + EPS_NORM), 0.0)
+
+    def norm_tables(phase):
+        tot = total_stats(phase)
+        inv = norm_scale(tot)
+        tabs[:, 0:C], tabs[:, C : 2 * C] = expand([tot * inv, inv])
+
+    def row_table(r, width):
+        return table_of(tabs[pl.ds(pl.multiple_of(8 * r, 8), 8), 0:width])
 
     def conv_into(r, src, first_row):
         for j in range(3):
@@ -423,7 +439,7 @@
     def _():
         feat_up.wait_recv()
 
-    def phase_one(r, carry):
+    def phase_one(r):
         conv_into(r, uext, 0)
         lo, hi = OFF - 16, OFF + T + 16
         n = hi - lo
@@ -436,31 +452,30 @@
         nrm1[r, 0:lo] = jnp.zeros((lo, C), F32)
         nrm1[r, hi:] = jnp.zeros((TX - hi, C), F32)
         vo = v[OFF - lo : OFF - lo + T]
-        oh = ohrow[r].astype(BF)
-        send_stats(0, r, segment_sums(oh, vo), segment_sums(oh, vo * vo))
-        return carry
-
-    lax.fori_loop(0, R, phase_one, 0)
+        keep_sums(r, vo, vo * vo)
+
+    for r in range(R):
+        phase_one(r)
+        if r == R - 1:
+            send_stats(0)
+        if gather:
+            if r == 0:
+                pass_on(1, (1, 2, 4, 5, 6))
+            elif r == 1:
+                pass_on(2, every)
+                pass_across(1, (1, 2, 4, 5, 6))
 
     if gather:
-        order = (4, 5, 6, 1, 2, 3, 7)
-        every = tuple(range(NR))
-        pass_on(1, order)
-        pass_on(2, every)
-        pass_across(1, order)
-        pass_across(2, every)
-        arrive(1, order)
-        arrive(2, every)
-        for kind in range(4):
-            spread_end(kind)
+        pass_on(1, (3, 7))
+        arrive(1, (1, 2, 4, 5, 6))
     tterm[...] = dot(emb[...].astype(BF), narrow[tw : tw + TE, :]) + gains[2:3, :]
 
     CH = TX // 4
+    tabs[:, 2 * C : 3 * C] = tterm[...]
+    norm_tables(0)
 
     def phase_two(r, carry):
-        mi, iv = expand(norm_tables(0, r))
-        tt = tterm[pl.ds(pl.multiple_of(8 * r, 8), 8), :]
-        tab = table_of(jnp.concatenate([mi, iv, tt], axis=1))
+        tab = row_table(r, 3 * C)
 
         def chunk(i, c2):
             rows = pl.ds(pl.multiple_of(i * CH, 16), CH)
@@ -469,7 +484,7 @@
             y = n * gains[0:1, :] + gains[1:2, :]
             t, d = mish_parts(y)
             nrm1[r, rows] = n
-            der1[r, rows] = d
+            der1[r, rows] = d.astype(BF)
             u2[r, rows] = (y * t + sp[:, 2 * C :]).astype(BF)
             return c2
 
@@ -481,11 +496,16 @@
             + zs[2, OFF + 1 : OFF + T + 1] * own_next(r)
         )
         nrm2[r] = v
-        oh = ohrow[r].astype(BF)
-        send_stats(1, r, segment_sums(oh, v), segment_sums(oh, v * v))
+        keep_sums(r, v, v * v)
         return carry
 
     lax.fori_loop(0, R, phase_two, 0)
+    send_stats(1)
+    if gather:
+        pass_across(2, every)
+        pass_across(1, (3, 7))
+        arrive(2, every)
+    norm_tables(1)
 
     def kv_slot(ref, r, g):
         return ref.at[r, pl.ds(pl.multiple_of(g * T, 128), T)]
@@ -502,8 +522,7 @@
     CT = T // NCH
 
     def phase_three(r, carry):
-        mi, iv = expand(norm_tables(1, r))
-        tab = table_of(jnp.concatenate([mi, iv], axis=1))
+        tab = row_table(r, 2 * C)
 
         def chunk(i, c2):
             rows = pl.ds(pl.multiple_of(i * CT, 16), CT)
@@ -513,12 +532,10 @@
             y = n * gains[3:4, :] + gains[4:5, :]
             t, d = mish_parts(y)
             nrm2[r, rows] = n
-            der2[r, rows] = d
+            der2[r, rows] = d.astype(BF)
             res = y * t + feat[r, rows].astype(F32)
             resid[r, rows] = res
             m, rs = layer_norm_parts(res)
-            n3[r, rows] = m
-            rs3[r, rows] = jnp.broadcast_to(rs, (CT, 128))
             low = (m * gains[5:6, :] + gains[6:7, :]).astype(BF)
             ll1[r, rows] = low
             qkv = dot(low, broad[:, : 3 * INNER])
@@ -552,8 +569,8 @@
             cols = slice(hh * 128, hh * 128 + 128)
             pm = r3s[2, pl.ds(8 + 1, HT, stride=2), :]
             nm = r3s[3, pl.ds(8 + 1, HT, stride=2), :]
-            gr3[r, hh, pl.ds(0, HT, stride=2), :] = even[:, cols]
-            gr3[r, hh, pl.ds(1, HT, stride=2), :] = own_gy[:, cols] * pm + zs[0, 1 : HT + 1, cols] * nm
+            r3s[hh, pl.ds(8, HT, stride=2), :] = even[:, cols]
+            r3s[hh, pl.ds(9, HT, stride=2), :] = own_gy[:, cols] * pm + zs[0, 1 : HT + 1, cols] * nm
         return carry
 
     def masks_strided(r):
@@ -565,20 +582,23 @@
         phase_down_back(r, carry)
         ggrad[11:12, :] += colsum(gyext[r, 0:HT].astype(F32))
         for hh in range(2):
-            gf[r, :, hh * 128 : hh * 128 + 128] = gr3[r, hh].astype(BF)
+            gf[r, :, hh * 128 : hh * 128 + 128] = r3s[hh, 8 : 8 + T].astype(BF)
         ggrad[10:11, :] += colsum(gf[r].astype(F32))
         return carry
 
+    if gather:
+        arrive(1, (3, 7))
+        for kind in range(4):
+            spread_end(kind)
     lax.fori_loop(0, R, down_back, 0)
 
-    def relay(r, carry):
+    def relay(r):
         cps = kv_copies(r)
         for i in (1, 4):
             cps[i].wait_recv()
             cps[i + 1].start()
-        return carry
-
-    lax.fori_loop(0, R, relay, 0)
+
+    relay(0)
 
     alpha = jnp.exp(hidden[1:2, :])
     inv_beta = jnp.exp(-hidden[2:3, :])
@@ -594,6 +614,16 @@
             out.append(remote(blk(diag), rbuf.at[r, i, 1], dkv_s.at[i, 1, r], dkv_r.at[i, 1, r], sib))
             out.append(remote(sumbuf.at[r, i], rbuf2.at[r, i], dkv_s.at[i, 2, r], dkv_r.at[i, 2, r], cross))
         return out
+
+    def phase_sum(r):
+        cps = dkv_copies(r)
+        for i in (1, 4):
+            cps[i].wait_recv()
+        blk = pl.ds(pl.multiple_of(cross * T, 128), T)
+        for i in range(2):
+            sumbuf[r, i] = (part[r, i, blk].astype(F32) + rbuf[r, i, 1].astype(F32)).astype(BF)
+        for i in (2, 5):
+            cps[i].start()
 
     def phase_four(r, carry):
         cps = kv_copies(r)
@@ -631,6 +661,14 @@
             invl[h] = jnp.broadcast_to(inv, (8, T))
             otb[h * HD : (h + 1) * HD, :] = dot(vt[h * HD : (h + 1) * HD, :], ebuf[h]) * inv
         att[r] = otb[...].T.astype(BF)
+
+        @pl.when(r + 1 < R)
+        def _():
+            relay(r + 1)
+
+        @pl.when(r > 0)
+        def _():
+            phase_sum(r - 1)
 
         def ff_chunk(i, c2):
             rows = pl.ds(pl.multiple_of(i * CT, 16), CT)
@@ -661,7 +699,7 @@
                 back = back + dot_nt(gi, w_in)
             r3 = (res2 + (out + gains[10:11, :])).astype(BF)
             r3b[r, rows] = r3
-            g_in = jnp.concatenate([gr3[r, 0, rows], gr3[r, 1, rows]], axis=1)
+            g_in = gfr.astype(F32)
             ggrad[8:9, :] += colsum(back * n)
             ggrad[9:10, :] += colsum(back)
             g_res2 = g_in + layer_norm_back(back, n, rs, gains[8:9, :])
@@ -718,32 +756,193 @@
 
     lax.fori_loop(0, R, phase_four, 0)
 
-    def phase_sum(r, carry):
-        cps = dkv_copies(r)
-        for i in (1, 4):
-            cps[i].wait_recv()
-        blk = pl.ds(pl.multiple_of(cross * T, 128), T)
-        for i in range(2):
-            sumbuf[r, i] = (part[r, i, blk].astype(F32) + rbuf[r, i, 1].astype(F32)).astype(BF)
-        for i in (2, 5):
-            cps[i].start()
-        return carry
-
-    lax.fori_loop(0, R, phase_sum, 0)
+    if gather:
+        rx, rc = f // 2, f % 2
+        shard_blocks = SH // 32
+        n_groups = {1: ((48, 72), (104, 136)), 2: ((24, 48), (72, 104)), 3: ((0, 24),)}
+        b_groups = {1: (4 * INNER, 2 * C), 2: (0, C)}
+        b_at = {1: C, 2: 0}
+
+        def half_cols(core, first, n):
+            return pl.ds(pl.multiple_of(first + core * n, 128), n)
+
+        def core_copies(g):
+            out = [
+                remote(ngrad.at[lo:hi, :, :, half_cols(1 - rc, 0, 128)], inh.at[lo:hi], rc_s.at[g - 1, i], rc_r.at[g - 1, i], sib)
+                for i, (lo, hi) in enumerate(n_groups[g])
+            ]
+            if g in b_groups:
+                first, n = b_groups[g]
+                out.append(
+                    remote(
+                        bgrad.at[:, :, :, half_cols(1 - rc, first, n)], inb.at[:, :, :, b_at[g] : b_at[g] + n],
+                        rc_s.at[g - 1, 2], rc_r.at[g - 1, 2], sib,
+                    )
+                )
+            return out
+
+        def cross_copies(g):
+            out = [
+                remote(ngrad.at[lo:hi, 1 - rx, :, half_cols(rc, 0, 128)], inq.at[lo:hi], rx_s.at[g - 1, i], rx_r.at[g - 1, i], cross)
+                for i, (lo, hi) in enumerate(n_groups[g])
+            ]
+            if g in b_groups:
+                first, n = b_groups[g]
+                out.append(
+                    remote(
+                        bgrad.at[:, 1 - rx, :, half_cols(rc, first, n)], inbq.at[:, :, b_at[g] : b_at[g] + n],
+                        rx_s.at[g - 1, 2], rx_r.at[g - 1, 2], cross,
+                    )
+                )
+            return out
+
+        def owner_copies(g, s, source):
+            out = []
+            for i, (lo, hi) in enumerate(n_groups[g]):
+                a, b = max(lo, shard_blocks * s), min(hi, shard_blocks * (s + 1))
+                if a < b:
+                    out.append(
+                        pltpu.make_async_remote_copy(
+                            src_ref=ngrad.at[a:b, rx, :, half_cols(rc, 0, 128)],
+                            dst_ref=got.at[source, a - shard_blocks * s : b - shard_blocks * s],
+                            send_sem=rd_s.at[g - 1, i, s], recv_sem=rd_r.at[g - 1, i, source],
+                            device_id=(s, f), device_id_type=MESH,
+                        )
+                    )
+            if g in b_groups:
+                first, n = b_groups[g]
+                out.append(
+                    pltpu.make_async_remote_copy(
+                        src_ref=bgrad.at[s, rx, :, half_cols(rc, first, n)],
+                        dst_ref=bgot.at[source, :, b_at[g] : b_at[g] + n],
+                        send_sem=rd_s.at[g - 1, 2, s], recv_sem=rd_r.at[g - 1, 2, source],
+                        device_id=(s, f), device_id_type=MESH,
+                    )
+                )
+            return out
+
+        def red_core(g):
+            for cp in core_copies(g):
+                cp.start()
+
+        def red_cross(g):
+            for cp in core_copies(g):
+                cp.wait()
+            mine = half_cols(rc, 0, 128)
+            for lo, hi in n_groups[g]:
+                ngrad[lo:hi, :, :, mine] = (ngrad[lo:hi, :, :, mine].astype(F32) + inh[lo:hi].astype(F32)).astype(BF)
+            if g in b_groups:
+                first, n = b_groups[g]
+                cols = half_cols(rc, first, n)
+                other = inb[:, :, :, b_at[g] : b_at[g] + n]
+                bgrad[:, :, :, cols] = (bgrad[:, :, :, cols].astype(F32) + other.astype(F32)).astype(BF)
+            for cp in cross_copies(g):
+                cp.start()
+
+        def red_owner(g):
+            for cp in cross_copies(g):
+                cp.wait()
+            mine = half_cols(rc, 0, 128)
+            for lo, hi in n_groups[g]:
+                ngrad[lo:hi, rx, :, mine] = (ngrad[lo:hi, rx, :, mine].astype(F32) + inq[lo:hi].astype(F32)).astype(BF)
+            if g in b_groups:
+                first, n = b_groups[g]
+                cols = half_cols(rc, first, n)
+                other = inbq[:, :, b_at[g] : b_at[g] + n]
+                bgrad[:, rx, :, cols] = (bgrad[:, rx, :, cols].astype(F32) + other.astype(F32)).astype(BF)
+            for s in range(NR):
+
+                @pl.when(rw != s)
+                def _():
+                    for cp in owner_copies(g, s, rw):
+                        cp.start()
+
+        def red_wait(g):
+            for s in range(NR):
+
+                @pl.when(rw != s)
+                def _():
+                    for cp in owner_copies(g, s, rw):
+                        cp.wait_send()
+
+                @pl.when(rw == s)
+                def _():
+                    for k in range(1, NR):
+                        for cp in owner_copies(g, s, (s + k) % NR):
+                            cp.wait_recv()
+
+        def red_finish():
+            mine = half_cols(rc, 0, 128)
+            total = ngrad[pl.ds(shard_blocks * rw, shard_blocks), rx, :, mine].astype(F32)
+            totals = [bgrad[rw, rx, :, half_cols(rc, *b_groups[g])].astype(F32) for g in (1, 2)]
+            for k in range(1, NR):
+                o = (rw + k) % NR
+                total = total + got[o].astype(F32)
+                for j, g in enumerate((1, 2)):
+                    totals[j] = totals[j] + bgot[o, :, b_at[g] : b_at[g] + b_groups[g][1]].astype(F32)
+            gfull[:, rx, :, mine] = total.astype(BF)
+            fin = []
+            blocks = [gfull.at[:, rx, :, mine]]
+            for j, g in enumerate((1, 2)):
+                cols = half_cols(rc, *b_groups[g])
+                bfull[rx, :, cols] = totals[j].astype(BF)
+                blocks.append(bfull.at[rx, :, cols])
+            for j, blk in enumerate(blocks):
+                for i, p in enumerate(peers):
+                    fin.append(remote(blk, blk, rf_s.at[j, i], rf_r.at[j, i], p))
+                    fin[-1].start()
+            return fin
+
+        def small_first():
+            s_pack[...] = small_rows()
+            out = [
+                remote(s_pack.at[pl.ds(pl.multiple_of(8 * p, 8), 8)], s_in.at[i], sa_s.at[i], sa_r.at[i], p)
+                for i, p in enumerate(peers)
+            ]
+            for cp in out:
+                cp.start()
+            return out
+
+        def small_second(first):
+            for cp in first:
+                cp.wait()
+            s_own[...] = s_pack[pl.ds(pl.multiple_of(8 * f, 8), 8)] + s_in[0] + s_in[1] + s_in[2]
+            out = [
+                pltpu.make_async_remote_copy(
+                    src_ref=s_own, dst_ref=s_rows.at[k - 1], send_sem=sb_s.at[k - 1], recv_sem=sb_r.at[k - 1],
+                    device_id=((rw + k) % NR, f), device_id_type=MESH,
+                )
+                for k in range(1, NR)
+            ]
+            for cp in out:
+                cp.start()
+            return out
+
+        def small_third(second):
+            for cp in second:
+                cp.wait()
+            at = pl.ds(pl.multiple_of(8 * f, 8), 8)
+            tot = s_own[...]
+            for k in range(1, NR):
+                tot = tot + s_rows[k - 1]
+            s_all[at] = tot
+            out = [remote(s_all.at[at], s_all.at[at], sc_s.at[i], sc_r.at[i], p) for i, p in enumerate(peers)]
+            for cp in out:
+                cp.start()
+            return out
+
+    def small_rows():
+        hid = [hgrad[k : k + 1, q * C : (q + 1) * C] for k in range(3) for q in range(FF // C)]
+        return jnp.concatenate([ggrad[...]] + hid + [jnp.zeros((4, C), F32)], axis=0)
 
     flat = lambda ref: ref[...].reshape(R * T, ref.shape[2])
-    gf_all = flat(gf)
-    for b in range(4):
-        cols = slice(b * 256, b * 256 + 256)
-        ngrad[tw + TE + b * 256 : tw + TE + b * 256 + 256, :] = dot_tn(
-            shaped[:, :, cols].reshape(R * T, 256), gf_all
-        ).astype(BF)
-        bgrad[:, 4 * INNER + b * 256 : 4 * INNER + b * 256 + 256] = dot_tn(
-            flat(nl2), ginner[:, :, cols].reshape(R * T, 256)
-        ).astype(BF)
-    bgrad[:, 3 * INNER : 4 * INNER] = dot_tn(flat(gm), flat(att)).astype(BF)
-    hgrad[1:2, :] = hgrad[1:2, :] * alpha_beta
-    hgrad[2:3, :] = hgrad[2:3, :] * (-inv_beta)
+
+    def put_n(first, value):
+        n = value.shape[0]
+        ngrad[first // 32 : (first + n) // 32] = value.astype(BF).reshape(n // 32, 2, 16, C)
+
+    def put_b(first, value):
+        bgrad[:, :, :, first : first + value.shape[1]] = value.astype(BF).reshape(C // 32, 2, 16, value.shape[1])
 
     zs[:, 0:C, :] = jnp.zeros((3, C, C), F32)
 
@@ -781,25 +980,34 @@
 
     lax.fori_loop(0, R, down_forward, 0)
     for j in range(3):
-        ngrad[down + j * C : down + (j + 1) * C, :] = zs[j, 0:C, :].astype(BF)
-
-    def mean_tables(phase, r, norm_phase):
-        tot = total_stats(phase, r) / jnp.maximum(counts[r], 1.0)
-        lanes = iota((8, 128), 1) < G
-        m1 = jnp.where(lanes, tot, 0.0)
-        m2 = jnp.where(lanes, pltpu.roll(tot, 128 - G, 1), 0.0)
-        nt = (statout[norm_phase, r] + statin[norm_phase, r, 0] + statin[norm_phase, r, 1] + statin[norm_phase, r, 2]) / jnp.maximum(counts[r], 1.0)
-        second = pltpu.roll(nt, 128 - G, 1)
-        iv = jnp.where(lanes, lax.rsqrt(jnp.maximum(second - nt * nt, 0.0) + EPS_NORM), 0.0)
-        return m1 * iv, m2 * iv, iv
-
-    def norm_back_start(phase, r, d, n, gain_row):
+        put_n(down + j * C, zs[j, 0:C, :])
+
+    gf_all = flat(gf)
+    for b in range(4):
+        cols = slice(b * 256, b * 256 + 256)
+        put_n(tw + TE + b * 256, dot_tn(shaped[:, :, cols].reshape(R * T, 256), gf_all))
+        put_b(4 * INNER + b * 256, dot_tn(flat(nl2), ginner[:, :, cols].reshape(R * T, 256)))
+    put_b(3 * INNER, dot_tn(flat(gm), flat(att)))
+    hgrad[1:2, :] = hgrad[1:2, :] * alpha_beta
+    hgrad[2:3, :] = hgrad[2:3, :] * (-inv_beta)
+    if gather:
+        red_core(1)
+
+    phase_sum(R - 1)
+
+    def mean_tables(phase, norm_phase):
+        tot = total_stats(phase)
+        iv = norm_scale(total_stats(norm_phase, wait=False))
+        m1 = jnp.where(group_lanes, tot, 0.0)
+        m2 = jnp.where(group_lanes, pltpu.roll(tot, 128 - G, 1), 0.0)
+        tabs[:, 0:C], tabs[:, C : 2 * C], tabs[:, 2 * C : 3 * C] = expand([m1 * iv, m2 * iv, iv])
+
+    def norm_back_start(r, d, n, gain_row):
         ggrad[gain_row : gain_row + 1, :] += colsum(d * n)
         ggrad[gain_row + 1 : gain_row + 2, :] += colsum(d)
         scaled = d * gains[gain_row : gain_row + 1, :]
         dn[r] = scaled
-        oh = ohrow[r].astype(BF)
-        send_stats(phase, r, segment_sums(oh, scaled), segment_sums(oh, scaled * n))
+        keep_sums(r, scaled, scaled * n)
 
     def phase_five(r, carry):
         cps = dkv_copies(r)
@@ -812,16 +1020,20 @@
             tot = part[r, i, blk].astype(F32) + rbuf[r, i, 0].astype(F32) + rbuf2[r, i].astype(F32)
             dqkv[r, :, (i + 1) * INNER : (i + 2) * INNER] = tot.astype(BF)
         back = dot_nt(dqkv[r], broad[:, : 3 * INNER])
-        n = n3[r]
+        n, rs = layer_norm_parts(resid[r])
         ggrad[5:6, :] += colsum(back * n)
         ggrad[6:7, :] += colsum(back)
-        g_res = gr2[r] + layer_norm_back(back, n, rs3[r][:, 0:1], gains[5:6, :])
+        g_res = gr2[r] + layer_norm_back(back, n, rs, gains[5:6, :])
         gr2[r] = g_res
-        norm_back_start(2, r, g_res * der2[r], nrm2[r], 3)
+        norm_back_start(r, g_res * der2[r].astype(F32), nrm2[r], 3)
         return carry
 
     lax.fori_loop(0, R, phase_five, 0)
-    bgrad[:, : 3 * INNER] = dot_tn(flat(ll1), flat(dqkv)).astype(BF)
+    send_stats(2)
+    if gather:
+        red_cross(1)
+    put_b(0, dot_tn(flat(ll1), flat(dqkv)))
+    mean_tables(2, 1)
 
     def gh_copies(phase, r):
         return (
@@ -829,10 +1041,8 @@
             to_prev(g2.at[r, pl.ds(OFF, 16)], g2.at[r, pl.ds(OFF + T, 16)], gh_s.at[phase, 1, r], gh_r.at[phase, 1, r]),
         )
 
-    def norm_back_end(phase, r, n, which):
-        a, b, iv = expand(mean_tables(phase, r, which))
-        tab = table_of(jnp.concatenate([a, b, iv], axis=1))
-        sp = dot(metab[r, OFF : OFF + T], tab)
+    def norm_back_end(r, n, which):
+        sp = dot(metab[r, OFF : OFF + T], row_table(r, 3 * C))
         g = dn[r] * sp[:, 2 * C :] - sp[:, :C] - n * sp[:, C : 2 * C]
         g2[r, OFF : OFF + T] = g.astype(BF)
         down_cp, up_cp = gh_copies(which, r)
@@ -845,7 +1055,7 @@
         def _():
             up_cp.start()
 
-    def conv_back(which, r, first_row):
+    def build_g3(which, r):
         down_cp, up_cp = gh_copies(which, r)
 
         @pl.when(f < 3)
@@ -872,6 +1082,8 @@
         g3[r, :, 0:C] = zs[0, OFF + 1 : OFF + T + 1].astype(BF)
         g3[r, :, C : 2 * C] = g2[r, OFF : OFF + T]
         g3[r, :, 2 * C : 3 * C] = zs[2, OFF - 1 : OFF + T - 1].astype(BF)
+
+    def conv_back(r, first_row):
         out = jnp.zeros((T, C), F32)
         for j in range(3):
             out = out + dot_nt(g3[r, :, j * C : (j + 1) * C], narrow[first_row + j * C : first_row + (j + 1) * C, :])
@@ -880,47 +1092,76 @@
     def kernel_grad(src, first_row):
         u = src[:, OFF : OFF + T, :].reshape(R * T, C)
         for j in range(3):
-            ngrad[first_row + j * C : first_row + (j + 1) * C, :] = dot_tn(
-                u, g3[:, :, j * C : (j + 1) * C].reshape(R * T, C)
-            ).astype(BF)
+            put_n(first_row + j * C, dot_tn(u, g3[:, :, j * C : (j + 1) * C].reshape(R * T, C)))
 
     def phase_six(r, carry):
-        norm_back_end(2, r, nrm2[r], 1)
+        norm_back_end(r, nrm2[r], 1)
         return carry
 
     lax.fori_loop(0, R, phase_six, 0)
 
     def phase_seven(r, carry):
-        gh = conv_back(1, r, 3 * C)
+        build_g3(1, r)
+        gh = conv_back(r, 3 * C)
         oh = ohrow[r].astype(BF)
         tgr = segment_sums(oh, gh)
         tg[pl.ds(pl.multiple_of(8 * r, 8), 8), :] = tgr
         ggrad[2:3, :] += colsum(tgr)
-        norm_back_start(3, r, gh * der1[r, OFF : OFF + T], nrm1[r, OFF : OFF + T], 0)
+        norm_back_start(r, gh * der1[r, OFF : OFF + T].astype(F32), nrm1[r, OFF : OFF + T], 0)
         return carry
 
     lax.fori_loop(0, R, phase_seven, 0)
+    send_stats(3)
+    if gather:
+        red_owner(1)
     kernel_grad(u2, 3 * C)
     t_hi, t_lo = split2(tg[...])
     eb = emb[...].astype(BF)
-    ngrad[tw : tw + TE, :] = (dot_tn(eb, t_hi) + dot_tn(eb, t_lo)).astype(BF)
+    put_n(tw, dot_tn(eb, t_hi) + dot_tn(eb, t_lo))
+    if gather:
+        red_core(2)
+    mean_tables(3, 0)
 
     def phase_eight(r, carry):
-        norm_back_end(3, r, nrm1[r, OFF : OFF + T], 0)
+        norm_back_end(r, nrm1[r, OFF : OFF + T], 0)
         return carry
 
     lax.fori_loop(0, R, phase_eight, 0)
 
-    def phase_nine(r, carry):
-        igrad[r] = gr2[r] + conv_back(0, r, 0)
+    if gather:
+        small_a = small_first()
+        red_cross(2)
+    else:
+        small[...] = small_rows()
+
+    def phase_g3(r, carry):
+        build_g3(0, r)
         return carry
 
-    lax.fori_loop(0, R, phase_nine, 0)
+    lax.fori_loop(0, R, phase_g3, 0)
     kernel_grad(uext, 0)
-
-    for k in range(3):
-        for q in range(FF // C):
-            small[16 + 4 * k + q : 17 + 4 * k + q, :] = hgrad[k : k + 1, q * C : (q + 1) * C]
+    if gather:
+        red_core(3)
+        small_b = small_second(small_a)
+        red_owner(2)
+    for r in range(R):
+        igrad[r] = gr2[r] + conv_back(r, 0)
+        if gather and r == 0:
+            red_cross(3)
+        if gather and r == R - 1:
+            red_owner(3)
+    if gather:
+        small_c = small_third(small_b)
+        for g in (1, 2, 3):
+            red_wait(g)
+        fin = red_finish()
+        for cp in small_c:
+            cp.wait()
+        small[...] = s_all[...]
+        for cp in fin:
+            cp.wait()
+        out_n[...] = gfull[...]
+        out_b[...] = bfull[...]
 
     @pl.when(f < 3)
     def _():
@@ -939,33 +1180,50 @@
     NR = fused
     vm = lambda shape, dt=F32: pltpu.VMEM(shape, dt)
     dma = lambda *shape: pltpu.SemaphoreType.DMA(shape)
-    wide_n, wide_b = ((KC, C), (C, KR)) if NR else ((16, 128), (16, 128))
     slots = max(NR, 1)
-    scratch = [
-        vm(wide_n, BF), vm(wide_b, BF), vm((16, C)), vm((8, FF)), vm((slots, 16, 128), BF), vm((16, 128)), vm((8, FF)),
+    if NR:
+        wide = [vm((KC, C), BF), vm((C, KR), BF)]
+        red = [
+            vm((KC // 32, 2, 16, C), BF), vm((C // 32, 2, 16, KR), BF), vm((KC // 32, 2, 16, 128), BF),
+            vm((C // 32, 2, 16, KR // 2), BF), vm((KC // 32, 16, 128), BF), vm((C // 32, 16, KR // 2), BF),
+            vm((NR, KC // NR // 32, 16, 128), BF), vm((NR, 16, KR // 2), BF),
+            vm((KC // NR // 32, 2, 16, C), BF), vm((2, 16, KR), BF),
+        ]
+        outs = ((KC // NR // 32, 2, 16, C), (2, 16, KR))
+    else:
+        wide = [vm((16, 128), BF)] * 2
+        red = [vm((16, 128), BF)] * 10
+        outs = ((KC // 32, 2, 16, C), (C // 32, 2, 16, KR))
+    scratch = wide + [
+        vm((16, C)), vm((8, FF)), vm((slots, 16, 128), BF), vm((16, 128)), vm((8, FF)), vm((16, C)),
+    ] + red + [
+        vm((32, C)), vm((3, 8, C)), vm((8, C)), vm((slots, 8, C)), vm((32, C)),
         vm((R, TX, C), BF), vm((R, T // 2 + 16, C), BF), vm((R, TX, 128), BF),
-        vm((R, 8, T)), vm((R, L, 128), BF), vm((24, L + 256)), vm((R, 8, 128)), vm((8 * R, TE)), vm((8 * R, C)),
-        vm((3, TX, C)), vm((R, TX, C)), vm((R, TX, C)), vm((R, TX, C), BF), vm((R, T, C)),
-        vm((R, T, C)), vm((R, T, C)), vm((R, T, C)), vm((R, T, 128)), vm((R, T, C), BF), vm((R, T, INNER), BF),
+        vm((R, 8, T)), vm((R, L, 128), BF), vm((24, L + 256)), vm((8 * R, 128)), vm((8 * R, TE)), vm((8 * R, C)),
+        vm((8 * R, C)), vm((8 * R, C)), vm((8 * R, 3 * C)),
+        vm((3, TX, C)), vm((R, TX, C)), vm((R, TX, C), BF), vm((R, TX, C), BF), vm((R, T, C)),
+        vm((R, T, C), BF), vm((R, T, C)), vm((R, T, C), BF), vm((R, T, INNER), BF),
         vm((R, L, INNER), BF), vm((R, L, INNER), BF),
-        vm((4, R, 3, 8, 128)), vm((4, R, 8, 128)),
+        vm((4, 3, 8 * R, 128)), vm((4, 8 * R, 128)),
         vm((INNER, L), BF), vm((INNER, L), BF), vm((L, T)), vm((H, L, T), BF), vm((INNER, T)),
         vm((H, 8, T)), vm((T, INNER)), vm((INNER, T)),
-        vm((R, 2, T, 128)), vm((R, T, C), BF), vm((R, T, C), BF),
+        vm((R, T, C), BF), vm((R, T, C), BF),
         vm((R, T, FF), BF), vm((R, T, FF), BF), vm((4, T + 8, 128)), vm((R, T + 16, C), BF),
         vm((R, T, C), BF), vm((R, T, INNER), BF), vm((INNER, T)),
         vm((R, 2, L, INNER), BF), vm((R, 2, 2, T, INNER), BF), vm((R, 2, T, INNER), BF), vm((R, 2, T, INNER), BF),
         vm((R, T, 3 * INNER), BF), vm((R, TX, C), BF), vm((8 * R, C)),
         dma(4, slots), dma(4, slots), dma(4, slots), dma(4, slots), dma(4, 2, slots), dma(4, 2, slots),
-        dma(2), dma(2), dma(1), dma(1), dma(4, R, 3), dma(4, R, 3), dma(2, 3, R), dma(2, 3, R),
+        dma(3, 3), dma(3, 3), dma(3, 3), dma(3, 3), dma(3, 3, slots), dma(3, 3, slots), dma(3, 3), dma(3, 3),
+        dma(3), dma(3), dma(slots), dma(slots), dma(3), dma(3),
+        dma(2), dma(2), dma(1), dma(1), dma(4, 3), dma(4, 3), dma(2, 3, R), dma(2, 3, R),
         dma(2, 3, R), dma(2, 3, R), dma(2, 2, R), dma(2, 2, R), dma(R), dma(R),
     ]
     out_shape = (
         jax.ShapeDtypeStruct((R, T // 2, C), BF),
         jax.ShapeDtypeStruct((R, T, C), F32),
-        jax.ShapeDtypeStruct((KC, C), BF),
-        jax.ShapeDtypeStruct((C, KR), BF),
         jax.ShapeDtypeStruct((32, C), F32),
+        jax.ShapeDtypeStruct(outs[0], BF),
+        jax.ShapeDtypeStruct(outs[1], BF),
     )
     spec = pl.BlockSpec(memory_space=pltpu.VMEM)
     return pl.pallas_call(
@@ -987,118 +1245,26 @@
     return (moment, square, master - rate * (corrected / scaled + DECAY_RATE * master))
 
 
-def reduce_kernel(
+def adam_kernel(
     NR,
-    ngrad, bgrad, small, nm, nf, ns, bm, bf_, bs, gm, gf, gs, hm, hf, hs,
-    nmo, nso, nuo, bmo, bso, buo, gmo, gso, guo, hmo, hso, huo, nco, bco,
-    half, bhalf, inh, inb, quart, bquart, inq, inbq, own, bown, got, bgot, full, bfull,
-    s_own, s_in, s_rows, s_all,
-    c_s, c_r, x_s, x_r, d_s, d_r, f_s, f_r, sa_s, sa_r, sb_s, sb_r, sc_s, sc_r,
+    gfull, bfull, small, nm, nf, ns, bm, bf_, bs, gm, gf, gs, hm, hf, hs, fout_in, igrad_in,
+    fout, igrad, nmo, nso, nuo, bmo, bso, buo, gmo, gso, guo, hmo, hso, huo, nco, bco,
 ):
-    f = lax.axis_index("frames")
+    igrad[...] = igrad_in[...]
+    fout[...] = fout_in[...]
+    SH, SB = nm.shape[0], bm.shape[0]
     rw = lax.axis_index("rows")
-    sib = f + 1 - 2 * (f % 2)
-    cross = (f + 2) % 4
-    diag = 3 - f
-    peers = (sib, cross, diag)
-    x, c = f // 2, f % 2
-    SH, SB = nm.shape[0], bm.shape[0]
-    BH, BQ = KR // 2, KR // 4
-
-    def remote(src, dst, ssem, rsem, row, frame):
-        return pltpu.make_async_remote_copy(
-            src_ref=src, dst_ref=dst, send_sem=ssem, recv_sem=rsem,
-            device_id=(row, frame), device_id_type=MESH,
-        )
-
-    barrier = pltpu.get_barrier_semaphore()
-    for p in peers:
-        pl.semaphore_signal(barrier, inc=1, device_id=(rw, p), device_id_type=MESH)
-    for k in range(1, NR):
-        pl.semaphore_signal(barrier, inc=1, device_id=((rw + k) % NR, f), device_id_type=MESH)
-    pl.semaphore_wait(barrier, 3 + NR - 1)
-
-    def cols(core, n):
-        return pl.ds(pl.multiple_of(core * n, 128), n)
-
-    core_n = remote(ngrad.at[:, cols(1 - c, 128)], inh, c_s.at[0], c_r.at[0], rw, sib)
-    core_b = remote(bgrad.at[:, cols(1 - c, BH)], inb, c_s.at[1], c_r.at[1], rw, sib)
-    core_n.start()
-    core_b.start()
-    small_a = [
-        remote(small.at[pl.ds(pl.multiple_of(8 * p, 8), 8)], s_in.at[i], sa_s.at[i], sa_r.at[i], rw, p)
-        for i, p in enumerate(peers)
-    ]
-    for cp in small_a:
-        cp.start()
-    core_n.wait()
-    for s in range(NR):
-        rows = slice(s * SH, (s + 1) * SH)
-        half[s] = (ngrad[rows, cols(c, 128)].astype(F32) + inh[rows].astype(F32)).astype(BF)
-    cross_n = remote(
-        half.at[:, pl.ds(pl.multiple_of((1 - x) * (SH // 2), 16), SH // 2)], inq, x_s.at[0], x_r.at[0], rw, cross
-    )
-    cross_n.start()
-    core_b.wait()
-    bhalf[...] = (bgrad[:, cols(c, BH)].astype(F32) + inb[...].astype(F32)).astype(BF)
-    cross_b = remote(bhalf.at[:, cols(1 - x, BQ)], inbq, x_s.at[1], x_r.at[1], rw, cross)
-    cross_b.start()
-    for cp in small_a:
-        cp.wait()
-    s_own[...] = small[pl.ds(pl.multiple_of(8 * f, 8), 8)] + s_in[0] + s_in[1] + s_in[2]
-    small_b = [remote(s_own, s_rows.at[k - 1], sb_s.at[k - 1], sb_r.at[k - 1], (rw + k) % NR, f) for k in range(1, NR)]
-    for cp in small_b:
-        cp.start()
-    cross_n.wait()
-    own_rows = pl.ds(pl.multiple_of(x * (SH // 2), 16), SH // 2)
-    for s in range(NR):
-        quart[s] = (half[s, own_rows].astype(F32) + inq[s].astype(F32)).astype(BF)
-    direct = []
-    for k in range(1, NR):
-        to = (rw + k) % NR
-        direct.append(remote(quart.at[to], got.at[k - 1], d_s.at[0, k - 1], d_r.at[0, k - 1], to, f))
-        direct[-1].start()
-    cross_b.wait()
-    bquart[...] = (bhalf[:, cols(x, BQ)].astype(F32) + inbq[...].astype(F32)).astype(BF)
-    directb = []
-    for k in range(1, NR):
-        to = (rw + k) % NR
-        rows = pl.ds(pl.multiple_of(to * SB, 16), SB)
-        directb.append(remote(bquart.at[rows], bgot.at[k - 1], d_s.at[1, k - 1], d_r.at[1, k - 1], to, f))
-        directb[-1].start()
-    for cp in small_b:
-        cp.wait()
-    s_all[pl.ds(pl.multiple_of(8 * f, 8), 8)] = (
-        s_own[...] + s_rows[0] + s_rows[1] + s_rows[2] + s_rows[3] + s_rows[4] + s_rows[5] + s_rows[6]
-    )
-    mine = s_all.at[pl.ds(pl.multiple_of(8 * f, 8), 8)]
-    small_c = [remote(mine, mine, sc_s.at[i], sc_r.at[i], rw, p) for i, p in enumerate(peers)]
-    for cp in small_c:
-        cp.start()
-    for cp in direct:
-        cp.wait()
-    total = quart[rw].astype(F32)
-    for k in range(NR - 1):
-        total = total + got[k].astype(F32)
-    blk = full.at[own_rows, cols(c, 128)]
-    full[own_rows, cols(c, 128)] = total.astype(BF)
-    fin = [remote(blk, blk, f_s.at[0, i], f_r.at[0, i], rw, p) for i, p in enumerate(peers)]
-    for cp in fin:
-        cp.start()
-    for cp in directb:
-        cp.wait()
-    totalb = bquart[pl.ds(pl.multiple_of(rw * SB, 16), SB), :].astype(F32)
-    for k in range(NR - 1):
-        totalb = totalb + bgot[k].astype(F32)
-    bcols = pl.ds(pl.multiple_of(c * BH + x * BQ, 128), BQ)
-    bfull[:, bcols] = totalb.astype(BF)
-    finb = [remote(bfull.at[:, bcols], bfull.at[:, bcols], f_s.at[1, i], f_r.at[1, i], rw, p) for i, p in enumerate(peers)]
-    for cp in finb:
-        cp.start()
-
-    for cp in small_c:
-        cp.wait()
-    tot = s_all[...]
+    for lo in range(0, SH // 32):
+        rows = slice(32 * lo, 32 * lo + 32)
+        g = gfull[lo].reshape(32, C).astype(F32)
+        m, sq, up = adam_update(g, nm[rows], nf[rows], ns[rows], RATE_SLABS)
+        nmo[rows], nso[rows], nuo[rows], nco[rows] = m, sq, up, up.astype(BF)
+    for q in range(KR // C):
+        cols = slice(q * C, q * C + C)
+        g = bfull[:, :, cols].reshape(SB, C).astype(F32)
+        m, sq, up = adam_update(g, bm[:, cols], bf_[:, cols], bs[:, cols], RATE_SLABS)
+        bmo[:, cols], bso[:, cols], buo[:, cols], bco[:, cols] = m, sq, up, up.astype(BF)
+    tot = small[...]
     gains_g = pltpu.roll(tot[0:16], (NR - rw) * (C // NR), 1)[:12, : C // NR]
     q = rw * (FF // NR) // C
     off = rw * (FF // NR) % C
@@ -1111,73 +1277,50 @@
     hidden_g = pltpu.roll(hid, C - off, 1)[:3, : FF // NR]
     gmo[...], gso[...], guo[...] = adam_update(gains_g, gm[...], gf[...], gs[...], RATE_GAINS)
     hmo[...], hso[...], huo[...] = adam_update(hidden_g, hm[...], hf[...], hs[...], RATE_GAINS)
-    for cp in fin:
-        cp.wait()
-    for lo in range(0, SH, 136):
-        rows = slice(lo, lo + 136)
-        m, sq, up = adam_update(full[...][rows].astype(F32), nm[rows], nf[rows], ns[rows], RATE_SLABS)
-        nmo[rows], nso[rows], nuo[rows] = m, sq, up
-    nco[...] = nuo[...].astype(BF)
-    for cp in finb:
-        cp.wait()
-    m, sq, up = adam_update(bfull[...].astype(F32), bm[...], bf_[...], bs[...], RATE_SLABS)
-    bmo[...], bso[...], buo[...] = m, sq, up
-    bco[...] = up.astype(BF)
-
-
-def run_reduce(NR, ngrad, bgrad, small, *state):
-    vm = lambda shape, dt=BF: pltpu.VMEM(shape, dt)
-    dma = lambda *shape: pltpu.SemaphoreType.DMA(shape)
-    SH, SB = KC // NR, C // NR
+
+
+def run_adam(NR, gfull, bfull, small, fout, igrad, *state):
     shape = lambda a, dt=F32: jax.ShapeDtypeStruct(a.shape, dt)
     nm, bm, gm, hm = state[0], state[3], state[6], state[9]
-    out_shape = tuple(shape(a) for a in (nm, bm, gm, hm) for _ in range(3)) + (shape(nm, BF), shape(bm, BF))
+    out_shape = (shape(fout, BF), shape(igrad)) + tuple(shape(a) for a in (nm, bm, gm, hm) for _ in range(3))
+    out_shape += (shape(nm, BF), shape(bm, BF))
     spec = pl.BlockSpec(memory_space=pltpu.VMEM)
-    scratch = [
-        vm((NR, SH, 128)), vm((C, KR // 2)), vm((KC, 128)), vm((C, KR // 2)),
-        vm((NR, SH // 2, 128)), vm((C, KR // 4)), vm((NR, SH // 2, 128)), vm((C, KR // 4)),
-        vm((16, 128)), vm((16, 128)), vm((NR - 1, SH // 2, 128)), vm((NR - 1, SB, KR // 4)),
-        vm((SH, C)), vm((SB, KR)),
-        vm((8, C), F32), vm((3, 8, C), F32), vm((NR - 1, 8, C), F32), vm((32, C), F32),
-        dma(2), dma(2), dma(2), dma(2), dma(2, NR - 1), dma(2, NR - 1), dma(2, 3), dma(2, 3),
-        dma(3), dma(3), dma(NR - 1), dma(NR - 1), dma(3), dma(3),
-    ]
     return pl.pallas_call(
-        functools.partial(reduce_kernel, NR),
+        functools.partial(adam_kernel, NR),
         out_shape=out_shape,
-        in_specs=[spec] * 15,
-        out_specs=tuple([spec] * 14),
-        scratch_shapes=scratch,
-        compiler_params=pltpu.CompilerParams(collective_id=1, has_side_effects=True, vmem_limit_bytes=48 * 2**20),
-    )(ngrad, bgrad, small, *state)
+        in_specs=[spec] * 17,
+        out_specs=tuple([spec] * 16),
+        compiler_params=pltpu.CompilerParams(vmem_limit_bytes=60 * 2**20),
+    )(gfull, bfull, small, *state, fout, igrad)
 
 
 def local(
     features, segment_ids, timesteps, cotangent, narrow_slab, broad_slab, model_gains, hidden_gains,
     narrow_first, narrow_second, broad_first, broad_second, gains_first, gains_second, hidden_first, hidden_second,
 ):
-    steps = timesteps.astype(F32).reshape(-1, 1)
+    steps = timesteps
     groups = lax.axis_size("rows")
     if groups == 8:
-        fout, igrad, ngrad, bgrad, small = run_main(
+        fout, igrad, small, gfull, bfull = run_main(
             groups, features, segment_ids, steps, cotangent, narrow_slab, broad_slab, model_gains, hidden_gains
         )
-        new = run_reduce(
-            groups, ngrad, bgrad, small,
-            narrow_slab, narrow_first, narrow_second, broad_slab, broad_first, broad_second,
-            model_gains, gains_first, gains_second, hidden_gains, hidden_first, hidden_second,
+        return tuple(
+            run_adam(
+                groups, gfull, bfull, small, fout, igrad,
+                narrow_slab, narrow_first, narrow_second, broad_slab, broad_first, broad_second,
+                model_gains, gains_first, gains_second, hidden_gains, hidden_first, hidden_second,
+            )
         )
-        return (fout, igrad, *new)
     narrow_w = lax.all_gather(narrow_slab.astype(BF), "rows", axis=0, tiled=True)
     broad_w = lax.all_gather(broad_slab.astype(BF), "rows", axis=0, tiled=True)
     gains_all = lax.all_gather(model_gains.astype(BF), "rows", axis=1, tiled=True).astype(F32)
     hidden_all = lax.all_gather(hidden_gains.astype(BF), "rows", axis=1, tiled=True).astype(F32)
-    fout, igrad, ngrad, bgrad, small = run_main(
+    fout, igrad, small, ngrad, bgrad = run_main(
         0, features, segment_ids, steps, cotangent, narrow_w, broad_w, gains_all, hidden_all
     )
     scat = lambda v: lax.psum(lax.psum_scatter(v, "rows", scatter_dimension=0, tiled=True), "frames")
-    narrow_g = scat(ngrad.astype(F32))
-    broad_g = scat(bgrad.astype(F32))
+    narrow_g = scat(ngrad.astype(F32).reshape(KC, C))
+    broad_g = scat(bgrad.astype(F32).reshape(C, KR))
     small = lax.psum(small, ("rows", "frames"))
     i = lax.axis_index("rows")
     own = lambda a, n: lax.dynamic_slice_in_dim(a, i * n, n, 1)

time: 236 us -> 190 us (0.81)
  Pallas kernels: 217 us -> 189 us
  local copies, waits for them, and re-layouts: 17.5 us -> 0 us
    pallas_call x1, Pallas kernels: 49.5 us -> 4.78 us  [run_adam(): pl.pallas_call(functools.partial(adam_kernel, NR), out_shape=out_shape, i...]
    pallas_call x1, Pallas kernels: 167 us -> 185 us  [run_main(): pl.pallas_call(functools.partial(main_kernel, NR), out_shape=out_shape, i...]
    unnamed x48 -> x0, local copies, waits for them, and re-layouts: 16.8 us -> none
where the time goes in v3:
time: 190 us
  Pallas kernels  189 us (99%)
    pallas_call x1, Pallas kernels, run_main(): pl.pallas_call(functools.partial(main_kernel, NR), out_shape=out_shape, i...  185 us
    pallas_call x1, Pallas kernels, run_adam(): pl.pallas_call(functools.partial(adam_kernel, NR), out_shape=out_shape, i...  4.78 us

profile of v3, /device:TPU:0, one launch (start us, length us, event | category | flops | bytes accessed | tf_op | source)
XLA Modules:
  0.0 190.2 jit_solution(18000476629745346964)
XLA Ops:
  0.6 184.6 %shard_map.279 = (bf16[3,256,256]{2,1,0:T(8,128)(2,1)}, f32[3,512,256]{2,1,0:T(8,128)}, f32[32,256]{1,0:T(8,128)}, bf16[17,2,16,256]{3,2,1,0:T(8,128)(2,1)}, bf16[2,16,1536]{2,1,0:T(8,128)(2,1)}) custom-call(bf16[3,512,256]{2,1,0:T(8,128)(2,1)} %feat.1, s32[3,2048]{1,0:T(4,128)} %ids.1, s32[3,8]{1,0:T(4,128)} %steps.1, bf16[3,256,256]{2,1,0:T(8,128)(2,1)} %cot.1, ...), custom_call_target="tpu_custom_call" | custom-call | flops 20000000000 | bytes 20000000 | tf_op jit(solution)/shard_map/pallas_call | solution.py:1229
  185.2 4.8 %shard_map.280 = (bf16[3,256,256]{2,1,0:T(8,128)(2,1)}, f32[3,512,256]{2,1,0:T(8,128)}, f32[544,256]{1,0:T(8,128)}, f32[544,256]{1,0:T(8,128)}, f32[544,256]{1,0...) custom-call(bf16[17,2,16,256]{3,2,1,0:T(8,128)(2,1)} %get-tuple-elem, ...), custom_call_target="tpu_custom_call" | custom-call | tf_op jit(solution)/shard_map/pallas_call | solution.py:1288

commit v4 on v3

--- a/solution.py
+++ b/solution.py
@@ -85,6 +85,14 @@
     return k, s, c
 
 
+def sine_pair(x):
+    t = x - jnp.floor(x + 0.5)
+    t2 = t * t
+    s = t * (3.141582022 + t2 * (-5.167142796 + t2 * (2.541899025 - t2 * 0.5546361918)))
+    c = 1.9999999069 + t2 * (-9.869585718 + t2 * (8.116823828 + t2 * (-2.663760321 + t2 * 0.4393935944)))
+    return s, c
+
+
 def iota(shape, dim):
     return lax.broadcasted_iota(jnp.int32, shape, dim)
 
@@ -140,20 +148,16 @@
     return jnp.sum(x, axis=0, keepdims=True)
 
 
-def piece_rows(first, count, x):
-    return pl.ds(pl.multiple_of(first + x * (count // 2), 16), count // 2)
-
-
 def main_kernel(
     NR,
     feat, ids, steps, cot, narrow_in, broad_in, gains_in, hidden_in,
     fout, igrad, small, out_n, out_b,
-    narrow_s, broad_s, gains, hidden, smallw, packf, hgrad, ggrad,
+    narrow_s, broad_s, gains, hidden, smallw, packf, hgrad, hacc, ggrad,
     ngrad_s, bgrad_s, inh, inb, inq, inbq, got, bgot, gfull, bfull, s_pack, s_in, s_own, s_rows, s_all,
     uext, gyext, metab, ohrow, keymask, idp, counts, emb, tterm, sums, squares, tabs,
-    zs, nrm1, der1, u2, nrm2, der2, resid, ll1, qs, kall, vall,
+    zs, nrm1, der1, u2, nrm2, der2, resid, ll1, qs, kvall,
     statin, statout,
-    kt, vt, sbuf, ebuf, otb, invl, dos, dost,
+    kt, vt, qt, ffbuf, sbuf, ebuf, otb, invl, dos, dost,
     gf, nl2, shaped, ginner, r3s, r3b, gm, att, dq,
     part, rbuf, rbuf2, sumbuf, dqkv, g2, tg,
     ga_s, ga_r, gx_s, gx_r, gc_s, gc_r,
@@ -173,16 +177,12 @@
     peers = (sib, cross, diag)
 
     gather = NR > 0
-    barrier = pltpu.get_barrier_semaphore()
-    for p in peers:
-        pl.semaphore_signal(barrier, inc=1, device_id=(rw, p), device_id_type=MESH)
-    for k in range(1, NR):
-        pl.semaphore_signal(barrier, inc=1, device_id=((rw + k) % NR, f), device_id_type=MESH)
-    narrow, broad = (narrow_s, broad_s) if gather else (narrow_in, broad_in)
     ngrad, bgrad = (ngrad_s, bgrad_s) if gather else (out_n, out_b)
+    broad = broad_s if gather else broad_in
     if gather:
         SH, SB = narrow_in.shape[0], broad_in.shape[0]
-        narrow[pl.ds(pl.multiple_of(rw * SH, 16), SH), :] = narrow_in[...].astype(BF)
+        NB = SH // 32
+        narrow_s[pl.ds(rw * NB, NB)] = narrow_in[...].astype(BF).reshape(NB, 2, 16, C)
         broad[pl.ds(pl.multiple_of(rw * SB, 16), SB), :] = broad_in[...].astype(BF)
         packf[...] = jnp.zeros(packf.shape, F32)
         packf[0:12, 0 : C // NR] = gains_in[...]
@@ -191,6 +191,17 @@
     else:
         gains[0:12, :] = gains_in[...]
         hidden[0:3, :] = hidden_in[...]
+
+    def wn(first, n):
+        if gather:
+            return narrow_s[first // 32 : (first + n) // 32].reshape(n, C)
+        return narrow_in[first : first + n, :]
+
+    barrier = pltpu.get_barrier_semaphore()
+    for p in peers:
+        pl.semaphore_signal(barrier, inc=1, device_id=(rw, p), device_id_type=MESH)
+    for k in range(1, NR):
+        pl.semaphore_signal(barrier, inc=1, device_id=((rw + k) % NR, f), device_id_type=MESH)
     pl.semaphore_wait(barrier, 3 + max(NR - 1, 0))
 
     def remote(src, dst, ssem, rsem, target):
@@ -200,86 +211,119 @@
         )
 
     if gather:
-        conv_first = {0: (0, SH), 1: (SH, 3 * C - SH)}
-        rest = {s: (s * SH, SH) for s in range(2, NR)}
-        rest[1] = (3 * C, 2 * SH - 3 * C)
-
-        def quarter_of(g, kind, s):
-            x, c = g // 2, g % 2
+        gx, gc = f // 2, f % 2
+        conv_blocks = 3 * C // 32
+        own_blocks = {
+            0: {0: (0, NB), 1: (NB, conv_blocks)},
+            1: {s: (max(NB * s, conv_blocks), NB * (s + 1)) for s in (1, 2, 4, 5, 6)},
+            4: {s: (NB * s, NB * (s + 1)) for s in (3, 7)},
+        }
+        ranges = {0: ((0, 24),), 1: ((24, 48), (72, 104)), 4: ((48, 72), (104, 136))}
+        kinds = (0, 1, 2, 4)
+
+        def narrow_piece(g, lo, hi):
+            return narrow_s.at[lo:hi, g // 2, :, pl.ds(pl.multiple_of(g % 2 * 128, 128), 128)]
+
+        def broad_piece(g, lo, hi):
+            width = KR // 4
+            return broad.at[lo:hi, pl.ds(pl.multiple_of(g * width, 128), width)]
+
+        def to_row(ref, ssem, rsem, row):
+            return pltpu.make_async_remote_copy(
+                src_ref=ref, dst_ref=ref, send_sem=ssem, recv_sem=rsem, device_id=(row, f), device_id_type=MESH
+            )
+
+        def sized(kind, n):
+            if kind == 2:
+                return broad.at[0 : n * SB, 0 : KR // 4]
             if kind == 3:
-                return smallw.at[s]
-            if kind == 2:
-                return broad.at[pl.ds(s * SB, SB), pl.ds(pl.multiple_of((2 * c + x) * (6 * C // 4), 128), 6 * C // 4)]
-            first, count = (conv_first if kind == 0 else rest)[s]
-            return narrow.at[piece_rows(first, count, x), pl.ds(pl.multiple_of(c * 128, 128), 128)]
-
-        def spread_copy(kind, s, k):
-            ref = quarter_of(f, kind, s)
-            return pltpu.make_async_remote_copy(
-                src_ref=ref, dst_ref=ref, send_sem=ga_s.at[kind, k], recv_sem=ga_r.at[kind, s],
-                device_id=((s + k) % NR, f), device_id_type=MESH,
-            )
-
-        def has(kind, s):
-            return {0: s in conv_first, 1: s in rest, 2: True, 3: True}[kind]
+                return smallw.at[0:n]
+            return narrow_s.at[0:n, 0, :, 0:128]
+
+        def waits(kind, n, sends, sem):
+            ref = sized(kind, n)
+            cp = remote(ref, ref, sem, sem, cross)
+            (cp.wait_send if sends else cp.wait_recv)()
+
+        def by_row(counts, act):
+            for n in sorted(set(counts)):
+                if n:
+                    rows_of = [s for s in range(NR) if counts[s] == n]
+                    cond = functools.reduce(jnp.logical_or, [rw == s for s in rows_of])
+
+                    @pl.when(cond)
+                    def _():
+                        act(n)
 
         def spread_start(kind):
-            for s in range(NR):
-                if has(kind, s):
+            if kind in own_blocks:
+                for s, (lo, hi) in own_blocks[kind].items():
 
                     @pl.when(rw == s)
                     def _():
                         for k in range(1, NR):
-                            spread_copy(kind, s, k).start()
+                            to_row(narrow_piece(f, lo, hi), ga_s.at[kind], ga_r.at[kind], (s + k) % NR).start()
+
+                return
+            for k in range(1, NR):
+                if kind == 2:
+                    at = pl.ds(pl.multiple_of(rw * SB, 16), SB)
+                    ref = broad.at[at, pl.ds(pl.multiple_of(f * (KR // 4), 128), KR // 4)]
+                else:
+                    ref = smallw.at[rw]
+                to_row(ref, ga_s.at[kind], ga_r.at[kind], (rw + k) % NR).start()
+
+        def held(kind):
+            sizes = [0] * NR
+            for s, (lo, hi) in own_blocks[kind].items():
+                sizes[s] = hi - lo
+            return sizes
+
+        def spread_arrive(kind):
+            if kind in own_blocks:
+                sizes = held(kind)
+                by_row([sum(sizes) - n for n in sizes], lambda n: waits(kind, n, False, ga_r.at[kind]))
+            else:
+                waits(kind, NR - 1, False, ga_r.at[kind])
 
         def spread_end(kind):
-            for s in range(NR):
-                if has(kind, s):
-
-                    @pl.when(rw == s)
-                    def _():
-                        for k in range(1, NR):
-                            spread_copy(kind, s, k).wait_send()
-
-        def cross_copy(kind, s):
-            ref = quarter_of(f, kind, s)
-            return remote(ref, ref, gx_s.at[kind, s], gx_r.at[kind, s], cross)
-
-        def sib_copies(kind, s):
-            a, b = quarter_of(f, kind, s), quarter_of(cross, kind, s)
-            return (
-                remote(a, a, gc_s.at[kind, 0, s], gc_r.at[kind, 0, s], sib),
-                remote(b, b, gc_s.at[kind, 1, s], gc_r.at[kind, 1, s], sib),
-            )
-
-        def pass_on(kind, order):
-            for s in order:
-
-                @pl.when(rw != s)
-                def _():
-                    spread_copy(kind, s, 1).wait_recv()
-                    cross_copy(kind, s).start()
-                    sib_copies(kind, s)[0].start()
-
-        def pass_across(kind, order):
-            for s in order:
-
-                @pl.when(rw != s)
-                def _():
-                    cross_copy(kind, s).wait_recv()
-                    sib_copies(kind, s)[1].start()
-
-        def arrive(kind, order):
-            for s in order:
-
-                @pl.when(rw != s)
-                def _():
-                    for cp in sib_copies(kind, s):
-                        cp.wait_recv()
-                        cp.wait_send()
-                    cross_copy(kind, s).wait_send()
-
-        every = tuple(range(NR))
+            if kind in own_blocks:
+                by_row([(NR - 1) * n for n in held(kind)], lambda n: waits(kind, n, True, ga_s.at[kind]))
+            else:
+                waits(kind, NR - 1, True, ga_s.at[kind])
+
+        def pieces(kind, g):
+            if kind == 2:
+                return [broad_piece(g, 0, C)]
+            return [narrow_piece(g, lo, hi) for lo, hi in ranges[kind]]
+
+        def units(kind):
+            return NR if kind == 2 else sum(hi - lo for lo, hi in ranges[kind])
+
+        def pass_on(kind):
+            spread_arrive(kind)
+            for ref in pieces(kind, f):
+                remote(ref, ref, gx_s.at[kind], gx_r.at[kind], cross).start()
+            for ref in pieces(kind, f):
+                remote(ref, ref, gc_s.at[kind, 0], gc_r.at[kind, 0], sib).start()
+
+        def pass_across(kind):
+            waits(kind, units(kind), False, gx_r.at[kind])
+            for ref in pieces(kind, cross):
+                remote(ref, ref, gc_s.at[kind, 1], gc_r.at[kind, 1], sib).start()
+
+        def arrive(kind):
+            for i in range(2):
+                waits(kind, units(kind), False, gc_r.at[kind, i])
+
+        def gather_end():
+            for kind in kinds:
+                spread_end(kind)
+                waits(kind, units(kind), True, gx_s.at[kind])
+                for i in range(2):
+                    waits(kind, units(kind), True, gc_s.at[kind, i])
+            spread_end(3)
+
         spread_start(3)
         spread_start(0)
 
@@ -371,18 +415,14 @@
     if gather:
         spread_start(1)
         spread_start(2)
-        pass_on(0, (0, 1))
-        for s in range(NR):
-
-            @pl.when(rw != s)
-            def _():
-                spread_copy(3, s, 1).wait_recv()
-
+        pass_on(0)
+        spread_start(4)
+        spread_arrive(3)
         wide = smallw[...].astype(F32)
         gains[...] = jnp.concatenate([wide[s, :, 0 : C // NR] for s in range(NR)], axis=1)
         hidden[0:3, :] = jnp.concatenate([wide[s, 12:15, :] for s in range(NR)], axis=1)
-        pass_across(0, (0, 1))
-        arrive(0, (0, 1))
+        pass_across(0)
+        arrive(0)
 
     def own_prev(r):
         return metab[r, OFF : OFF + T, 24:25].astype(F32)
@@ -392,7 +432,7 @@
 
     def stat_copies(phase):
         return [
-            remote(statout.at[phase], statin.at[phase, i], stat_s.at[phase, i], stat_r.at[phase, i], peers[i])
+            remote(statout.at[phase], statin.at[phase, i], stat_s.at[phase], stat_r.at[phase, i], peers[i])
             for i in range(3)
         ]
 
@@ -410,7 +450,8 @@
     def total_stats(phase, wait=True):
         if wait:
             for cp in stat_copies(phase):
-                cp.wait()
+                cp.wait_recv()
+            remote(statin.at[phase], statin.at[phase], stat_s.at[phase], stat_s.at[phase], sib).wait_send()
         return (statout[phase] + statin[phase, 0] + statin[phase, 1] + statin[phase, 2]) / jnp.maximum(counts[...], 1.0)
 
     group_lanes = iota((8 * R, 128), 1) < G
@@ -429,7 +470,7 @@
 
     def conv_into(r, src, first_row):
         for j in range(3):
-            zs[j] = dot(src[r], narrow[first_row + j * C : first_row + (j + 1) * C, :])
+            zs[j] = dot(src[r], wn(first_row + j * C, C))
 
     @pl.when(f > 0)
     def _():
@@ -460,15 +501,14 @@
             send_stats(0)
         if gather:
             if r == 0:
-                pass_on(1, (1, 2, 4, 5, 6))
+                pass_on(1)
             elif r == 1:
-                pass_on(2, every)
-                pass_across(1, (1, 2, 4, 5, 6))
-
-    if gather:
-        pass_on(1, (3, 7))
-        arrive(1, (1, 2, 4, 5, 6))
-    tterm[...] = dot(emb[...].astype(BF), narrow[tw : tw + TE, :]) + gains[2:3, :]
+                pass_on(2)
+                pass_across(1)
+
+    if gather:
+        arrive(1)
+    tterm[...] = dot(emb[...].astype(BF), wn(tw, TE)) + gains[2:3, :]
 
     CH = TX // 4
     tabs[:, 2 * C : 3 * C] = tterm[...]
@@ -502,21 +542,19 @@
     lax.fori_loop(0, R, phase_two, 0)
     send_stats(1)
     if gather:
-        pass_across(2, every)
-        pass_across(1, (3, 7))
-        arrive(2, every)
+        pass_across(2)
+        pass_on(4)
+        arrive(2)
     norm_tables(1)
 
-    def kv_slot(ref, r, g):
-        return ref.at[r, pl.ds(pl.multiple_of(g * T, 128), T)]
-
     def kv_copies(r):
-        out = []
-        for i, ref in enumerate((kall, vall)):
-            out.append(remote(kv_slot(ref, r, f), kv_slot(ref, r, f), kv_s.at[i, 0, r], kv_r.at[i, 0, r], sib))
-            out.append(remote(kv_slot(ref, r, f), kv_slot(ref, r, f), kv_s.at[i, 1, r], kv_r.at[i, 1, r], cross))
-            out.append(remote(kv_slot(ref, r, cross), kv_slot(ref, r, cross), kv_s.at[i, 2, r], kv_r.at[i, 2, r], sib))
-        return out
+        slot = lambda g: kvall.at[r, :, pl.ds(pl.multiple_of(g * T, 128), T)]
+        mine, other = slot(f), slot(cross)
+        return (
+            remote(mine, mine, kv_s.at[0, r], kv_r.at[0, r], sib),
+            remote(mine, mine, kv_s.at[1, r], kv_r.at[1, r], cross),
+            remote(other, other, kv_s.at[2, r], kv_r.at[2, r], sib),
+        )
 
     NCH = 4
     CT = T // NCH
@@ -541,14 +579,20 @@
             qkv = dot(low, broad[:, : 3 * INNER])
             qs[r, rows] = (qkv[:, :INNER].astype(BF).astype(F32) * HD ** (-0.5)).astype(BF)
             krows = pl.ds(pl.multiple_of(f * T + i * CT, 16), CT)
-            kall[r, krows] = qkv[:, INNER : 2 * INNER].astype(BF)
-            vall[r, krows] = qkv[:, 2 * INNER :].astype(BF)
+            kvall[r, 0, krows] = qkv[:, INNER : 2 * INNER].astype(BF)
+            kvall[r, 1, krows] = qkv[:, 2 * INNER :].astype(BF)
             return c2
 
         lax.fori_loop(0, NCH, chunk, 0)
+        if gather:
+
+            @pl.when(r == 0)
+            def _():
+                pass_across(4)
+
         cps = kv_copies(r)
-        for i in (0, 1, 3, 4):
-            cps[i].start()
+        cps[1].start()
+        cps[0].start()
         return carry
 
     lax.fori_loop(0, R, phase_three, 0)
@@ -561,9 +605,9 @@
 
     def phase_down_back(r, carry):
         gy = gyext[r, 0:HT]
-        even = dot_nt(gy, narrow[down + C : down + 2 * C, :])
-        own_gy = dot_nt(gy, narrow[down + 2 * C : down + 3 * C, :])
-        nxt = dot_nt(gyext[r], narrow[down : down + C, :])
+        even = dot_nt(gy, wn(down + C, C))
+        own_gy = dot_nt(gy, wn(down + 2 * C, C))
+        nxt = dot_nt(gyext[r], wn(down, C))
         zs[0, 0 : HT + 16] = nxt
         for hh in range(2):
             cols = slice(hh * 128, hh * 128 + 128)
@@ -587,79 +631,83 @@
         return carry
 
     if gather:
-        arrive(1, (3, 7))
-        for kind in range(4):
-            spread_end(kind)
+        arrive(4)
     lax.fori_loop(0, R, down_back, 0)
 
     def relay(r):
         cps = kv_copies(r)
-        for i in (1, 4):
-            cps[i].wait_recv()
-            cps[i + 1].start()
+        cps[1].wait_recv()
+        cps[2].start()
 
     relay(0)
+    if gather:
+        gather_end()
 
     alpha = jnp.exp(hidden[1:2, :])
     inv_beta = jnp.exp(-hidden[2:3, :])
     alpha_beta = alpha * inv_beta
+    alpha_pi = alpha * (1.0 / math.pi)
     NK = L // 256
+    CF = T // 2
+    hacc[...] = jnp.zeros(hacc.shape, F32)
     lane128 = iota((T, 128), 1)
 
     def dkv_copies(r):
-        out = []
-        for i in range(2):
-            blk = lambda g: part.at[r, i, pl.ds(pl.multiple_of(g * T, 128), T)]
-            out.append(remote(blk(sib), rbuf.at[r, i, 0], dkv_s.at[i, 0, r], dkv_r.at[i, 0, r], sib))
-            out.append(remote(blk(diag), rbuf.at[r, i, 1], dkv_s.at[i, 1, r], dkv_r.at[i, 1, r], sib))
-            out.append(remote(sumbuf.at[r, i], rbuf2.at[r, i], dkv_s.at[i, 2, r], dkv_r.at[i, 2, r], cross))
-        return out
+        return (
+            remote(part.at[r, sib], rbuf.at[r, 0], dkv_s.at[0, r], dkv_r.at[0, r], sib),
+            remote(part.at[r, diag], rbuf.at[r, 1], dkv_s.at[1, r], dkv_r.at[1, r], sib),
+            remote(sumbuf.at[r], rbuf2.at[r], dkv_s.at[2, r], dkv_r.at[2, r], cross),
+        )
 
     def phase_sum(r):
         cps = dkv_copies(r)
-        for i in (1, 4):
-            cps[i].wait_recv()
-        blk = pl.ds(pl.multiple_of(cross * T, 128), T)
-        for i in range(2):
-            sumbuf[r, i] = (part[r, i, blk].astype(F32) + rbuf[r, i, 1].astype(F32)).astype(BF)
-        for i in (2, 5):
-            cps[i].start()
+        cps[1].wait_recv()
+        sumbuf[r] = (part[r, cross].astype(F32) + rbuf[r, 1].astype(F32)).astype(BF)
+        cps[2].start()
 
     def phase_four(r, carry):
         cps = kv_copies(r)
-        for i in (0, 2, 3, 5):
-            cps[i].wait_recv()
-        for i in range(6):
-            cps[i].wait_send()
-        kt[...] = kall[r].T
-        vt[...] = vall[r].T
+        cps[0].wait_recv()
+        cps[2].wait_recv()
+        for cp in cps:
+            cp.wait_send()
+        kt[...] = kvall[r, 0].T
+        vt[...] = kvall[r, 1].T
         qv = qs[r]
         ohq = jnp.where(lane128 < 8, metab[r, OFF : OFF + T], jnp.zeros((T, 128), BF))
         zero_q = jnp.zeros((T, 128), BF)
         q_heads = [jnp.where(lane128 // HD == h, qv, zero_q) for h in range(H)]
-        for h in range(H):
-            qa = jnp.concatenate([q_heads[h], ohq], axis=1)
-
-            def score(i, m):
-                keys = pl.ds(pl.multiple_of(i * 256, 256), 256)
-                ka = jnp.concatenate([kall[r, keys], keymask[r, keys]], axis=1)
-                s = dot_nt(ka, qa)
-                sbuf[keys] = s
-                return jnp.maximum(m, jnp.max(s.reshape(32, 8, T), axis=0))
-
-            m8 = lax.fori_loop(0, NK, score, jnp.full((8, T), -3e38, F32))
-            m1 = jnp.max(m8, axis=0, keepdims=True)
-
-            def expo(i, l8):
-                keys = pl.ds(pl.multiple_of(i * 256, 256), 256)
-                e = jnp.exp(sbuf[keys] - m1)
-                ebuf[h, keys] = e.astype(BF)
-                return l8 + jnp.sum(e.reshape(32, 8, T), axis=0)
-
-            l8 = lax.fori_loop(0, NK, expo, jnp.zeros((8, T), F32))
+        TQ = T // 2
+        units = [(h, q) for h in range(H) for q in range(2)]
+
+        def scores(n):
+            h, q = units[n]
+            qrows = slice(q * TQ, q * TQ + TQ)
+            qa = jnp.concatenate([q_heads[h][qrows], ohq[qrows]], axis=1)
+            m8 = jnp.full((8, TQ), -3e38, F32)
+            for i in range(NK):
+                keys = slice(i * 256, i * 256 + 256)
+                ka = jnp.concatenate([kvall[r, 0, keys], keymask[r, keys]], axis=1)
+                sc = dot_nt(ka, qa)
+                sbuf[n % 2, keys] = sc
+                m8 = jnp.maximum(m8, jnp.max(sc.reshape(32, 8, TQ), axis=0))
+            return jnp.max(m8, axis=0, keepdims=True)
+
+        top = scores(0)
+        for n, (h, q) in enumerate(units):
+            later = scores(n + 1) if n + 1 < len(units) else None
+            qcols = slice(q * TQ, q * TQ + TQ)
+            l8 = jnp.zeros((8, TQ), F32)
+            for i in range(NK):
+                keys = slice(i * 256, i * 256 + 256)
+                e = jnp.exp(sbuf[n % 2, keys] - top)
+                ebuf[h, keys, qcols] = e.astype(BF)
+                l8 = l8 + jnp.sum(e.reshape(32, 8, TQ), axis=0)
             inv = 1.0 / jnp.sum(l8, axis=0, keepdims=True)
-            invl[h] = jnp.broadcast_to(inv, (8, T))
-            otb[h * HD : (h + 1) * HD, :] = dot(vt[h * HD : (h + 1) * HD, :], ebuf[h]) * inv
+            invl[h, :, qcols] = jnp.broadcast_to(inv, (8, TQ))
+            hrows = slice(h * HD, (h + 1) * HD)
+            otb[hrows, qcols] = dot(vt[hrows, :], ebuf[h, :, qcols]) * inv
+            top = later
         att[r] = otb[...].T.astype(BF)
 
         @pl.when(r + 1 < R)
@@ -671,32 +719,46 @@
             phase_sum(r - 1)
 
         def ff_chunk(i, c2):
-            rows = pl.ds(pl.multiple_of(i * CT, 16), CT)
+            rows = pl.ds(pl.multiple_of(i * CF, 16), CF)
             res2 = resid[r, rows] + (dot_nt(att[r, rows], broad[:, 3 * INNER : 4 * INNER]) + gains[7:8, :])
             n, rs = layer_norm_parts(res2)
             low = (n * gains[8:9, :] + gains[9:10, :]).astype(BF)
             nl2[r, rows] = low
             gfr = gf[r, rows]
-            out = jnp.zeros((CT, C), F32)
-            back = jnp.zeros((CT, C), F32)
+            def products(b):
+                w_in = broad[:, 4 * INNER + b * 256 : 4 * INNER + b * 256 + 256]
+                w_out = wn(tw + TE + b * 256, 256)
+                ffbuf[b % 2, 0] = dot(low, w_in)
+                ffbuf[b % 2, 1] = dot_nt(gfr, w_out)
+                return w_in, w_out
+
+            out, back = None, None
+            weights = products(0)
             for b in range(4):
+                following = products(b + 1) if b < 3 else None
                 cols = slice(b * 256, b * 256 + 256)
-                w_in = broad[:, 4 * INNER + b * 256 : 4 * INNER + b * 256 + 256]
-                w_out = narrow[tw + TE + b * 256 : tw + TE + b * 256 + 256, :]
-                inner = dot(low, w_in) + hidden[0:1, cols]
-                gs = dot_nt(gfr, w_out)
-                _, s, c = reduced_angle(inner * alpha[:, cols])
-                s2 = s * s
-                sc2 = (2.0 * s) * c
-                sh = (inner + s2 * inv_beta[:, cols]).astype(BF)
-                shaped[r, rows, cols] = sh
-                gi = (gs * (1.0 + sc2 * alpha_beta[:, cols])).astype(BF)
-                ginner[r, rows, cols] = gi
-                hgrad[0:1, cols] += colsum(gi.astype(F32))
-                hgrad[1:2, cols] += colsum(gs * inner * sc2)
-                hgrad[2:3, cols] += colsum(gs * s2)
-                out = out + dot(sh, w_out)
-                back = back + dot_nt(gi, w_in)
+                acc = [hacc[k, :, cols] for k in range(3)]
+                shs, gis = [], []
+                for u in range(0, CF, 32):
+                    inner = ffbuf[b % 2, 0, u : u + 32] + hidden[0:1, cols]
+                    gs = ffbuf[b % 2, 1, u : u + 32]
+                    s, c = sine_pair(inner * alpha_pi[:, cols])
+                    s2 = s * s
+                    part_g = gs * (s * c)
+                    shs.append((inner + s2 * inv_beta[:, cols]).astype(BF))
+                    gi = gs + part_g * alpha_beta[:, cols]
+                    gis.append(gi.astype(BF))
+                    for k, v in enumerate((gi, part_g * inner, gs * s2)):
+                        acc[k] = acc[k] + jnp.sum(v.reshape(4, 8, 256), axis=0)
+                for k in range(3):
+                    hacc[k, :, cols] = acc[k]
+                sh_all, gi_all = jnp.concatenate(shs, axis=0), jnp.concatenate(gis, axis=0)
+                shaped[r, rows, cols] = sh_all
+                ginner[r, rows, cols] = gi_all
+                more, more_back = dot(sh_all, weights[1]), dot_nt(gi_all, weights[0])
+                out = more if out is None else out + more
+                back = more_back if back is None else back + more_back
+                weights = following
             r3 = (res2 + (out + gains[10:11, :])).astype(BF)
             r3b[r, rows] = r3
             g_in = gfr.astype(F32)
@@ -710,7 +772,7 @@
             dos[rows] = dot(low_g, broad[:, 3 * INNER : 4 * INNER]).astype(BF).astype(F32)
             return c2
 
-        lax.fori_loop(0, NCH, ff_chunk, 0)
+        lax.fori_loop(0, T // CF, ff_chunk, 0)
 
         @pl.when(f < 3)
         def _():
@@ -720,45 +782,40 @@
         for h in range(H):
             hrows = slice(h * HD, (h + 1) * HD)
             dost[hrows, :] = dot_t[hrows] * invl[h, 0:1, :]
-        dscaled = dost[...].T.astype(BF)
         zero_t = jnp.zeros((HD, T), BF)
-        d_rows, d_cols = [], []
+        d_rows, d_cols, d_half = [], [], []
+        per_block = T // 256
         for h in range(H):
             hrows = slice(h * HD, (h + 1) * HD)
             d_rows.append(colsum(otb[hrows, :] * dost[hrows, :]))
             dh = dost[hrows, :].astype(BF)
+            d_half.append(dh)
             d_cols.append(jnp.concatenate([dh, zero_t] if h == 0 else [zero_t, dh], axis=0))
-        d_heads = [jnp.where(lane128 // HD == h, dscaled, zero_q) for h in range(H)]
-        dq[...] = jnp.zeros((INNER, T), F32)
-
-        def key_grad(i, c2):
-            keys = pl.ds(pl.multiple_of(i * 256, 256), 256)
-            dk = jnp.zeros((256, INNER), F32)
-            dv = jnp.zeros((256, INNER), F32)
+        qt[...] = qs[r].T
+        for i in range(NK):
+            keys = slice(i * 256, i * 256 + 256)
             for h in range(H):
                 hrows = slice(h * HD, (h + 1) * HD)
                 eh = ebuf[h, keys]
-                dp = dot(vall[r, keys], d_cols[h])
+                dp = dot(kvall[r, 1, keys], d_cols[h])
                 ds = (eh.astype(F32) * (dp - d_rows[h])).astype(BF)
-                dk = dk + dot(ds, q_heads[h])
-                dv = dv + dot(eh, d_heads[h])
-                dq[hrows, :] += dot(kt[hrows, keys], ds)
-            part[r, 0, keys] = dk.astype(BF)
-            part[r, 1, keys] = dv.astype(BF)
-            return c2
-
-        lax.fori_loop(0, NK, key_grad, 0)
+                part[r, i // per_block, 0, hrows, i % per_block * 256 : i % per_block * 256 + 256] = dot_nt(qt[hrows, :], ds).astype(BF)
+                part[r, i // per_block, 1, hrows, i % per_block * 256 : i % per_block * 256 + 256] = dot_nt(d_half[h], eh).astype(BF)
+                if i == 0:
+                    dq[hrows, :] = dot(kt[hrows, keys], ds)
+                else:
+                    dq[hrows, :] += dot(kt[hrows, keys], ds)
         dqkv[r, :, 0:INNER] = (dq[...].T * HD ** (-0.5)).astype(BF)
         cps = dkv_copies(r)
-        for i in (1, 4, 0, 3):
-            cps[i].start()
+        cps[1].start()
+        cps[0].start()
         return carry
 
     lax.fori_loop(0, R, phase_four, 0)
 
     if gather:
         rx, rc = f // 2, f % 2
-        shard_blocks = SH // 32
+        shard_blocks = NB
         n_groups = {1: ((48, 72), (104, 136)), 2: ((24, 48), (72, 104)), 3: ((0, 24),)}
         b_groups = {1: (4 * INNER, 2 * C), 2: (0, C)}
         b_at = {1: C, 2: 0}
@@ -805,7 +862,7 @@
                         pltpu.make_async_remote_copy(
                             src_ref=ngrad.at[a:b, rx, :, half_cols(rc, 0, 128)],
                             dst_ref=got.at[source, a - shard_blocks * s : b - shard_blocks * s],
-                            send_sem=rd_s.at[g - 1, i, s], recv_sem=rd_r.at[g - 1, i, source],
+                            send_sem=rd_s.at[g - 1, 0], recv_sem=rd_r.at[g - 1, 0],
                             device_id=(s, f), device_id_type=MESH,
                         )
                     )
@@ -815,7 +872,7 @@
                     pltpu.make_async_remote_copy(
                         src_ref=bgrad.at[s, rx, :, half_cols(rc, first, n)],
                         dst_ref=bgot.at[source, :, b_at[g] : b_at[g] + n],
-                        send_sem=rd_s.at[g - 1, 2, s], recv_sem=rd_r.at[g - 1, 2, source],
+                        send_sem=rd_s.at[g - 1, 1], recv_sem=rd_r.at[g - 1, 1],
                         device_id=(s, f), device_id_type=MESH,
                     )
                 )
@@ -858,18 +915,21 @@
                         cp.start()
 
         def red_wait(g):
-            for s in range(NR):
-
-                @pl.when(rw != s)
-                def _():
-                    for cp in owner_copies(g, s, rw):
-                        cp.wait_send()
-
-                @pl.when(rw == s)
-                def _():
-                    for k in range(1, NR):
-                        for cp in owner_copies(g, s, (s + k) % NR):
-                            cp.wait_recv()
+            overlap = [
+                sum(max(0, min(hi, NB * (s + 1)) - max(lo, NB * s)) for lo, hi in n_groups[g]) for s in range(NR)
+            ]
+
+            def take(n, sends, sem):
+                cp = remote(inq.at[0:n], inq.at[0:n], sem, sem, cross)
+                (cp.wait_send if sends else cp.wait_recv)()
+
+            by_row([sum(overlap) - n for n in overlap], lambda n: take(n, True, rd_s.at[g - 1, 0]))
+            by_row([(NR - 1) * n for n in overlap], lambda n: take(n, False, rd_r.at[g - 1, 0]))
+            if g in b_groups:
+                ref = bgot.at[0 : NR - 1, :, b_at[g] : b_at[g] + b_groups[g][1]]
+                cp = remote(ref, ref, rd_s.at[g - 1, 1], rd_r.at[g - 1, 1], cross)
+                cp.wait_send()
+                cp.wait_recv()
 
         def red_finish():
             mine = half_cols(rc, 0, 128)
@@ -888,48 +948,39 @@
                 bfull[rx, :, cols] = totals[j].astype(BF)
                 blocks.append(bfull.at[rx, :, cols])
             for j, blk in enumerate(blocks):
-                for i, p in enumerate(peers):
-                    fin.append(remote(blk, blk, rf_s.at[j, i], rf_r.at[j, i], p))
-                    fin[-1].start()
-            return fin
+                for p in peers:
+                    remote(blk, blk, rf_s.at[j], rf_r.at[j], p).start()
+                fin.append((rf_s.at[j], rf_r.at[j]))
+            sizes = [inq.at[0 : 3 * NB]] + [bgot.at[0:3, :, b_at[g] : b_at[g] + b_groups[g][1]] for g in (1, 2)]
+            return [remote(ref, ref, ss, rs, cross) for ref, (ss, rs) in zip(sizes, fin)]
 
         def small_first():
             s_pack[...] = small_rows()
-            out = [
-                remote(s_pack.at[pl.ds(pl.multiple_of(8 * p, 8), 8)], s_in.at[i], sa_s.at[i], sa_r.at[i], p)
-                for i, p in enumerate(peers)
-            ]
-            for cp in out:
-                cp.start()
-            return out
-
-        def small_second(first):
-            for cp in first:
-                cp.wait()
+            for i, p in enumerate(peers):
+                remote(s_pack.at[pl.ds(pl.multiple_of(8 * p, 8), 8)], s_in.at[i], sa_s.at[0], sa_r.at[0], p).start()
+
+        def small_second():
+            remote(s_in, s_in, sa_s.at[0], sa_r.at[0], sib).wait()
             s_own[...] = s_pack[pl.ds(pl.multiple_of(8 * f, 8), 8)] + s_in[0] + s_in[1] + s_in[2]
-            out = [
+            for k in range(1, NR):
                 pltpu.make_async_remote_copy(
-                    src_ref=s_own, dst_ref=s_rows.at[k - 1], send_sem=sb_s.at[k - 1], recv_sem=sb_r.at[k - 1],
+                    src_ref=s_own, dst_ref=s_rows.at[k - 1], send_sem=sb_s.at[0], recv_sem=sb_r.at[0],
                     device_id=((rw + k) % NR, f), device_id_type=MESH,
-                )
-                for k in range(1, NR)
-            ]
-            for cp in out:
-                cp.start()
-            return out
-
-        def small_third(second):
-            for cp in second:
-                cp.wait()
+                ).start()
+
+        def small_third():
+            ref = s_rows.at[0 : NR - 1]
+            remote(ref, ref, sb_s.at[0], sb_r.at[0], sib).wait()
             at = pl.ds(pl.multiple_of(8 * f, 8), 8)
             tot = s_own[...]
             for k in range(1, NR):
                 tot = tot + s_rows[k - 1]
             s_all[at] = tot
-            out = [remote(s_all.at[at], s_all.at[at], sc_s.at[i], sc_r.at[i], p) for i, p in enumerate(peers)]
-            for cp in out:
-                cp.start()
-            return out
+            for p in peers:
+                remote(s_all.at[at], s_all.at[at], sc_s.at[0], sc_r.at[0], p).start()
+
+        def small_last():
+            remote(s_in, s_in, sc_s.at[0], sc_r.at[0], sib).wait()
 
     def small_rows():
         hid = [hgrad[k : k + 1, q * C : (q + 1) * C] for k in range(3) for q in range(FF // C)]
@@ -972,8 +1023,7 @@
         gy = cot[r]
         out = gains[11:12, :]
         for j, blk in enumerate((before, even, odd)):
-            w = slice(down + j * C, down + (j + 1) * C)
-            out = out + dot(blk, narrow[w, :])
+            out = out + dot(blk, wn(down + j * C, C))
             zs[j, 0:C, :] += dot_tn(blk, gy)
         fout[r] = out.astype(BF)
         return carry
@@ -988,8 +1038,9 @@
         put_n(tw + TE + b * 256, dot_tn(shaped[:, :, cols].reshape(R * T, 256), gf_all))
         put_b(4 * INNER + b * 256, dot_tn(flat(nl2), ginner[:, :, cols].reshape(R * T, 256)))
     put_b(3 * INNER, dot_tn(flat(gm), flat(att)))
-    hgrad[1:2, :] = hgrad[1:2, :] * alpha_beta
-    hgrad[2:3, :] = hgrad[2:3, :] * (-inv_beta)
+    hgrad[0:1, :] = colsum(hacc[0])
+    hgrad[1:2, :] = colsum(hacc[1]) * alpha_beta
+    hgrad[2:3, :] = colsum(hacc[2]) * (-inv_beta)
     if gather:
         red_core(1)
 
@@ -1011,14 +1062,13 @@
 
     def phase_five(r, carry):
         cps = dkv_copies(r)
-        for i in (0, 3, 2, 5):
-            cps[i].wait_recv()
-        for i in range(6):
-            cps[i].wait_send()
-        blk = pl.ds(pl.multiple_of(f * T, 128), T)
+        cps[0].wait_recv()
+        cps[2].wait_recv()
+        for cp in cps:
+            cp.wait_send()
         for i in range(2):
-            tot = part[r, i, blk].astype(F32) + rbuf[r, i, 0].astype(F32) + rbuf2[r, i].astype(F32)
-            dqkv[r, :, (i + 1) * INNER : (i + 2) * INNER] = tot.astype(BF)
+            tot = part[r, f, i].astype(F32) + rbuf[r, 0, i].astype(F32) + rbuf2[r, i].astype(F32)
+            dqkv[r, :, (i + 1) * INNER : (i + 2) * INNER] = tot.T.astype(BF)
         back = dot_nt(dqkv[r], broad[:, : 3 * INNER])
         n, rs = layer_norm_parts(resid[r])
         ggrad[5:6, :] += colsum(back * n)
@@ -1086,7 +1136,7 @@
     def conv_back(r, first_row):
         out = jnp.zeros((T, C), F32)
         for j in range(3):
-            out = out + dot_nt(g3[r, :, j * C : (j + 1) * C], narrow[first_row + j * C : first_row + (j + 1) * C, :])
+            out = out + dot_nt(g3[r, :, j * C : (j + 1) * C], wn(first_row + j * C, C))
         return out
 
     def kernel_grad(src, first_row):
@@ -1129,7 +1179,7 @@
     lax.fori_loop(0, R, phase_eight, 0)
 
     if gather:
-        small_a = small_first()
+        small_first()
         red_cross(2)
     else:
         small[...] = small_rows()
@@ -1142,7 +1192,7 @@
     kernel_grad(uext, 0)
     if gather:
         red_core(3)
-        small_b = small_second(small_a)
+        small_second()
         red_owner(2)
     for r in range(R):
         igrad[r] = gr2[r] + conv_back(r, 0)
@@ -1151,12 +1201,11 @@
         if gather and r == R - 1:
             red_owner(3)
     if gather:
-        small_c = small_third(small_b)
+        small_third()
         for g in (1, 2, 3):
             red_wait(g)
         fin = red_finish()
-        for cp in small_c:
-            cp.wait()
+        small_last()
         small[...] = s_all[...]
         for cp in fin:
             cp.wait()
@@ -1182,7 +1231,7 @@
     dma = lambda *shape: pltpu.SemaphoreType.DMA(shape)
     slots = max(NR, 1)
     if NR:
-        wide = [vm((KC, C), BF), vm((C, KR), BF)]
+        wide = [vm((KC // 32, 2, 16, C), BF), vm((C, KR), BF)]
         red = [
             vm((KC // 32, 2, 16, C), BF), vm((C // 32, 2, 16, KR), BF), vm((KC // 32, 2, 16, 128), BF),
             vm((C // 32, 2, 16, KR // 2), BF), vm((KC // 32, 16, 128), BF), vm((C // 32, 16, KR // 2), BF),
@@ -1195,7 +1244,7 @@
         red = [vm((16, 128), BF)] * 10
         outs = ((KC // 32, 2, 16, C), (C // 32, 2, 16, KR))
     scratch = wide + [
-        vm((16, C)), vm((8, FF)), vm((slots, 16, 128), BF), vm((16, 128)), vm((8, FF)), vm((16, C)),
+        vm((16, C)), vm((8, FF)), vm((slots, 16, 128), BF), vm((16, 128)), vm((8, FF)), vm((3, 8, FF)), vm((16, C)),
     ] + red + [
         vm((32, C)), vm((3, 8, C)), vm((8, C)), vm((slots, 8, C)), vm((32, C)),
         vm((R, TX, C), BF), vm((R, T // 2 + 16, C), BF), vm((R, TX, 128), BF),
@@ -1203,20 +1252,20 @@
         vm((8 * R, C)), vm((8 * R, C)), vm((8 * R, 3 * C)),
         vm((3, TX, C)), vm((R, TX, C)), vm((R, TX, C), BF), vm((R, TX, C), BF), vm((R, T, C)),
         vm((R, T, C), BF), vm((R, T, C)), vm((R, T, C), BF), vm((R, T, INNER), BF),
-        vm((R, L, INNER), BF), vm((R, L, INNER), BF),
+        vm((R, 2, L, INNER), BF),
         vm((4, 3, 8 * R, 128)), vm((4, 8 * R, 128)),
-        vm((INNER, L), BF), vm((INNER, L), BF), vm((L, T)), vm((H, L, T), BF), vm((INNER, T)),
+        vm((INNER, L), BF), vm((INNER, L), BF), vm((INNER, T), BF), vm((2, 2, T // 2, C)), vm((2, L, T // 2)), vm((H, L, T), BF), vm((INNER, T)),
         vm((H, 8, T)), vm((T, INNER)), vm((INNER, T)),
         vm((R, T, C), BF), vm((R, T, C), BF),
         vm((R, T, FF), BF), vm((R, T, FF), BF), vm((4, T + 8, 128)), vm((R, T + 16, C), BF),
         vm((R, T, C), BF), vm((R, T, INNER), BF), vm((INNER, T)),
-        vm((R, 2, L, INNER), BF), vm((R, 2, 2, T, INNER), BF), vm((R, 2, T, INNER), BF), vm((R, 2, T, INNER), BF),
+        vm((R, 4, 2, INNER, T), BF), vm((R, 2, 2, INNER, T), BF), vm((R, 2, INNER, T), BF), vm((R, 2, INNER, T), BF),
         vm((R, T, 3 * INNER), BF), vm((R, TX, C), BF), vm((8 * R, C)),
-        dma(4, slots), dma(4, slots), dma(4, slots), dma(4, slots), dma(4, 2, slots), dma(4, 2, slots),
-        dma(3, 3), dma(3, 3), dma(3, 3), dma(3, 3), dma(3, 3, slots), dma(3, 3, slots), dma(3, 3), dma(3, 3),
-        dma(3), dma(3), dma(slots), dma(slots), dma(3), dma(3),
-        dma(2), dma(2), dma(1), dma(1), dma(4, 3), dma(4, 3), dma(2, 3, R), dma(2, 3, R),
-        dma(2, 3, R), dma(2, 3, R), dma(2, 2, R), dma(2, 2, R), dma(R), dma(R),
+        dma(5), dma(5), dma(5), dma(5), dma(5, 2), dma(5, 2),
+        dma(3, 3), dma(3, 3), dma(3, 3), dma(3, 3), dma(3, 2), dma(3, 2), dma(3), dma(3),
+        dma(1), dma(1), dma(1), dma(1), dma(1), dma(1),
+        dma(2), dma(2), dma(1), dma(1), dma(4), dma(4, 3), dma(3, R), dma(3, R),
+        dma(3, R), dma(3, R), dma(2, 2, R), dma(2, 2, R), dma(R), dma(R),
     ]
     out_shape = (
         jax.ShapeDtypeStruct((R, T // 2, C), BF),

time: 190 us -> 165 us (0.87)
  Pallas kernels: 189 us -> 164 us
    pallas_call x1, Pallas kernels: 185 us -> 160 us  [run_main(): pl.pallas_call(functools.partial(main_kernel, NR), out_shape=out_shape, i...]
where the time goes in v4:
time: 165 us
  Pallas kernels  164 us (99%)
    pallas_call x1, Pallas kernels, run_main(): pl.pallas_call(functools.partial(main_kernel, NR), out_shape=out_shape, i...  160 us
    pallas_call x1, Pallas kernels, run_adam(): pl.pallas_call(functools.partial(adam_kernel, NR), out_shape=out_shape, i...  4.78 us

profile of v4, /device:TPU:0, one launch (start us, length us, event | category | flops | bytes accessed | tf_op | source)
XLA Modules:
  0.0 165.2 jit_solution(8027620855426207558)
XLA Ops:
  0.6 159.6 %shard_map.279 = (bf16[3,256,256]{2,1,0:T(8,128)(2,1)}, f32[3,512,256]{2,1,0:T(8,128)}, f32[32,256]{1,0:T(8,128)}, bf16[17,2,16,256]{3,2,1,0:T(8,128)(2,1)}, bf16[2,16,1536]{2,1,0:T(8,128)(2,1)}) custom-call(bf16[3,512,256]{2,1,0:T(8,128)(2,1)} %feat.1, s32[3,2048]{1,0:T(4,128)} %ids.1, s32[3,8]{1,0:T(4,128)} %steps.1, bf16[3,256,256]{2,1,0:T(8,128)(2,1)} %cot.1, ...), custom_call_target="tpu_custom_call" | custom-call | flops 20000000000 | bytes 20000000 | tf_op jit(solution)/shard_map/pallas_call | solution.py:1278
  160.2 4.8 %shard_map.280 = (bf16[3,256,256]{2,1,0:T(8,128)(2,1)}, f32[3,512,256]{2,1,0:T(8,128)}, f32[544,256]{1,0:T(8,128)}, f32[544,256]{1,0:T(8,128)}, f32[544,256]{1,0...) custom-call(bf16[17,2,16,256]{3,2,1,0:T(8,128)(2,1)} %get-tuple-elem, ...), custom_call_target="tpu_custom_call" | custom-call | tf_op jit(solution)/shard_map/pallas_call | solution.py:1337

commit v5 on v4

--- a/solution.py
+++ b/solution.py
@@ -70,7 +70,7 @@
     n = e * (e + 2.0)
     rc = recip(n + 2.0)
     t = n * rc
-    d = t + y * (2.0 * rc) * (1.0 + t) * (e * recip(1.0 + e))
+    d = t + y * (2.0 * rc) * (1.0 + t) * (e * pltpu.reciprocal(1.0 + e, approx=True))
     return t, d
 
 
@@ -159,10 +159,10 @@
     statin, statout,
     kt, vt, qt, ffbuf, sbuf, ebuf, otb, invl, dos, dost,
     gf, nl2, shaped, ginner, r3s, r3b, gm, att, dq,
-    part, rbuf, rbuf2, sumbuf, dqkv, g2, tg,
+    part, rbuf, rbuf2, sumbuf, dqkv, g2, tg, edge,
     ga_s, ga_r, gx_s, gx_r, gc_s, gc_r,
     rc_s, rc_r, rx_s, rx_r, rd_s, rd_r, rf_s, rf_r, sa_s, sa_r, sb_s, sb_r, sc_s, sc_r,
-    halo_s, halo_r, cot_s, cot_r, stat_s, stat_r, kv_s, kv_r, dkv_s, dkv_r, gh_s, gh_r, r3_s, r3_r,
+    halo_s, halo_r, cot_s, cot_r, stat_s, stat_r, kv_s, kv_r, dkv_s, dkv_r, eg_s, eg_r, r3_s, r3_r,
 ):
     R, T = feat.shape[0], feat.shape[1]
     gr2, dn, g3 = igrad, resid, shaped
@@ -353,10 +353,12 @@
 
     @pl.when(f == 0)
     def _():
+        edge[:, 0] = jnp.zeros((3, R, 8, C), F32)
         uext[:, OFF - 16 : OFF, :] = jnp.zeros((R, 16, C), BF)
 
     @pl.when(f == 3)
     def _():
+        edge[:, 1] = jnp.zeros((3, R, 8, C), F32)
         uext[:, OFF + T : OFF + T + 16, :] = jnp.zeros((R, 16, C), BF)
         gyext[:, HT : HT + 16, :] = jnp.zeros((R, 16, C), BF)
 
@@ -430,6 +432,36 @@
     def own_next(r):
         return metab[r, OFF : OFF + T, 25:26].astype(F32)
 
+    def edge_copies(which, src):
+        return (
+            to_next(src.at[:, pl.ds(T - 8, 8)], edge.at[which, 0], eg_s.at[which, 0], eg_r.at[which, 0]),
+            to_prev(src.at[:, pl.ds(0, 8)], edge.at[which, 1], eg_s.at[which, 1], eg_r.at[which, 1]),
+        )
+
+    def send_edges(which, src):
+        down_cp, up_cp = edge_copies(which, src)
+
+        @pl.when(f < 3)
+        def _():
+            down_cp.start()
+
+        @pl.when(f > 0)
+        def _():
+            up_cp.start()
+
+    def await_edges(which, src):
+        down_cp, up_cp = edge_copies(which, src)
+
+        @pl.when(f < 3)
+        def _():
+            down_cp.wait_send()
+            up_cp.wait_recv()
+
+        @pl.when(f > 0)
+        def _():
+            up_cp.wait_send()
+            down_cp.wait_recv()
+
     def stat_copies(phase):
         return [
             remote(statout.at[phase], statin.at[phase, i], stat_s.at[phase], stat_r.at[phase, i], peers[i])
@@ -596,6 +628,7 @@
         return carry
 
     lax.fori_loop(0, R, phase_three, 0)
+    send_edges(2, nrm2)
 
     @pl.when(f < 3)
     def _():
@@ -713,10 +746,6 @@
         @pl.when(r + 1 < R)
         def _():
             relay(r + 1)
-
-        @pl.when(r > 0)
-        def _():
-            phase_sum(r - 1)
 
         def ff_chunk(i, c2):
             rows = pl.ds(pl.multiple_of(i * CF, 16), CF)
@@ -792,23 +821,29 @@
             d_half.append(dh)
             d_cols.append(jnp.concatenate([dh, zero_t] if h == 0 else [zero_t, dh], axis=0))
         qt[...] = qs[r].T
-        for i in range(NK):
-            keys = slice(i * 256, i * 256 + 256)
-            for h in range(H):
-                hrows = slice(h * HD, (h + 1) * HD)
-                eh = ebuf[h, keys]
-                dp = dot(kvall[r, 1, keys], d_cols[h])
-                ds = (eh.astype(F32) * (dp - d_rows[h])).astype(BF)
-                part[r, i // per_block, 0, hrows, i % per_block * 256 : i % per_block * 256 + 256] = dot_nt(qt[hrows, :], ds).astype(BF)
-                part[r, i // per_block, 1, hrows, i % per_block * 256 : i % per_block * 256 + 256] = dot_nt(d_half[h], eh).astype(BF)
-                if i == 0:
-                    dq[hrows, :] = dot(kt[hrows, keys], ds)
-                else:
-                    dq[hrows, :] += dot(kt[hrows, keys], ds)
+        cps = dkv_copies(r)
+        for n, block in enumerate((diag, sib, cross, f)):
+            for i in range(per_block):
+                keys = pl.ds(pl.multiple_of(block * T + i * 256, 256), 256)
+                within = slice(i * 256, i * 256 + 256)
+                for h in range(H):
+                    hrows = slice(h * HD, (h + 1) * HD)
+                    eh = ebuf[h, keys]
+                    dp = dot(kvall[r, 1, keys], d_cols[h])
+                    ds = (eh.astype(F32) * (dp - d_rows[h])).astype(BF)
+                    part[r, block, 0, hrows, within] = dot_nt(qt[hrows, :], ds).astype(BF)
+                    part[r, block, 1, hrows, within] = dot_nt(d_half[h], eh).astype(BF)
+                    if n == 0 and i == 0:
+                        dq[hrows, :] = dot(kt[hrows, keys], ds)
+                    else:
+                        dq[hrows, :] += dot(kt[hrows, keys], ds)
+            if n == 0:
+                cps[1].start()
+            elif n == 1:
+                cps[0].start()
+            elif n == 2:
+                phase_sum(r)
         dqkv[r, :, 0:INNER] = (dq[...].T * HD ** (-0.5)).astype(BF)
-        cps = dkv_copies(r)
-        cps[1].start()
-        cps[0].start()
         return carry
 
     lax.fori_loop(0, R, phase_four, 0)
@@ -1044,8 +1079,6 @@
     if gather:
         red_core(1)
 
-    phase_sum(R - 1)
-
     def mean_tables(phase, norm_phase):
         tot = total_stats(phase)
         iv = norm_scale(total_stats(norm_phase, wait=False))
@@ -1080,52 +1113,29 @@
 
     lax.fori_loop(0, R, phase_five, 0)
     send_stats(2)
+    send_edges(1, dn)
     if gather:
         red_cross(1)
     put_b(0, dot_tn(flat(ll1), flat(dqkv)))
     mean_tables(2, 1)
-
-    def gh_copies(phase, r):
-        return (
-            to_next(g2.at[r, pl.ds(OFF + T - 16, 16)], g2.at[r, pl.ds(OFF - 16, 16)], gh_s.at[phase, 0, r], gh_r.at[phase, 0, r]),
-            to_prev(g2.at[r, pl.ds(OFF, 16)], g2.at[r, pl.ds(OFF + T, 16)], gh_s.at[phase, 1, r], gh_r.at[phase, 1, r]),
-        )
-
-    def norm_back_end(r, n, which):
-        sp = dot(metab[r, OFF : OFF + T], row_table(r, 3 * C))
-        g = dn[r] * sp[:, 2 * C :] - sp[:, :C] - n * sp[:, C : 2 * C]
-        g2[r, OFF : OFF + T] = g.astype(BF)
-        down_cp, up_cp = gh_copies(which, r)
-
-        @pl.when(f < 3)
-        def _():
-            down_cp.start()
-
-        @pl.when(f > 0)
-        def _():
-            up_cp.start()
-
-    def build_g3(which, r):
-        down_cp, up_cp = gh_copies(which, r)
-
-        @pl.when(f < 3)
-        def _():
-            down_cp.wait_send()
-            up_cp.wait_recv()
-
-        @pl.when(f > 0)
-        def _():
-            up_cp.wait_send()
-            down_cp.wait_recv()
-
-        @pl.when(f == 0)
-        def _():
-            g2[r, OFF - 16 : OFF, :] = jnp.zeros((16, C), BF)
-
-        @pl.when(f == 3)
-        def _():
-            g2[r, OFF + T : OFF + T + 16, :] = jnp.zeros((16, C), BF)
-
+    await_edges(2, nrm2)
+    await_edges(1, dn)
+
+    def norm_back_end(r, n, which, n_above, n_below):
+        tab = row_table(r, 3 * C)
+
+        def back(rows, d, norm):
+            sp = dot(metab[r, rows], tab)[-d.shape[0] :] if rows.stop == OFF else dot(metab[r, rows], tab)[: d.shape[0]]
+            return d * sp[:, 2 * C :] - sp[:, :C] - norm * sp[:, C : 2 * C]
+
+        zero = jnp.zeros((8, C), F32)
+        above = back(slice(OFF - 16, OFF), edge[which, 0, r], n_above)
+        below = back(slice(OFF + T, OFF + T + 16), edge[which, 1, r], n_below)
+        g2[r, OFF - 16 : OFF] = jnp.concatenate([zero, above], axis=0).astype(BF)
+        g2[r, OFF + T : OFF + T + 16] = jnp.concatenate([below, zero], axis=0).astype(BF)
+        g2[r, OFF : OFF + T] = back(slice(OFF, OFF + T), dn[r], n).astype(BF)
+
+    def build_g3(r):
         g = g2[r].astype(F32)
         zs[0] = g * metab[r, :, 24:25].astype(F32)
         zs[2] = g * metab[r, :, 25:26].astype(F32)
@@ -1144,14 +1154,9 @@
         for j in range(3):
             put_n(first_row + j * C, dot_tn(u, g3[:, :, j * C : (j + 1) * C].reshape(R * T, C)))
 
-    def phase_six(r, carry):
-        norm_back_end(r, nrm2[r], 1)
-        return carry
-
-    lax.fori_loop(0, R, phase_six, 0)
-
     def phase_seven(r, carry):
-        build_g3(1, r)
+        norm_back_end(r, nrm2[r], 1, edge[2, 0, r], edge[2, 1, r])
+        build_g3(r)
         gh = conv_back(r, 3 * C)
         oh = ohrow[r].astype(BF)
         tgr = segment_sums(oh, gh)
@@ -1162,6 +1167,7 @@
 
     lax.fori_loop(0, R, phase_seven, 0)
     send_stats(3)
+    send_edges(0, dn)
     if gather:
         red_owner(1)
     kernel_grad(u2, 3 * C)
@@ -1171,12 +1177,7 @@
     if gather:
         red_core(2)
     mean_tables(3, 0)
-
-    def phase_eight(r, carry):
-        norm_back_end(r, nrm1[r, OFF : OFF + T], 0)
-        return carry
-
-    lax.fori_loop(0, R, phase_eight, 0)
+    await_edges(0, dn)
 
     if gather:
         small_first()
@@ -1185,7 +1186,10 @@
         small[...] = small_rows()
 
     def phase_g3(r, carry):
-        build_g3(0, r)
+        norm_back_end(
+            r, nrm1[r, OFF : OFF + T], 0, nrm1[r, OFF - 8 : OFF], nrm1[r, OFF + T : OFF + T + 8]
+        )
+        build_g3(r)
         return carry
 
     lax.fori_loop(0, R, phase_g3, 0)
@@ -1260,12 +1264,12 @@
         vm((R, T, FF), BF), vm((R, T, FF), BF), vm((4, T + 8, 128)), vm((R, T + 16, C), BF),
         vm((R, T, C), BF), vm((R, T, INNER), BF), vm((INNER, T)),
         vm((R, 4, 2, INNER, T), BF), vm((R, 2, 2, INNER, T), BF), vm((R, 2, INNER, T), BF), vm((R, 2, INNER, T), BF),
-        vm((R, T, 3 * INNER), BF), vm((R, TX, C), BF), vm((8 * R, C)),
+        vm((R, T, 3 * INNER), BF), vm((R, TX, C), BF), vm((8 * R, C)), vm((3, 2, R, 8, C)),
         dma(5), dma(5), dma(5), dma(5), dma(5, 2), dma(5, 2),
         dma(3, 3), dma(3, 3), dma(3, 3), dma(3, 3), dma(3, 2), dma(3, 2), dma(3), dma(3),
         dma(1), dma(1), dma(1), dma(1), dma(1), dma(1),
         dma(2), dma(2), dma(1), dma(1), dma(4), dma(4, 3), dma(3, R), dma(3, R),
-        dma(3, R), dma(3, R), dma(2, 2, R), dma(2, 2, R), dma(R), dma(R),
+        dma(3, R), dma(3, R), dma(3, 2), dma(3, 2), dma(R), dma(R),
     ]
     out_shape = (
         jax.ShapeDtypeStruct((R, T // 2, C), BF),

time: 165 us -> 158 us (0.958)
  Pallas kernels: 164 us -> 157 us
    pallas_call x1, Pallas kernels: 160 us -> 152 us  [run_main(): pl.pallas_call(functools.partial(main_kernel, NR), out_shape=out_shape, i...]
where the time goes in v5:
time: 158 us
  Pallas kernels  157 us (99%)
    pallas_call x1, Pallas kernels, run_main(): pl.pallas_call(functools.partial(main_kernel, NR), out_shape=out_shape, i...  152 us
    pallas_call x1, Pallas kernels, run_adam(): pl.pallas_call(functools.partial(adam_kernel, NR), out_shape=out_shape, i...  4.78 us

profile of v5, /device:TPU:0, one launch (start us, length us, event | category | flops | bytes accessed | tf_op | source)
XLA Modules:
  0.0 157.9 jit_solution(10466845906258669190)
XLA Ops:
  0.6 152.3 %shard_map.279 = (bf16[3,256,256]{2,1,0:T(8,128)(2,1)}, f32[3,512,256]{2,1,0:T(8,128)}, f32[32,256]{1,0:T(8,128)}, bf16[17,2,16,256]{3,2,1,0:T(8,128)(2,1)}, bf16[2,16,1536]{2,1,0:T(8,128)(2,1)}) custom-call(bf16[3,512,256]{2,1,0:T(8,128)(2,1)} %feat.1, s32[3,2048]{1,0:T(4,128)} %ids.1, s32[3,8]{1,0:T(4,128)} %steps.1, bf16[3,256,256]{2,1,0:T(8,128)(2,1)} %cot.1, ...), custom_call_target="tpu_custom_call" | custom-call | flops 20000000000 | bytes 20000000 | tf_op jit(solution)/shard_map/pallas_call | solution.py:1282
  152.9 4.8 %shard_map.280 = (bf16[3,256,256]{2,1,0:T(8,128)(2,1)}, f32[3,512,256]{2,1,0:T(8,128)}, f32[544,256]{1,0:T(8,128)}, f32[544,256]{1,0:T(8,128)}, f32[544,256]{1,0...) custom-call(bf16[17,2,16,256]{3,2,1,0:T(8,128)(2,1)} %get-tuple-elem, ...), custom_call_target="tpu_custom_call" | custom-call | tf_op jit(solution)/shard_map/pallas_call | solution.py:1341

commit v6 on v5

--- a/solution.py
+++ b/solution.py
@@ -153,7 +153,7 @@
     feat, ids, steps, cot, narrow_in, broad_in, gains_in, hidden_in,
     fout, igrad, small, out_n, out_b,
     narrow_s, broad_s, gains, hidden, smallw, packf, hgrad, hacc, ggrad,
-    ngrad_s, bgrad_s, inh, inb, inq, inbq, got, bgot, gfull, bfull, s_pack, s_in, s_own, s_rows, s_all,
+    ngrad_s, bgrad_s, inh, inb, inq, inbq, got, bgot, gfull, bfull, s_pack, s_in, s_own, s_rows, s_all, embp, ttout, ttin, tgbuf, tgall,
     uext, gyext, metab, ohrow, keymask, idp, counts, emb, tterm, sums, squares, tabs,
     zs, nrm1, der1, u2, nrm2, der2, resid, ll1, qs, kvall,
     statin, statout,
@@ -161,7 +161,7 @@
     gf, nl2, shaped, ginner, r3s, r3b, gm, att, dq,
     part, rbuf, rbuf2, sumbuf, dqkv, g2, tg, edge,
     ga_s, ga_r, gx_s, gx_r, gc_s, gc_r,
-    rc_s, rc_r, rx_s, rx_r, rd_s, rd_r, rf_s, rf_r, sa_s, sa_r, sb_s, sb_r, sc_s, sc_r,
+    rc_s, rc_r, rx_s, rx_r, rd_s, rd_r, rf_s, rf_r, sa_s, sa_r, sb_s, sb_r, sc_s, sc_r, tt_s, tt_r, tf_s, tf_r, to_s, to_r,
     halo_s, halo_r, cot_s, cot_r, stat_s, stat_r, kv_s, kv_r, dkv_s, dkv_r, eg_s, eg_r, r3_s, r3_r,
 ):
     R, T = feat.shape[0], feat.shape[1]
@@ -187,6 +187,11 @@
         packf[...] = jnp.zeros(packf.shape, F32)
         packf[0:12, 0 : C // NR] = gains_in[...]
         packf[12:15, :] = hidden_in[...]
+        step_f = steps[...].astype(F32)
+        step_hi = jnp.floor(step_f * (1.0 / 32.0))
+        for r in range(R):
+            packf[15:16, NSEG * r : NSEG * r + NSEG] = step_hi[r : r + 1]
+            packf[15:16, 64 + NSEG * r : 64 + NSEG * r + NSEG] = step_f[r : r + 1] - 32.0 * step_hi[r : r + 1]
         smallw[rw] = packf[...].astype(BF)
     else:
         gains[0:12, :] = gains_in[...]
@@ -215,10 +220,13 @@
         conv_blocks = 3 * C // 32
         own_blocks = {
             0: {0: (0, NB), 1: (NB, conv_blocks)},
-            1: {s: (max(NB * s, conv_blocks), NB * (s + 1)) for s in (1, 2, 4, 5, 6)},
-            4: {s: (NB * s, NB * (s + 1)) for s in (3, 7)},
+            1: {1: (24, 34), 2: (34, 48)},
+            4: {2: (48, 51), 3: (51, 68), 4: (68, 72), 6: (104, 119), 7: (119, 136)},
         }
-        ranges = {0: ((0, 24),), 1: ((24, 48), (72, 104)), 4: ((48, 72), (104, 136))}
+        ranges = {0: ((0, 24),), 1: ((24, 48),), 4: ((48, 72), (104, 136))}
+        t_lo, t_hi = 9 * C // 32, (9 * C + TE) // 32
+        owners = [s for s in range(NR) if max(NB * s, t_lo) < min(NB * (s + 1), t_hi)]
+        is_owner = functools.reduce(jnp.logical_or, [rw == o for o in owners])
         kinds = (0, 1, 2, 4)
 
         def narrow_piece(g, lo, hi):
@@ -323,6 +331,11 @@
                 for i in range(2):
                     waits(kind, units(kind), True, gc_s.at[kind, i])
             spread_end(3)
+
+            @pl.when(is_owner)
+            def _():
+                ref = ttout.at[0 : (NR - 1) * 8 * R]
+                remote(ref, ref, tt_s.at[0], tt_s.at[0], cross).wait_send()
 
         spread_start(3)
         spread_start(0)
@@ -404,14 +417,15 @@
     gyext[:, 0:HT, :] = cot[...]
 
     half = TE // 2
-    freq = jnp.exp(iota((8, half), 1).astype(F32) * (-math.log(10000.0) / half))
-    for r in range(R):
-        turn = jnp.broadcast_to(steps[r : r + 1, :].astype(F32), (8, NSEG))
-        ang = jnp.sum(jnp.where(iota((8, NSEG), 0) == iota((8, NSEG), 1), turn, 0.0), axis=1, keepdims=True) * freq
-        k, s, c = reduced_angle(ang)
-        sign = 1.0 - 2.0 * (k - 2.0 * jnp.floor(k * 0.5))
-        both = jnp.concatenate([s * sign, c * sign], axis=1)
-        emb[8 * r : 8 * r + 8, :] = both * mish_parts(both)[0]
+    if not gather:
+        freq = jnp.exp(iota((8, half), 1).astype(F32) * (-math.log(10000.0) / half))
+        for r in range(R):
+            turn = jnp.broadcast_to(steps[r : r + 1, :].astype(F32), (8, NSEG))
+            ang = jnp.sum(jnp.where(iota((8, NSEG), 0) == iota((8, NSEG), 1), turn, 0.0), axis=1, keepdims=True) * freq
+            k, s, c = reduced_angle(ang)
+            sign = 1.0 - 2.0 * (k - 2.0 * jnp.floor(k * 0.5))
+            both = jnp.concatenate([s * sign, c * sign], axis=1)
+            emb[8 * r : 8 * r + 8, :] = both * mish_parts(both)[0]
     tw = 9 * C
 
     if gather:
@@ -423,6 +437,30 @@
         wide = smallw[...].astype(F32)
         gains[...] = jnp.concatenate([wide[s, :, 0 : C // NR] for s in range(NR)], axis=1)
         hidden[0:3, :] = jnp.concatenate([wide[s, 12:15, :] for s in range(NR)], axis=1)
+        @pl.when(is_owner)
+        def _():
+            same = iota((8 * R, 8 * R), 0) == iota((8 * R, 8 * R), 1)
+            column = []
+            for g in range(NR):
+                row = wide[g, 15:16, 0 : 8 * R] * 32.0 + wide[g, 15:16, 64 : 64 + 8 * R]
+                spread = jnp.broadcast_to(row, (8 * R, 8 * R))
+                column.append(jnp.sum(jnp.where(same, spread, 0.0), axis=1, keepdims=True))
+            at = iota((1, SH), 1) + (NB * rw - t_lo) * 32
+            low = at < half
+            freq = jnp.exp(jnp.where(low, at, at - half).astype(F32) * (-math.log(10000.0) / half))
+            k, si, co = reduced_angle(jnp.concatenate(column, axis=0) * freq)
+            v = jnp.where(low, si, co) * (1.0 - 2.0 * (k - 2.0 * jnp.floor(k * 0.5)))
+            v = jnp.where((at >= 0) & (at < TE), v * mish_parts(v)[0], 0.0)
+            embp[...] = v.astype(BF)
+            ttout[...] = dot(embp[...], narrow_s[pl.ds(rw * NB, NB)].reshape(SH, C))
+            for k2 in range(1, NR):
+                to = (rw + k2) % NR
+                pltpu.make_async_remote_copy(
+                    src_ref=ttout.at[pl.ds(pl.multiple_of(to * 8 * R, 8), 8 * R)], dst_ref=ttin.at[rw],
+                    send_sem=tt_s.at[0], recv_sem=tt_r.at[0], device_id=(to, f), device_id_type=MESH,
+                ).start()
+            ttin[rw] = ttout[pl.ds(pl.multiple_of(rw * 8 * R, 8), 8 * R)]
+
         pass_across(0)
         arrive(0)
 
@@ -540,7 +578,18 @@
 
     if gather:
         arrive(1)
-    tterm[...] = dot(emb[...].astype(BF), wn(tw, TE)) + gains[2:3, :]
+    if gather:
+
+        def take_terms(n):
+            remote(ttin.at[0:n], ttin.at[0:n], tt_r.at[0], tt_r.at[0], cross).wait_recv()
+
+        by_row([len(owners) - (s in owners) for s in range(NR)], take_terms)
+        total = gains[2:3, :]
+        for o in owners:
+            total = total + ttin[o]
+        tterm[...] = total
+    else:
+        tterm[...] = dot(emb[...].astype(BF), wn(tw, TE)) + gains[2:3, :]
 
     CH = TX // 4
     tabs[:, 2 * C : 3 * C] = tterm[...]
@@ -851,7 +900,7 @@
     if gather:
         rx, rc = f // 2, f % 2
         shard_blocks = NB
-        n_groups = {1: ((48, 72), (104, 136)), 2: ((24, 48), (72, 104)), 3: ((0, 24),)}
+        n_groups = {1: ((48, 72), (104, 136)), 2: ((24, 48),), 3: ((0, 24),)}
         b_groups = {1: (4 * INNER, 2 * C), 2: (0, C)}
         b_at = {1: C, 2: 0}
 
@@ -966,28 +1015,66 @@
                 cp.wait_send()
                 cp.wait_recv()
 
-        def red_finish():
+        def send_final(j, blk, size):
+            for p in peers:
+                remote(blk, blk, rf_s.at[j], rf_r.at[j], p).start()
+            return remote(size, size, rf_s.at[j], rf_r.at[j], cross)
+
+        def red_finish_broad():
+            out = []
+            for j, g in enumerate((1, 2)):
+                cols = half_cols(rc, *b_groups[g])
+                here = slice(b_at[g], b_at[g] + b_groups[g][1])
+                total = bgrad[rw, rx, :, cols].astype(F32)
+                for k in range(1, NR):
+                    total = total + bgot[(rw + k) % NR, :, here].astype(F32)
+                bfull[rx, :, cols] = total.astype(BF)
+                out.append(send_final(j, bfull.at[rx, :, cols], bgot.at[0:3, :, here]))
+            return out
+
+        def red_finish_narrow():
             mine = half_cols(rc, 0, 128)
             total = ngrad[pl.ds(shard_blocks * rw, shard_blocks), rx, :, mine].astype(F32)
-            totals = [bgrad[rw, rx, :, half_cols(rc, *b_groups[g])].astype(F32) for g in (1, 2)]
             for k in range(1, NR):
-                o = (rw + k) % NR
-                total = total + got[o].astype(F32)
-                for j, g in enumerate((1, 2)):
-                    totals[j] = totals[j] + bgot[o, :, b_at[g] : b_at[g] + b_groups[g][1]].astype(F32)
+                total = total + got[(rw + k) % NR].astype(F32)
             gfull[:, rx, :, mine] = total.astype(BF)
-            fin = []
-            blocks = [gfull.at[:, rx, :, mine]]
-            for j, g in enumerate((1, 2)):
-                cols = half_cols(rc, *b_groups[g])
-                bfull[rx, :, cols] = totals[j].astype(BF)
-                blocks.append(bfull.at[rx, :, cols])
-            for j, blk in enumerate(blocks):
-                for p in peers:
-                    remote(blk, blk, rf_s.at[j], rf_r.at[j], p).start()
-                fin.append((rf_s.at[j], rf_r.at[j]))
-            sizes = [inq.at[0 : 3 * NB]] + [bgot.at[0:3, :, b_at[g] : b_at[g] + b_groups[g][1]] for g in (1, 2)]
-            return [remote(ref, ref, ss, rs, cross) for ref, (ss, rs) in zip(sizes, fin)]
+            return [send_final(2, gfull.at[:, rx, :, mine], inq.at[0 : 3 * NB])]
+
+        def terms_first():
+            tgbuf[f] = tg[...]
+            for p in peers:
+                remote(tgbuf.at[f], tgbuf.at[f], tf_s.at[0], tf_r.at[0], p).start()
+
+        def terms_second():
+            remote(tgbuf.at[0:3], tgbuf.at[0:3], tf_s.at[0], tf_r.at[0], cross).wait()
+            tgall[rw] = tgbuf[0] + tgbuf[1] + tgbuf[2] + tgbuf[3]
+            for o in owners:
+
+                @pl.when(rw != o)
+                def _():
+                    pltpu.make_async_remote_copy(
+                        src_ref=tgall.at[rw], dst_ref=tgall.at[rw], send_sem=to_s.at[0], recv_sem=to_r.at[0],
+                        device_id=(o, f), device_id_type=MESH,
+                    ).start()
+
+        def terms_third():
+            def sent(n):
+                remote(tgall.at[0:n], tgall.at[0:n], to_s.at[0], to_s.at[0], cross).wait_send()
+
+            by_row([len(owners) - (s in owners) for s in range(NR)], sent)
+
+            @pl.when(is_owner)
+            def _():
+                ref = tgall.at[0 : NR - 1]
+                remote(ref, ref, to_r.at[0], to_r.at[0], cross).wait_recv()
+                hi, lo = split2(tgall[...].reshape(NR * 8 * R, C))
+                grad = (dot_tn(embp[...], hi) + dot_tn(embp[...], lo)).astype(BF).reshape(NB, 2, 16, C)
+                for o in owners:
+                    a, b = max(NB * o, t_lo) - NB * o, min(NB * (o + 1), t_hi) - NB * o
+
+                    @pl.when(rw == o)
+                    def _():
+                        out_n[a:b] = grad[a:b]
 
         def small_first():
             s_pack[...] = small_rows()
@@ -1169,13 +1256,16 @@
     send_stats(3)
     send_edges(0, dn)
     if gather:
+        terms_first()
         red_owner(1)
     kernel_grad(u2, 3 * C)
-    t_hi, t_lo = split2(tg[...])
-    eb = emb[...].astype(BF)
-    put_n(tw, dot_tn(eb, t_hi) + dot_tn(eb, t_lo))
     if gather:
         red_core(2)
+        terms_second()
+    else:
+        part_hi, part_lo = split2(tg[...])
+        eb = emb[...].astype(BF)
+        put_n(tw, dot_tn(eb, part_hi) + dot_tn(eb, part_lo))
     mean_tables(3, 0)
     await_edges(0, dn)
 
@@ -1198,23 +1288,25 @@
         red_core(3)
         small_second()
         red_owner(2)
+        red_cross(3)
     for r in range(R):
         igrad[r] = gr2[r] + conv_back(r, 0)
-        if gather and r == 0:
-            red_cross(3)
-        if gather and r == R - 1:
+        if gather and r == 1:
             red_owner(3)
     if gather:
         small_third()
-        for g in (1, 2, 3):
-            red_wait(g)
-        fin = red_finish()
+        red_wait(1)
+        red_wait(2)
+        fin = red_finish_broad()
+        red_wait(3)
+        fin += red_finish_narrow()
         small_last()
         small[...] = s_all[...]
         for cp in fin:
             cp.wait()
         out_n[...] = gfull[...]
         out_b[...] = bfull[...]
+        terms_third()
 
     @pl.when(f < 3)
     def _():
@@ -1251,6 +1343,7 @@
         vm((16, C)), vm((8, FF)), vm((slots, 16, 128), BF), vm((16, 128)), vm((8, FF)), vm((3, 8, FF)), vm((16, C)),
     ] + red + [
         vm((32, C)), vm((3, 8, C)), vm((8, C)), vm((slots, 8, C)), vm((32, C)),
+        vm((slots * 8 * R, KC // slots if NR else 128), BF), vm((slots * 8 * R, C)), vm((slots, 8 * R, C)), vm((4, 8 * R, C)), vm((slots, 8 * R, C)),
         vm((R, TX, C), BF), vm((R, T // 2 + 16, C), BF), vm((R, TX, 128), BF),
         vm((R, 8, T)), vm((R, L, 128), BF), vm((24, L + 256)), vm((8 * R, 128)), vm((8 * R, TE)), vm((8 * R, C)),
         vm((8 * R, C)), vm((8 * R, C)), vm((8 * R, 3 * C)),
@@ -1267,7 +1360,7 @@
         vm((R, T, 3 * INNER), BF), vm((R, TX, C), BF), vm((8 * R, C)), vm((3, 2, R, 8, C)),
         dma(5), dma(5), dma(5), dma(5), dma(5, 2), dma(5, 2),
         dma(3, 3), dma(3, 3), dma(3, 3), dma(3, 3), dma(3, 2), dma(3, 2), dma(3), dma(3),
-        dma(1), dma(1), dma(1), dma(1), dma(1), dma(1),
+        dma(1), dma(1), dma(1), dma(1), dma(1), dma(1), dma(1), dma(1), dma(1), dma(1), dma(1), dma(1),
         dma(2), dma(2), dma(1), dma(1), dma(4), dma(4, 3), dma(3, R), dma(3, R),
         dma(3, R), dma(3, R), dma(3, 2), dma(3, 2), dma(R), dma(R),
     ]

time: 158 us -> 150 us (0.949)
  Pallas kernels: 157 us -> 149 us
    pallas_call x1, Pallas kernels: 152 us -> 145 us  [run_main(): pl.pallas_call(functools.partial(main_kernel, NR), out_shape=out_shape, i...]
where the time goes in v6:
time: 150 us
  Pallas kernels  149 us (99%)
    pallas_call x1, Pallas kernels, run_main(): pl.pallas_call(functools.partial(main_kernel, NR), out_shape=out_shape, i...  145 us
    pallas_call x1, Pallas kernels, run_adam(): pl.pallas_call(functools.partial(adam_kernel, NR), out_shape=out_shape, i...  4.78 us

profile of v6, /device:TPU:0, one launch (start us, length us, event | category | flops | bytes accessed | tf_op | source)
XLA Modules:
  0.0 150.2 jit_solution(2065102951765063286)
XLA Ops:
  0.6 144.6 %shard_map.279 = (bf16[3,256,256]{2,1,0:T(8,128)(2,1)}, f32[3,512,256]{2,1,0:T(8,128)}, f32[32,256]{1,0:T(8,128)}, bf16[17,2,16,256]{3,2,1,0:T(8,128)(2,1)}, bf16[2,16,1536]{2,1,0:T(8,128)(2,1)}) custom-call(bf16[3,512,256]{2,1,0:T(8,128)(2,1)} %feat.1, s32[3,2048]{1,0:T(4,128)} %ids.1, s32[3,8]{1,0:T(4,128)} %steps.1, bf16[3,256,256]{2,1,0:T(8,128)(2,1)} %cot.1, ...), custom_call_target="tpu_custom_call" | custom-call | flops 20000000000 | bytes 20000000 | tf_op jit(solution)/shard_map/pallas_call | solution.py:1375
  145.2 4.8 %shard_map.280 = (bf16[3,256,256]{2,1,0:T(8,128)(2,1)}, f32[3,512,256]{2,1,0:T(8,128)}, f32[544,256]{1,0:T(8,128)}, f32[544,256]{1,0:T(8,128)}, f32[544,256]{1,0...) custom-call(bf16[17,2,16,256]{3,2,1,0:T(8,128)(2,1)} %get-tuple-elem, ...), custom_call_target="tpu_custom_call" | custom-call | tf_op jit(solution)/shard_map/pallas_call | solution.py:1434

commit v7 on v6

--- a/solution.py
+++ b/solution.py
@@ -609,7 +609,7 @@
             u2[r, rows] = (y * t + sp[:, 2 * C :]).astype(BF)
             return c2
 
-        lax.fori_loop(0, 4, chunk, 0)
+        lax.fori_loop(0, 4, chunk, 0, unroll=True)
         conv_into(r, u2, 3 * C)
         v = (
             zs[0, OFF - 1 : OFF + T - 1] * own_prev(r)
@@ -664,7 +664,7 @@
             kvall[r, 1, krows] = qkv[:, 2 * INNER :].astype(BF)
             return c2
 
-        lax.fori_loop(0, NCH, chunk, 0)
+        lax.fori_loop(0, NCH, chunk, 0, unroll=True)
         if gather:
 
             @pl.when(r == 0)
@@ -730,7 +730,7 @@
     alpha_beta = alpha * inv_beta
     alpha_pi = alpha * (1.0 / math.pi)
     NK = L // 256
-    CF = T // 2
+    CF = T
     hacc[...] = jnp.zeros(hacc.shape, F32)
     lane128 = iota((T, 128), 1)
 
@@ -1166,19 +1166,25 @@
     if gather:
         red_core(1)
 
-    def mean_tables(phase, norm_phase):
+    def mean_tables(phase, norm_phase, gain_row):
         tot = total_stats(phase)
         iv = norm_scale(total_stats(norm_phase, wait=False))
         m1 = jnp.where(group_lanes, tot, 0.0)
         m2 = jnp.where(group_lanes, pltpu.roll(tot, 128 - G, 1), 0.0)
-        tabs[:, 0:C], tabs[:, C : 2 * C], tabs[:, 2 * C : 3 * C] = expand([m1 * iv, m2 * iv, iv])
-
-    def norm_back_start(r, d, n, gain_row):
-        ggrad[gain_row : gain_row + 1, :] += colsum(d * n)
-        ggrad[gain_row + 1 : gain_row + 2, :] += colsum(d)
-        scaled = d * gains[gain_row : gain_row + 1, :]
-        dn[r] = scaled
-        keep_sums(r, scaled, scaled * n)
+        tabs[:, 0:C], tabs[:, C : 2 * C], wide_iv = expand([m1 * iv, m2 * iv, iv])
+        tabs[:, 2 * C : 3 * C] = wide_iv * gains[gain_row : gain_row + 1, :]
+
+    def norm_back_start(r, gain_row):
+        oh = ohrow[r].astype(BF)
+        at = pl.ds(pl.multiple_of(8 * r, 8), 8)
+        gain = gains[gain_row : gain_row + 1, :]
+        first, second = segment_sums(oh, dn[r]), segment_sums(oh, zs[0, 0:T])
+        ggrad[gain_row : gain_row + 1, :] += colsum(second)
+        ggrad[gain_row + 1 : gain_row + 2, :] += colsum(first)
+        sums[at], squares[at] = first * gain, second * gain
+
+    def fold(x):
+        return jnp.sum(x.reshape(x.shape[0] // 8, 8, x.shape[1]), axis=0)
 
     def phase_five(r, carry):
         cps = dkv_copies(r)
@@ -1189,13 +1195,23 @@
         for i in range(2):
             tot = part[r, f, i].astype(F32) + rbuf[r, 0, i].astype(F32) + rbuf2[r, i].astype(F32)
             dqkv[r, :, (i + 1) * INNER : (i + 2) * INNER] = tot.T.astype(BF)
-        back = dot_nt(dqkv[r], broad[:, : 3 * INNER])
-        n, rs = layer_norm_parts(resid[r])
-        ggrad[5:6, :] += colsum(back * n)
-        ggrad[6:7, :] += colsum(back)
-        g_res = gr2[r] + layer_norm_back(back, n, rs, gains[5:6, :])
-        gr2[r] = g_res
-        norm_back_start(r, g_res * der2[r].astype(F32), nrm2[r], 3)
+        zs[1, 0:T] = dot_nt(dqkv[r], broad[:, : 3 * INNER])
+        acc_n = jnp.zeros((8, C), F32)
+        acc = jnp.zeros((8, C), F32)
+        for u in range(0, T, 64):
+            rows = slice(u, u + 64)
+            back = zs[1, rows]
+            n, rs = layer_norm_parts(resid[r, rows])
+            acc_n = acc_n + fold(back * n)
+            acc = acc + fold(back)
+            g_res = gr2[r, rows] + layer_norm_back(back, n, rs, gains[5:6, :])
+            gr2[r, rows] = g_res
+            d = g_res * der2[r, rows].astype(F32)
+            dn[r, rows] = d
+            zs[0, rows] = d * nrm2[r, rows]
+        ggrad[5:6, :] += colsum(acc_n)
+        ggrad[6:7, :] += colsum(acc)
+        norm_back_start(r, 3)
         return carry
 
     lax.fori_loop(0, R, phase_five, 0)
@@ -1204,7 +1220,7 @@
     if gather:
         red_cross(1)
     put_b(0, dot_tn(flat(ll1), flat(dqkv)))
-    mean_tables(2, 1)
+    mean_tables(2, 1, 3)
     await_edges(2, nrm2)
     await_edges(1, dn)
 
@@ -1220,7 +1236,9 @@
         below = back(slice(OFF + T, OFF + T + 16), edge[which, 1, r], n_below)
         g2[r, OFF - 16 : OFF] = jnp.concatenate([zero, above], axis=0).astype(BF)
         g2[r, OFF + T : OFF + T + 16] = jnp.concatenate([below, zero], axis=0).astype(BF)
-        g2[r, OFF : OFF + T] = back(slice(OFF, OFF + T), dn[r], n).astype(BF)
+        for u in range(0, T, 128):
+            rows = slice(OFF + u, OFF + u + 128)
+            g2[r, rows] = back(rows, dn[r, u : u + 128], n[u : u + 128]).astype(BF)
 
     def build_g3(r):
         g = g2[r].astype(F32)
@@ -1249,7 +1267,11 @@
         tgr = segment_sums(oh, gh)
         tg[pl.ds(pl.multiple_of(8 * r, 8), 8), :] = tgr
         ggrad[2:3, :] += colsum(tgr)
-        norm_back_start(r, gh * der1[r, OFF : OFF + T].astype(F32), nrm1[r, OFF : OFF + T], 0)
+        for u in range(0, T, 64):
+            d = gh[u : u + 64] * der1[r, OFF + u : OFF + u + 64].astype(F32)
+            dn[r, u : u + 64] = d
+            zs[0, u : u + 64] = d * nrm1[r, OFF + u : OFF + u + 64]
+        norm_back_start(r, 0)
         return carry
 
     lax.fori_loop(0, R, phase_seven, 0)
@@ -1266,7 +1288,7 @@
         part_hi, part_lo = split2(tg[...])
         eb = emb[...].astype(BF)
         put_n(tw, dot_tn(eb, part_hi) + dot_tn(eb, part_lo))
-    mean_tables(3, 0)
+    mean_tables(3, 0, 0)
     await_edges(0, dn)
 
     if gather:
@@ -1351,7 +1373,7 @@
         vm((R, T, C), BF), vm((R, T, C)), vm((R, T, C), BF), vm((R, T, INNER), BF),
         vm((R, 2, L, INNER), BF),
         vm((4, 3, 8 * R, 128)), vm((4, 8 * R, 128)),
-        vm((INNER, L), BF), vm((INNER, L), BF), vm((INNER, T), BF), vm((2, 2, T // 2, C)), vm((2, L, T // 2)), vm((H, L, T), BF), vm((INNER, T)),
+        vm((INNER, L), BF), vm((INNER, L), BF), vm((INNER, T), BF), vm((2, 2, T, C)), vm((2, L, T // 2)), vm((H, L, T), BF), vm((INNER, T)),
         vm((H, 8, T)), vm((T, INNER)), vm((INNER, T)),
         vm((R, T, C), BF), vm((R, T, C), BF),
         vm((R, T, FF), BF), vm((R, T, FF), BF), vm((4, T + 8, 128)), vm((R, T + 16, C), BF),

time: 150 us -> 146 us (0.973)
  Pallas kernels: 149 us -> 145 us
    pallas_call x1, Pallas kernels: 145 us -> 140 us  [run_main(): pl.pallas_call(functools.partial(main_kernel, NR), out_shape=out_shape, i...]
where the time goes in v7:
time: 146 us
  Pallas kernels  145 us (99%)
    pallas_call x1, Pallas kernels, run_main(): pl.pallas_call(functools.partial(main_kernel, NR), out_shape=out_shape, i...  140 us
    pallas_call x1, Pallas kernels, run_adam(): pl.pallas_call(functools.partial(adam_kernel, NR), out_shape=out_shape, i...  4.78 us

profile of v7, /device:TPU:0, one launch (start us, length us, event | category | flops | bytes accessed | tf_op | source)
XLA Modules:
  0.0 145.9 jit_solution(9569774121858575036)
XLA Ops:
  0.6 140.3 %shard_map.279 = (bf16[3,256,256]{2,1,0:T(8,128)(2,1)}, f32[3,512,256]{2,1,0:T(8,128)}, f32[32,256]{1,0:T(8,128)}, bf16[17,2,16,256]{3,2,1,0:T(8,128)(2,1)}, bf16[2,16,1536]{2,1,0:T(8,128)(2,1)}) custom-call(bf16[3,512,256]{2,1,0:T(8,128)(2,1)} %feat.1, s32[3,2048]{1,0:T(4,128)} %ids.1, s32[3,8]{1,0:T(4,128)} %steps.1, bf16[3,256,256]{2,1,0:T(8,128)(2,1)} %cot.1, ...), custom_call_target="tpu_custom_call" | custom-call | flops 20000000000 | bytes 20000000 | tf_op jit(solution)/shard_map/pallas_call | solution.py:1397
  141.0 4.8 %shard_map.280 = (bf16[3,256,256]{2,1,0:T(8,128)(2,1)}, f32[3,512,256]{2,1,0:T(8,128)}, f32[544,256]{1,0:T(8,128)}, f32[544,256]{1,0:T(8,128)}, f32[544,256]{1,0...) custom-call(bf16[17,2,16,256]{3,2,1,0:T(8,128)(2,1)} %get-tuple-elem, ...), custom_call_target="tpu_custom_call" | custom-call | tf_op jit(solution)/shard_map/pallas_call | solution.py:1456

commit v8 on v7

--- a/solution.py
+++ b/solution.py
@@ -729,7 +729,7 @@
     inv_beta = jnp.exp(-hidden[2:3, :])
     alpha_beta = alpha * inv_beta
     alpha_pi = alpha * (1.0 / math.pi)
-    NK = L // 256
+    NK = L // 512
     CF = T
     hacc[...] = jnp.zeros(hacc.shape, F32)
     lane128 = iota((T, 128), 1)
@@ -768,11 +768,11 @@
             qa = jnp.concatenate([q_heads[h][qrows], ohq[qrows]], axis=1)
             m8 = jnp.full((8, TQ), -3e38, F32)
             for i in range(NK):
-                keys = slice(i * 256, i * 256 + 256)
+                keys = slice(i * 512, i * 512 + 512)
                 ka = jnp.concatenate([kvall[r, 0, keys], keymask[r, keys]], axis=1)
                 sc = dot_nt(ka, qa)
                 sbuf[n % 2, keys] = sc
-                m8 = jnp.maximum(m8, jnp.max(sc.reshape(32, 8, TQ), axis=0))
+                m8 = jnp.maximum(m8, jnp.max(sc.reshape(64, 8, TQ), axis=0))
             return jnp.max(m8, axis=0, keepdims=True)
 
         top = scores(0)
@@ -781,10 +781,10 @@
             qcols = slice(q * TQ, q * TQ + TQ)
             l8 = jnp.zeros((8, TQ), F32)
             for i in range(NK):
-                keys = slice(i * 256, i * 256 + 256)
+                keys = slice(i * 512, i * 512 + 512)
                 e = jnp.exp(sbuf[n % 2, keys] - top)
                 ebuf[h, keys, qcols] = e.astype(BF)
-                l8 = l8 + jnp.sum(e.reshape(32, 8, TQ), axis=0)
+                l8 = l8 + jnp.sum(e.reshape(64, 8, TQ), axis=0)
             inv = 1.0 / jnp.sum(l8, axis=0, keepdims=True)
             invl[h, :, qcols] = jnp.broadcast_to(inv, (8, TQ))
             hrows = slice(h * HD, (h + 1) * HD)
@@ -862,7 +862,7 @@
             dost[hrows, :] = dot_t[hrows] * invl[h, 0:1, :]
         zero_t = jnp.zeros((HD, T), BF)
         d_rows, d_cols, d_half = [], [], []
-        per_block = T // 256
+        per_block = 1
         for h in range(H):
             hrows = slice(h * HD, (h + 1) * HD)
             d_rows.append(colsum(otb[hrows, :] * dost[hrows, :]))
@@ -873,8 +873,8 @@
         cps = dkv_copies(r)
         for n, block in enumerate((diag, sib, cross, f)):
             for i in range(per_block):
-                keys = pl.ds(pl.multiple_of(block * T + i * 256, 256), 256)
-                within = slice(i * 256, i * 256 + 256)
+                keys = pl.ds(pl.multiple_of(block * T, 256), T)
+                within = slice(0, T)
                 for h in range(H):
                     hrows = slice(h * HD, (h + 1) * HD)
                     eh = ebuf[h, keys]

time: 146 us -> 145 us (level)
  Pallas kernels: 145 us -> 143 us
    pallas_call x1, Pallas kernels: 140 us -> 139 us  [run_main(): pl.pallas_call(functools.partial(main_kernel, NR), out_shape=out_shape, i...]
where the time goes in v8:
time: 145 us; the launch traced here: 144 us
  Pallas kernels  143 us (99%)
    pallas_call x1, Pallas kernels, run_main(): pl.pallas_call(functools.partial(main_kernel, NR), out_shape=out_shape, i...  139 us
    pallas_call x1, Pallas kernels, run_adam(): pl.pallas_call(functools.partial(adam_kernel, NR), out_shape=out_shape, i...  4.78 us

profile of v8, /device:TPU:0, one launch (start us, length us, event | category | flops | bytes accessed | tf_op | source)
XLA Modules:
  0.0 144.3 jit_solution(9605788569830620260)
XLA Ops:
  0.6 138.6 %shard_map.279 = (bf16[3,256,256]{2,1,0:T(8,128)(2,1)}, f32[3,512,256]{2,1,0:T(8,128)}, f32[32,256]{1,0:T(8,128)}, bf16[17,2,16,256]{3,2,1,0:T(8,128)(2,1)}, bf16[2,16,1536]{2,1,0:T(8,128)(2,1)}) custom-call(bf16[3,512,256]{2,1,0:T(8,128)(2,1)} %feat.1, s32[3,2048]{1,0:T(4,128)} %ids.1, s32[3,8]{1,0:T(4,128)} %steps.1, bf16[3,256,256]{2,1,0:T(8,128)(2,1)} %cot.1, ...), custom_call_target="tpu_custom_call" | custom-call | flops 20000000000 | bytes 20000000 | tf_op jit(solution)/shard_map/pallas_call | solution.py:1397
  139.3 4.8 %shard_map.280 = (bf16[3,256,256]{2,1,0:T(8,128)(2,1)}, f32[3,512,256]{2,1,0:T(8,128)}, f32[544,256]{1,0:T(8,128)}, f32[544,256]{1,0:T(8,128)}, f32[544,256]{1,0...) custom-call(bf16[17,2,16,256]{3,2,1,0:T(8,128)(2,1)} %get-tuple-elem, ...), custom_call_target="tpu_custom_call" | custom-call | tf_op jit(solution)/shard_map/pallas_call | solution.py:1456
